TPU v7x, 128 devices: a whole 4x4x4 slice. The times are simulated.
128 devices in a mesh: seq: 16 (over x_hi, y, core), chan: 8 (over x_lo, z).
Axes of the slice: x: 4 (x_hi: 2, x_lo: 2; x = x_hi * 2 + x_lo), y: 4, z: 4, core: 2. Of those that a mesh axis runs over, the one named last changes fastest.
Arguments:
- out_gate: bfloat16 [4096, 8192], P('seq', 'chan'), may hold values from -6 to 6
- in_gate: bfloat16 [4096, 8192], P('seq', 'chan'), may hold values from -6 to 6
- signal: bfloat16 [4096, 8192], P('seq', 'chan'), may hold values from -6 to 6
- filter_taps: bfloat16 [4096, 8192], P('seq', 'chan'), may hold values from -5 to 5
- skip_gain: float32 [8192], P('chan'), may hold values from -4 to 4
- out_proj: bfloat16 [8192, 8192], P(None, 'chan'), may hold values from -0.09375 to 0.09375
Outputs:
- layer_out: bfloat16 [4096, 8192], P('seq', 'chan')
All inputs are finite; a program needn't handle non-finite values.
Results may differ from a plain program's by a relative error of at most 0.02.
Values may be sent and summed in bfloat16 or wider, within the bound.
No kernel may reach another device: no remote copies, remote signals or barrier semaphores. Data moves between devices by JAX's collectives and lax.ppermute only.
A program may use at most 128 MiB of HBM per device.

v0:
```python
import math

import jax
import jax.numpy as jnp
from jax import lax
from jax.sharding import PartitionSpec as P


def passed_along(block, axis, distance):
    devices = range(lax.axis_size(axis))
    route = [(i - distance, i) for i in devices if i - distance in devices]
    return lax.ppermute(block, axis, route)


def fourier_tables(block_len):
    length = 2 * block_len
    freq_index = jnp.arange(block_len, dtype=jnp.int32)[:, None]
    moment = jnp.arange(block_len, dtype=jnp.int32)[None, :]
    angle_table = 2.0 * math.pi / length * (freq_index * moment % length).astype(jnp.float32)
    alternate = jnp.where(moment % 2 == 0, 1.0, -1.0).astype(jnp.float32)
    cosine = jnp.cos(angle_table)
    sine_table = jnp.sin(angle_table)
    forward_imag = jnp.where(freq_index == 0, alternate, -sine_table)
    forward = jnp.concatenate([cosine, forward_imag], axis=0)
    weight = jnp.where(moment == 0, 1.0, 2.0).astype(jnp.float32) / length
    inverse_real = cosine * weight
    inverse_imag = jnp.where(moment == 0, alternate.T / length, -2.0 / length * sine_table)
    inverse = jnp.concatenate([inverse_real, inverse_imag], axis=1)
    keep_mask = (jnp.arange(block_len) > 0).astype(jnp.float32)
    sign_half = jnp.where(jnp.arange(block_len) % 2 == 0, 1.0, -1.0).astype(jnp.float32)
    sign_pattern = jnp.concatenate([sign_half, sign_half])
    forward_high = forward.astype(jnp.bfloat16)
    forward_low = (forward - forward_high.astype(jnp.float32)).astype(jnp.bfloat16)
    return ((forward_high, forward_low), inverse, keep_mask, sign_pattern)


def spectral_product(factor_left, factor_right, keep_mask, split_axis):
    left_real, left_imag = jnp.split(factor_left, 2, axis=split_axis)
    right_real, right_imag = jnp.split(factor_right, 2, axis=split_axis)
    cross_term = left_imag * right_imag
    real_part = left_real * right_real - keep_mask * cross_term
    imag_part = (
        keep_mask * (left_real * right_imag + left_imag * right_real)
        + (1.0 - keep_mask) * cross_term
    )
    return jnp.concatenate([real_part, imag_part], axis=split_axis)


def transform(tables, time_rows):
    first = jnp.dot(tables[0], time_rows, preferred_element_type=jnp.float32)
    return first + jnp.dot(tables[1], time_rows, preferred_element_type=jnp.float32)


def shards(out_gate, in_gate, signal, filter_taps, skip_gain, out_proj):
    block_len = out_gate.shape[0]
    seq_count = lax.axis_size("seq")
    highest = lax.Precision.HIGHEST
    gated_rows = (in_gate.astype(jnp.float32) * signal.astype(jnp.float32)).astype(jnp.bfloat16)
    tables, inverse, keep_mask, sign_pattern = fourier_tables(block_len)
    all_taps = lax.all_gather(filter_taps, "seq", axis=0, tiled=True)
    keep_col = keep_mask[:, None]
    sign_col = sign_pattern[:, None]

    def lag_spectrum(lag_index):
        return transform(
            tables, lax.dynamic_slice_in_dim(all_taps, lag_index * block_len, block_len, 0)
        )

    first_spec = lag_spectrum(0)
    running = spectral_product(first_spec, transform(tables, gated_rows), keep_col, 0)

    def add_source(lag_index, carry):
        running_sum, previous, held_rows = carry
        held_rows = passed_along(held_rows, "seq", 1)
        current = lag_spectrum(lag_index)
        pair_spec = current + sign_col * previous
        running_sum = running_sum + spectral_product(
            pair_spec, transform(tables, held_rows), keep_col, 0
        )
        return (running_sum, current, held_rows)

    running, last_spec, last_held = lax.fori_loop(
        1, seq_count, add_source, (running, first_spec, gated_rows)
    )
    conv_rows = jnp.dot(inverse, running, precision=highest)
    mixed_rows = (
        out_gate.astype(jnp.float32)
        * (conv_rows + skip_gain[None, :] * gated_rows.astype(jnp.float32))
    ).astype(jnp.bfloat16)
    summed = lax.psum_scatter(
        lax.dot_general(
            out_proj, mixed_rows, (((1,), (1,)), ((), ())), preferred_element_type=jnp.float32
        ).astype(jnp.bfloat16),
        "chan",
        scatter_dimension=0,
        tiled=True,
    ).astype(jnp.float32)
    return summed.T.astype(jnp.bfloat16)


def solution(mesh):
    return jax.shard_map(
        shards,
        mesh=mesh,
        in_specs=(
            P("seq", "chan"),
            P("seq", "chan"),
            P("seq", "chan"),
            P("seq", "chan"),
            P("chan"),
            P(None, "chan"),
        ),
        out_specs=P("seq", "chan"),
        check_vma=False,
    )
```

profile of v0, /device:TPU:0, one launch (start us, length us, event | category | flops | bytes accessed | tf_op | source)
XLA Modules:
  0.0 416.0 jit_solution(1783234137124301524)
XLA Ops:
  11.8 1.7 broadcast_multiply_fusion
  14.4 70.8 %all-gather.2.cloned.1.call-done = bf16[4096,1024]{1,0:T(8,128)(2,1)} async-done(((bf16[256,1024]{1,0:T(8,128)(2,1)}), bf16[4096,1024]{1,0:T(8,128)(2,1)}) %all-gather.2.cloned.1.call-update) | async-done | bytes 8388624 | tf_op jit(solution)/shard_map/all_gather | solution.py:60
  89.8 204.9 %while.19 = (s32[]{:T(128)}, f32[512,1024]{1,0:T(8,128)S(1)}, f32[512,1024]{1,0:T(8,128)}, bf16[256,1024]{1,0:T(8,128)(2,1)}, bf16[4096,1024]{1,0:T(8,128)(2,1)}...) while((s32[]{:T(128)}, f32[512,1024]{1,0:T(8,128)S(1)}, ...), condition=%wide.region_1.2_spmd.clone.clone, body=%wide.region_0.1_spmd.clone.clone.sunk | while | flops 1079509760 | bytes 52436232 | solution.py:82
  90.0 2.2 collective-permute-start
  93.9 2.1 multiply_add_fusion.4
  99.2 4.1 collective-permute-start
  103.3 1.6 fusion.61
  105.0 2.1 multiply_add_fusion.4
  110.3 6.4 %collective-permute-start = (bf16[256,1024]{1,0:T(8,128)(2,1)}, bf16[256,1024]{1,0:T(8,128)(2,1)S(1)}, u32[]{:S(2)}, u32[]{:S(2)}) collective-permute-start(bf16[256,1024]{1,0:T(8,128)(2,1)} %get-tuple-element.307), channel_id=1, source_target_pairs={{0,8},{8,16},{16,24},{24,32},{32,40},{40,48},{48,56},{56,64},{64,7... | collective-permute-start | bytes 1572872 | tf_op jit(solution)/shard_map/while/body/eval_jaxpr/ppermute | solution.py:12
  116.8 1.6 fusion.61
  118.5 2.1 multiply_add_fusion.4
  123.8 6.4 %collective-permute-start = (bf16[256,1024]{1,0:T(8,128)(2,1)}, bf16[256,1024]{1,0:T(8,128)(2,1)S(1)}, u32[]{:S(2)}, u32[]{:S(2)}) collective-permute-start(bf16[256,1024]{1,0:T(8,128)(2,1)} %get-tuple-element.307), channel_id=1, source_target_pairs={{0,8},{8,16},{16,24},{24,32},{32,40},{40,48},{48,56},{56,64},{64,7... | collective-permute-start | bytes 1572872 | tf_op jit(solution)/shard_map/while/body/eval_jaxpr/ppermute | solution.py:12
  130.2 1.6 fusion.61
  132.0 2.1 multiply_add_fusion.4
  137.2 6.4 %collective-permute-start = (bf16[256,1024]{1,0:T(8,128)(2,1)}, bf16[256,1024]{1,0:T(8,128)(2,1)S(1)}, u32[]{:S(2)}, u32[]{:S(2)}) collective-permute-start(bf16[256,1024]{1,0:T(8,128)(2,1)} %get-tuple-element.307), channel_id=1, source_target_pairs={{0,8},{8,16},{16,24},{24,32},{32,40},{40,48},{48,56},{56,64},{64,7... | collective-permute-start | bytes 1572872 | tf_op jit(solution)/shard_map/while/body/eval_jaxpr/ppermute | solution.py:12
  143.7 1.6 fusion.61
  145.4 2.1 multiply_add_fusion.4
  150.7 6.4 %collective-permute-start = (bf16[256,1024]{1,0:T(8,128)(2,1)}, bf16[256,1024]{1,0:T(8,128)(2,1)S(1)}, u32[]{:S(2)}, u32[]{:S(2)}) collective-permute-start(bf16[256,1024]{1,0:T(8,128)(2,1)} %get-tuple-element.307), channel_id=1, source_target_pairs={{0,8},{8,16},{16,24},{24,32},{32,40},{40,48},{48,56},{56,64},{64,7... | collective-permute-start | bytes 1572872 | tf_op jit(solution)/shard_map/while/body/eval_jaxpr/ppermute | solution.py:12
  157.1 1.6 fusion.61
  158.9 2.1 multiply_add_fusion.4
  164.1 6.4 %collective-permute-start = (bf16[256,1024]{1,0:T(8,128)(2,1)}, bf16[256,1024]{1,0:T(8,128)(2,1)S(1)}, u32[]{:S(2)}, u32[]{:S(2)}) collective-permute-start(bf16[256,1024]{1,0:T(8,128)(2,1)} %get-tuple-element.307), channel_id=1, source_target_pairs={{0,8},{8,16},{16,24},{24,32},{32,40},{40,48},{48,56},{56,64},{64,7... | collective-permute-start | bytes 1572872 | tf_op jit(solution)/shard_map/while/body/eval_jaxpr/ppermute | solution.py:12
  170.6 1.6 fusion.61
  172.3 2.1 multiply_add_fusion.4
  177.6 6.4 %collective-permute-start = (bf16[256,1024]{1,0:T(8,128)(2,1)}, bf16[256,1024]{1,0:T(8,128)(2,1)S(1)}, u32[]{:S(2)}, u32[]{:S(2)}) collective-permute-start(bf16[256,1024]{1,0:T(8,128)(2,1)} %get-tuple-element.307), channel_id=1, source_target_pairs={{0,8},{8,16},{16,24},{24,32},{32,40},{40,48},{48,56},{56,64},{64,7... | collective-permute-start | bytes 1572872 | tf_op jit(solution)/shard_map/while/body/eval_jaxpr/ppermute | solution.py:12
  184.0 1.6 fusion.61
  185.8 2.1 multiply_add_fusion.4
  191.0 6.4 %collective-permute-start = (bf16[256,1024]{1,0:T(8,128)(2,1)}, bf16[256,1024]{1,0:T(8,128)(2,1)S(1)}, u32[]{:S(2)}, u32[]{:S(2)}) collective-permute-start(bf16[256,1024]{1,0:T(8,128)(2,1)} %get-tuple-element.307), channel_id=1, source_target_pairs={{0,8},{8,16},{16,24},{24,32},{32,40},{40,48},{48,56},{56,64},{64,7... | collective-permute-start | bytes 1572872 | tf_op jit(solution)/shard_map/while/body/eval_jaxpr/ppermute | solution.py:12
  197.5 1.6 fusion.61
  199.2 2.1 multiply_add_fusion.4
  204.5 6.4 %collective-permute-start = (bf16[256,1024]{1,0:T(8,128)(2,1)}, bf16[256,1024]{1,0:T(8,128)(2,1)S(1)}, u32[]{:S(2)}, u32[]{:S(2)}) collective-permute-start(bf16[256,1024]{1,0:T(8,128)(2,1)} %get-tuple-element.307), channel_id=1, source_target_pairs={{0,8},{8,16},{16,24},{24,32},{32,40},{40,48},{48,56},{56,64},{64,7... | collective-permute-start | bytes 1572872 | tf_op jit(solution)/shard_map/while/body/eval_jaxpr/ppermute | solution.py:12
  211.0 1.6 fusion.61
  212.7 2.1 multiply_add_fusion.4
  218.0 6.4 %collective-permute-start = (bf16[256,1024]{1,0:T(8,128)(2,1)}, bf16[256,1024]{1,0:T(8,128)(2,1)S(1)}, u32[]{:S(2)}, u32[]{:S(2)}) collective-permute-start(bf16[256,1024]{1,0:T(8,128)(2,1)} %get-tuple-element.307), channel_id=1, source_target_pairs={{0,8},{8,16},{16,24},{24,32},{32,40},{40,48},{48,56},{56,64},{64,7... | collective-permute-start | bytes 1572872 | tf_op jit(solution)/shard_map/while/body/eval_jaxpr/ppermute | solution.py:12
  224.4 1.6 fusion.61
  226.1 2.1 multiply_add_fusion.4
  231.4 6.4 %collective-permute-start = (bf16[256,1024]{1,0:T(8,128)(2,1)}, bf16[256,1024]{1,0:T(8,128)(2,1)S(1)}, u32[]{:S(2)}, u32[]{:S(2)}) collective-permute-start(bf16[256,1024]{1,0:T(8,128)(2,1)} %get-tuple-element.307), channel_id=1, source_target_pairs={{0,8},{8,16},{16,24},{24,32},{32,40},{40,48},{48,56},{56,64},{64,7... | collective-permute-start | bytes 1572872 | tf_op jit(solution)/shard_map/while/body/eval_jaxpr/ppermute | solution.py:12
  237.9 1.6 fusion.61
  239.6 2.1 multiply_add_fusion.4
  244.9 8.6 %collective-permute-start = (bf16[256,1024]{1,0:T(8,128)(2,1)}, bf16[256,1024]{1,0:T(8,128)(2,1)S(1)}, u32[]{:S(2)}, u32[]{:S(2)}) collective-permute-start(bf16[256,1024]{1,0:T(8,128)(2,1)} %get-tuple-element.307), channel_id=1, source_target_pairs={{0,8},{8,16},{16,24},{24,32},{32,40},{40,48},{48,56},{56,64},{64,7... | collective-permute-start | bytes 1572872 | tf_op jit(solution)/shard_map/while/body/eval_jaxpr/ppermute | solution.py:12
  253.5 1.6 fusion.61
  255.3 2.1 multiply_add_fusion.4
  260.5 10.0 %collective-permute-start = (bf16[256,1024]{1,0:T(8,128)(2,1)}, bf16[256,1024]{1,0:T(8,128)(2,1)S(1)}, u32[]{:S(2)}, u32[]{:S(2)}) collective-permute-start(bf16[256,1024]{1,0:T(8,128)(2,1)} %get-tuple-element.307), channel_id=1, source_target_pairs={{0,8},{8,16},{16,24},{24,32},{32,40},{40,48},{48,56},{56,64},{64,7... | collective-permute-start | bytes 1572872 | tf_op jit(solution)/shard_map/while/body/eval_jaxpr/ppermute | solution.py:12
  272.3 2.1 multiply_add_fusion.4
  277.6 10.0 %collective-permute-start = (bf16[256,1024]{1,0:T(8,128)(2,1)}, bf16[256,1024]{1,0:T(8,128)(2,1)S(1)}, u32[]{:S(2)}, u32[]{:S(2)}) collective-permute-start(bf16[256,1024]{1,0:T(8,128)(2,1)} %get-tuple-element.307), channel_id=1, source_target_pairs={{0,8},{8,16},{16,24},{24,32},{32,40},{40,48},{48,56},{56,64},{64,7... | collective-permute-start | bytes 1572872 | tf_op jit(solution)/shard_map/while/body/eval_jaxpr/ppermute | solution.py:12
  289.4 2.1 multiply_add_fusion.4
  294.7 3.2 fusion.9
  297.9 9.5 %fusion.7 = bf16[8192,256]{0,1:T(8,128)(2,1)} fusion(bf16[256,1024]{1,0:T(8,128)(2,1)S(1)} %fusion.9, bf16[8192,1024]{1,0:T(8,128)(2,1)} %param.13), kind=kOutput, calls=%fused_computation.16 | convolution fusion | flops 4297064448 | bytes 21495808 | tf_op jit(solution)/shard_map/dot_general | solution.py:91
  307.4 101.8 %reduce-scatter.2.cloned.1.call-done = bf16[1024,256]{0,1:T(8,128)(2,1)} async-done(((bf16[8192,256]{0,1:T(8,128)(2,1)}), bf16[1024,256]{0,1:T(8,128)(2,1)}) %reduce-scatter.2.cloned.1.call-update) | async-done | bytes 524304 | tf_op jit(solution)/shard_map/reduce_scatter | solution.py:90
  (210 shorter events, 64.4 us)
Async XLA Ops:
  6.5 78.6 %all-gather.2.cloned.1.call-start = ((), (), s32[]{:S(2)}) async-start(), calls=%async_computation.1 | async-start | bytes 8912896 | tf_op jit(solution)/shard_map/all_gather | solution.py:60
  7.3 401.9 %reduce-scatter.2.cloned.1.call-start = ((), (), s32[]{:S(2)}) async-start(), calls=%async_computation.2 | async-start | bytes 4718592 | tf_op jit(solution)/shard_map/reduce_scatter | solution.py:90
  8.8 5.1 %copy-start.3 = (bf16[256,1024]{1,0:T(8,128)(2,1)}, bf16[256,1024]{1,0:T(8,128)(2,1)S(1)}, u32[]{:S(2)}) copy-start(bf16[256,1024]{1,0:T(8,128)(2,1)S(1)} %multiply_convert_fusion) | copy-start | bytes 1572868
  88.1 1.4 copy-start
  89.8 204.9 %copy-start.4 = (f32[1024]{0:T(1024)S(1)}, f32[1024]{0:T(1024)}, u32[]{:S(2)}) copy-start(f32[1024]{0:T(1024)} %param.12) | copy-start | bytes 12292
  90.0 6.1 %collective-permute-start = (bf16[256,1024]{1,0:T(8,128)(2,1)}, bf16[256,1024]{1,0:T(8,128)(2,1)S(1)}, u32[]{:S(2)}, u32[]{:S(2)}) collective-permute-start(bf16[256,1024]{1,0:T(8,128)(2,1)} %get-tuple-element.307), channel_id=1, source_target_pairs={{0,8},{8,16},{16,24},{24,32},{32,40},{40,48},{48,56},{56,64},{64,7... | collective-permute-start | bytes 1572872 | tf_op jit(solution)/shard_map/while/body/eval_jaxpr/ppermute | solution.py:12
  92.2 1.7 copy-start.1
  96.0 1.4 copy-start.2
  99.2 7.9 %collective-permute-start = (bf16[256,1024]{1,0:T(8,128)(2,1)}, bf16[256,1024]{1,0:T(8,128)(2,1)S(1)}, u32[]{:S(2)}, u32[]{:S(2)}) collective-permute-start(bf16[256,1024]{1,0:T(8,128)(2,1)} %get-tuple-element.307), channel_id=1, source_target_pairs={{0,8},{8,16},{16,24},{24,32},{32,40},{40,48},{48,56},{56,64},{64,7... | collective-permute-start | bytes 1572872 | tf_op jit(solution)/shard_map/while/body/eval_jaxpr/ppermute | solution.py:12
  103.3 1.7 copy-start.1
  107.1 1.4 copy-start.2
  110.3 10.3 %collective-permute-start = (bf16[256,1024]{1,0:T(8,128)(2,1)}, bf16[256,1024]{1,0:T(8,128)(2,1)S(1)}, u32[]{:S(2)}, u32[]{:S(2)}) collective-permute-start(bf16[256,1024]{1,0:T(8,128)(2,1)} %get-tuple-element.307), channel_id=1, source_target_pairs={{0,8},{8,16},{16,24},{24,32},{32,40},{40,48},{48,56},{56,64},{64,7... | collective-permute-start | bytes 1572872 | tf_op jit(solution)/shard_map/while/body/eval_jaxpr/ppermute | solution.py:12
  116.7 1.7 copy-start.1
  120.6 1.4 copy-start.2
  123.8 10.3 %collective-permute-start = (bf16[256,1024]{1,0:T(8,128)(2,1)}, bf16[256,1024]{1,0:T(8,128)(2,1)S(1)}, u32[]{:S(2)}, u32[]{:S(2)}) collective-permute-start(bf16[256,1024]{1,0:T(8,128)(2,1)} %get-tuple-element.307), channel_id=1, source_target_pairs={{0,8},{8,16},{16,24},{24,32},{32,40},{40,48},{48,56},{56,64},{64,7... | collective-permute-start | bytes 1572872 | tf_op jit(solution)/shard_map/while/body/eval_jaxpr/ppermute | solution.py:12
  130.2 1.7 copy-start.1
  134.0 1.4 copy-start.2
  137.2 10.3 %collective-permute-start = (bf16[256,1024]{1,0:T(8,128)(2,1)}, bf16[256,1024]{1,0:T(8,128)(2,1)S(1)}, u32[]{:S(2)}, u32[]{:S(2)}) collective-permute-start(bf16[256,1024]{1,0:T(8,128)(2,1)} %get-tuple-element.307), channel_id=1, source_target_pairs={{0,8},{8,16},{16,24},{24,32},{32,40},{40,48},{48,56},{56,64},{64,7... | collective-permute-start | bytes 1572872 | tf_op jit(solution)/shard_map/while/body/eval_jaxpr/ppermute | solution.py:12
  143.7 1.7 copy-start.1
  147.5 1.4 copy-start.2
  150.7 10.3 %collective-permute-start = (bf16[256,1024]{1,0:T(8,128)(2,1)}, bf16[256,1024]{1,0:T(8,128)(2,1)S(1)}, u32[]{:S(2)}, u32[]{:S(2)}) collective-permute-start(bf16[256,1024]{1,0:T(8,128)(2,1)} %get-tuple-element.307), channel_id=1, source_target_pairs={{0,8},{8,16},{16,24},{24,32},{32,40},{40,48},{48,56},{56,64},{64,7... | collective-permute-start | bytes 1572872 | tf_op jit(solution)/shard_map/while/body/eval_jaxpr/ppermute | solution.py:12
  157.1 1.7 copy-start.1
  160.9 1.4 copy-start.2
  164.1 10.3 %collective-permute-start = (bf16[256,1024]{1,0:T(8,128)(2,1)}, bf16[256,1024]{1,0:T(8,128)(2,1)S(1)}, u32[]{:S(2)}, u32[]{:S(2)}) collective-permute-start(bf16[256,1024]{1,0:T(8,128)(2,1)} %get-tuple-element.307), channel_id=1, source_target_pairs={{0,8},{8,16},{16,24},{24,32},{32,40},{40,48},{48,56},{56,64},{64,7... | collective-permute-start | bytes 1572872 | tf_op jit(solution)/shard_map/while/body/eval_jaxpr/ppermute | solution.py:12
  170.6 1.7 copy-start.1
  174.4 1.4 copy-start.2
  177.6 10.3 %collective-permute-start = (bf16[256,1024]{1,0:T(8,128)(2,1)}, bf16[256,1024]{1,0:T(8,128)(2,1)S(1)}, u32[]{:S(2)}, u32[]{:S(2)}) collective-permute-start(bf16[256,1024]{1,0:T(8,128)(2,1)} %get-tuple-element.307), channel_id=1, source_target_pairs={{0,8},{8,16},{16,24},{24,32},{32,40},{40,48},{48,56},{56,64},{64,7... | collective-permute-start | bytes 1572872 | tf_op jit(solution)/shard_map/while/body/eval_jaxpr/ppermute | solution.py:12
  184.0 1.7 copy-start.1
  187.9 1.4 copy-start.2
  191.0 10.3 %collective-permute-start = (bf16[256,1024]{1,0:T(8,128)(2,1)}, bf16[256,1024]{1,0:T(8,128)(2,1)S(1)}, u32[]{:S(2)}, u32[]{:S(2)}) collective-permute-start(bf16[256,1024]{1,0:T(8,128)(2,1)} %get-tuple-element.307), channel_id=1, source_target_pairs={{0,8},{8,16},{16,24},{24,32},{32,40},{40,48},{48,56},{56,64},{64,7... | collective-permute-start | bytes 1572872 | tf_op jit(solution)/shard_map/while/body/eval_jaxpr/ppermute | solution.py:12
  197.5 1.7 copy-start.1
  201.3 1.4 copy-start.2
  204.5 10.3 %collective-permute-start = (bf16[256,1024]{1,0:T(8,128)(2,1)}, bf16[256,1024]{1,0:T(8,128)(2,1)S(1)}, u32[]{:S(2)}, u32[]{:S(2)}) collective-permute-start(bf16[256,1024]{1,0:T(8,128)(2,1)} %get-tuple-element.307), channel_id=1, source_target_pairs={{0,8},{8,16},{16,24},{24,32},{32,40},{40,48},{48,56},{56,64},{64,7... | collective-permute-start | bytes 1572872 | tf_op jit(solution)/shard_map/while/body/eval_jaxpr/ppermute | solution.py:12
  210.9 1.7 copy-start.1
  214.8 1.4 copy-start.2
  218.0 10.3 %collective-permute-start = (bf16[256,1024]{1,0:T(8,128)(2,1)}, bf16[256,1024]{1,0:T(8,128)(2,1)S(1)}, u32[]{:S(2)}, u32[]{:S(2)}) collective-permute-start(bf16[256,1024]{1,0:T(8,128)(2,1)} %get-tuple-element.307), channel_id=1, source_target_pairs={{0,8},{8,16},{16,24},{24,32},{32,40},{40,48},{48,56},{56,64},{64,7... | collective-permute-start | bytes 1572872 | tf_op jit(solution)/shard_map/while/body/eval_jaxpr/ppermute | solution.py:12
  224.4 1.7 copy-start.1
  228.2 1.4 copy-start.2
  231.4 10.3 %collective-permute-start = (bf16[256,1024]{1,0:T(8,128)(2,1)}, bf16[256,1024]{1,0:T(8,128)(2,1)S(1)}, u32[]{:S(2)}, u32[]{:S(2)}) collective-permute-start(bf16[256,1024]{1,0:T(8,128)(2,1)} %get-tuple-element.307), channel_id=1, source_target_pairs={{0,8},{8,16},{16,24},{24,32},{32,40},{40,48},{48,56},{56,64},{64,7... | collective-permute-start | bytes 1572872 | tf_op jit(solution)/shard_map/while/body/eval_jaxpr/ppermute | solution.py:12
  237.9 1.7 copy-start.1
  241.7 1.4 copy-start.2
  244.9 12.5 %collective-permute-start = (bf16[256,1024]{1,0:T(8,128)(2,1)}, bf16[256,1024]{1,0:T(8,128)(2,1)S(1)}, u32[]{:S(2)}, u32[]{:S(2)}) collective-permute-start(bf16[256,1024]{1,0:T(8,128)(2,1)} %get-tuple-element.307), channel_id=1, source_target_pairs={{0,8},{8,16},{16,24},{24,32},{32,40},{40,48},{48,56},{56,64},{64,7... | collective-permute-start | bytes 1572872 | tf_op jit(solution)/shard_map/while/body/eval_jaxpr/ppermute | solution.py:12
  253.5 1.7 copy-start.1
  257.3 1.4 copy-start.2
  260.5 13.9 %collective-permute-start = (bf16[256,1024]{1,0:T(8,128)(2,1)}, bf16[256,1024]{1,0:T(8,128)(2,1)S(1)}, u32[]{:S(2)}, u32[]{:S(2)}) collective-permute-start(bf16[256,1024]{1,0:T(8,128)(2,1)} %get-tuple-element.307), channel_id=1, source_target_pairs={{0,8},{8,16},{16,24},{24,32},{32,40},{40,48},{48,56},{56,64},{64,7... | collective-permute-start | bytes 1572872 | tf_op jit(solution)/shard_map/while/body/eval_jaxpr/ppermute | solution.py:12
  270.6 1.7 copy-start.1
  277.6 13.9 %collective-permute-start = (bf16[256,1024]{1,0:T(8,128)(2,1)}, bf16[256,1024]{1,0:T(8,128)(2,1)S(1)}, u32[]{:S(2)}, u32[]{:S(2)}) collective-permute-start(bf16[256,1024]{1,0:T(8,128)(2,1)} %get-tuple-element.307), channel_id=1, source_target_pairs={{0,8},{8,16},{16,24},{24,32},{32,40},{40,48},{48,56},{56,64},{64,7... | collective-permute-start | bytes 1572872 | tf_op jit(solution)/shard_map/while/body/eval_jaxpr/ppermute | solution.py:12
  287.7 1.7 copy-start.1
  (2 other events, 2.7 us)
Sparse Core Ops, SparseCore 0:
  9.8 75.3 all-gather.1
  307.5 101.6 reduce-scatter.1
where the time goes:
time: 419 us; the launch traced here: 416 us
  waiting for transfers between devices  173 us (41%)
  starting transfers between devices  99.1 us (24%)
  matrix products  85.7 us (20%)
  local copies, waits for them, and re-layouts  21.5 us (5%)
  other arithmetic  21.4 us (5%)
  between operations  13.5 us (3%)
    reduce_scatter x1, waiting for transfers between devices, shards(): lax.psum_scatter(lax.dot_general(out_proj, mixed_rows, (((1,), (1,)), (()...  102 us
    ppermute x15, starting transfers between devices, passed_along(): return lax.ppermute(block, axis, route)  99 us
    all_gather x1, waiting for transfers between devices, shards(): all_taps = lax.all_gather(filter_taps, 'seq', axis=0, tiled=True)  70.8 us
    dot_general x32, matrix products, transform(): jnp.dot(tables[1], time_rows, preferred_element_type=jnp.float32)  39.5 us
    dot_general x32, matrix products, transform(): first = jnp.dot(tables[0], time_rows, preferred_element_type=jnp.float32)  33.5 us
    while x75, local copies, waits for them, and re-layouts  19.8 us
    dot_general x1, matrix products, shards(): lax.dot_general(out_proj, mixed_rows, (((1,), (1,)), ((), ())), preferred...  9.48 us
  transfers between devices with their start and end apart: 17, of which 2 were waited for; matrix products, arithmetic and copies ran while one was open for 15% of the time, Pallas kernels for 0%

commit v1 on v0

v1 whole, which is shorter than its diff:
```python
import numpy as np

import jax
import jax.numpy as jnp
from jax import lax
from jax.experimental import pallas as pl
from jax.experimental.pallas import tpu as pltpu
from jax.sharding import PartitionSpec as P

F32, BF16 = jnp.float32, jnp.bfloat16


def split_bf16(table):
    high = table.astype(BF16)
    low = (table - high.astype(np.float64)).astype(BF16)
    return high, low


def transform_tables(n):
    freq = np.arange(n, dtype=np.float64) + 0.5
    angle = np.pi / n * np.outer(np.arange(n, dtype=np.float64), freq)
    forward = np.concatenate([np.cos(angle), -np.sin(angle)], axis=1)
    inverse = np.concatenate([np.cos(angle).T, -np.sin(angle).T], axis=0) / n
    return split_bf16(forward) + split_bf16(inverse)


def prepare_kernel(in_gate, signal, taps, out_gate, packed, out_gate_t):
    gated = (in_gate[...].astype(F32) * signal[...].astype(F32)).astype(BF16)
    parts, both, tokens = packed.shape
    half = both // 2
    packed[:, :half, :] = gated.T.reshape(parts, half, tokens)
    packed[:, half:, :] = taps[...].T.reshape(parts, half, tokens)
    out_gate_t[...] = out_gate[...].T


def prepare(in_gate, signal, taps, out_gate, parts):
    tokens, channels = in_gate.shape
    per_part = channels // parts
    wide = 128
    block = pl.BlockSpec((tokens, wide), lambda i: (0, i))
    return pl.pallas_call(
        prepare_kernel,
        grid=(channels // wide,),
        in_specs=[block] * 4,
        out_specs=[
            pl.BlockSpec((wide // per_part, 2 * per_part, tokens), lambda i: (i, 0, 0)),
            pl.BlockSpec((wide, tokens), lambda i: (i, 0)),
        ],
        out_shape=[
            jax.ShapeDtypeStruct((parts, 2 * per_part, tokens), BF16),
            jax.ShapeDtypeStruct((channels, tokens), BF16),
        ],
        name="prepare",
    )(in_gate, signal, taps, out_gate)


def conv_kernel(packed, fwd_high, fwd_low, inv_high, inv_low, skip, out, g_spec, p_spec, acc_high, acc_low):
    blocks, both, n = packed.shape
    ch = both // 2
    lane = lax.broadcasted_iota(jnp.int32, (1, n), 1)
    sign = jnp.where(lane % 2 == 0, 1.0, -1.0).astype(F32)

    def transform(rows):
        return jnp.dot(rows, fwd_high[...], preferred_element_type=F32) + jnp.dot(
            rows, fwd_low[...], preferred_element_type=F32
        )

    group = 4
    tail = None
    for b in range(0, blocks, group):
        rows = packed[b : b + group]
        g_spec[b : b + group] = transform(rows[:, :ch].reshape(group * ch, n)).reshape(group, ch, 2 * n)
        h = transform(rows[:, ch:].reshape(group * ch, n)).reshape(group, ch, 2 * n)
        for j in range(group):
            if tail is None:
                p_spec[b + j] = h[j]
            else:
                p_spec[b + j, :, :n] = h[j, :, :n] - sign * tail[:, n:]
                p_spec[b + j, :, n:] = h[j, :, n:] + sign * tail[:, :n]
            tail = h[j]

    lanes, subs = 128, 16

    def products(step, carry):
        rows = pl.ds(pl.multiple_of(step * subs, subs), subs)
        for f in range(0, n, lanes):
            re, im = slice(f, f + lanes), slice(n + f, n + f + lanes)
            for i in range(blocks):
                acc_re = acc_im = None
                for a in range(i + 1):
                    gr, gi = g_spec[a, rows, re], g_spec[a, rows, im]
                    pr, pi = p_spec[i - a, rows, re], p_spec[i - a, rows, im]
                    t_re, t_im = gr * pr - gi * pi, gr * pi + gi * pr
                    acc_re = t_re if acc_re is None else acc_re + t_re
                    acc_im = t_im if acc_im is None else acc_im + t_im
                for value, cols in ((acc_re, re), (acc_im, im)):
                    high = value.astype(BF16)
                    acc_high[i, rows, cols] = high
                    acc_low[i, rows, cols] = (value - high.astype(F32)).astype(BF16)
        return carry

    lax.fori_loop(0, ch // subs, products, 0)

    for b in range(0, blocks, group):
        high = acc_high[b : b + group].reshape(group * ch, 2 * n)
        low = acc_low[b : b + group].reshape(group * ch, 2 * n)
        conv = (
            jnp.dot(high, inv_high[...], preferred_element_type=F32)
            + jnp.dot(low, inv_high[...], preferred_element_type=F32)
            + jnp.dot(high, inv_low[...], preferred_element_type=F32)
        ).reshape(group, ch, n)
        gated = packed[b : b + group, :ch, :].astype(F32)
        out[b : b + group] = (conv + skip[...][None] * gated).astype(BF16)


def convolve(packed, skip):
    blocks, both, n = packed.shape
    ch = both // 2
    tables = transform_tables(n)
    return pl.pallas_call(
        conv_kernel,
        in_specs=[pl.BlockSpec(memory_space=pltpu.VMEM)] * 6,
        out_specs=pl.BlockSpec(memory_space=pltpu.VMEM),
        out_shape=jax.ShapeDtypeStruct((blocks, ch, n), BF16),
        scratch_shapes=[
            pltpu.VMEM((blocks, ch, 2 * n), F32),
            pltpu.VMEM((blocks, ch, 2 * n), F32),
            pltpu.VMEM((blocks, ch, 2 * n), BF16),
            pltpu.VMEM((blocks, ch, 2 * n), BF16),
        ],
        compiler_params=pltpu.CompilerParams(vmem_limit_bytes=40 * 2**20),
        name="convolve",
    )(packed, *(jnp.asarray(t) for t in tables), skip)


def shards(out_gate, in_gate, signal, filter_taps, skip_gain, out_proj):
    tokens, channels = out_gate.shape
    parts, chans = lax.axis_size("seq"), lax.axis_size("chan")
    per_part = channels // parts
    packed, out_gate_t = prepare(in_gate, signal, filter_taps, out_gate, parts)
    packed = lax.all_to_all(packed, "seq", 0, 0)
    skip = lax.dynamic_slice_in_dim(skip_gain, lax.axis_index("seq") * per_part, per_part, 0)
    conv = convolve(packed, skip[:, None])
    conv = lax.all_to_all(conv, "seq", 0, 0).reshape(channels, tokens)
    mixed = (out_gate_t.astype(F32) * conv.astype(F32)).astype(BF16)
    partial = jnp.dot(out_proj, mixed, preferred_element_type=F32).astype(BF16)
    shares = lax.all_to_all(partial.reshape(chans, -1, tokens), "chan", 0, 0)
    return jnp.sum(shares.astype(F32), axis=0).T.astype(BF16)


def solution(mesh):
    return jax.shard_map(
        shards,
        mesh=mesh,
        in_specs=(
            P("seq", "chan"),
            P("seq", "chan"),
            P("seq", "chan"),
            P("seq", "chan"),
            P("chan"),
            P(None, "chan"),
        ),
        out_specs=P("seq", "chan"),
        check_vma=False,
    )
```

time: 419 us -> 123 us (0.29)
  waiting for transfers between devices: 173 us -> 17.8 us
  starting transfers between devices: 99.1 us -> 7.12 us
  matrix products: 85.7 us -> 8.34 us
  blocking collectives: 0 us -> 69.1 us
  other arithmetic: 21.4 us -> 4 us
  local copies, waits for them, and re-layouts: 21.5 us -> 4.42 us
  between operations: 13.5 us -> 0.05 us
  Pallas kernels: 0 us -> 11.1 us
    reduce_scatter x1 -> x0, waiting for transfers between devices: 102 us -> none  [shards(): lax.psum_scatter(lax.dot_general(out_proj, mixed_rows, (((1,), (1,)), (()...]
    ppermute x15 -> x0, starting transfers between devices: 99 us -> none  [passed_along(): return lax.ppermute(block, axis, route)]
    dot_general x66 -> x1, matrix products: 85.7 us -> 8.34 us  [shards(): partial = jnp.dot(out_proj, mixed, preferred_element_type=F32).astype(BF16)]
    all_gather x1 -> x0, waiting for transfers between devices: 70.8 us -> none  [shards(): all_taps = lax.all_gather(filter_taps, 'seq', axis=0, tiled=True)]
    all_to_all x0 -> x2, blocking collectives: none -> 69.1 us  [the longest x1 54.2 us: shards(): shares = lax.all_to_all(partial.reshape(chans, -1, tokens), 'chan', 0, 0)]
    while x75 -> x0, local copies, waits for them, and re-layouts: 19.8 us -> none
    all_to_all x0 -> x1, waiting for transfers between devices: none -> 17.8 us  [shards(): packed = lax.all_to_all(packed, 'seq', 0, 0)]
    pallas_call x0 -> x2, Pallas kernels: none -> 11.1 us  [the longest x1 5.79 us: prepare(): pl.pallas_call(prepare_kernel, grid=(channels // wide,), in_specs=[block]...]
  transfers between devices with their start and end apart: 17 -> 1, of which waited for: 2 -> 1; matrix products, arithmetic and copies ran while one was open for 15% -> 0% of each run, Pallas kernels for 0% -> 0%
where the time goes in v1:
time: 123 us; the launch traced here: 122 us
  blocking collectives  69.1 us (56%)
  waiting for transfers between devices  17.8 us (14%)
  Pallas kernels  11.1 us (9%)
  matrix products  8.34 us (7%)
  starting transfers between devices  7.12 us (6%)
  local copies, waits for them, and re-layouts  4.42 us (4%)
  other arithmetic  4 us (3%)
    all_to_all x1, blocking collectives, shards(): shares = lax.all_to_all(partial.reshape(chans, -1, tokens), 'chan', 0, 0)  54.2 us
    all_to_all x1, waiting for transfers between devices, shards(): packed = lax.all_to_all(packed, 'seq', 0, 0)  17.8 us
    all_to_all x1, blocking collectives, shards(): conv = lax.all_to_all(conv, 'seq', 0, 0).reshape(channels, tokens)  15 us
    dot_general x1, matrix products, shards(): partial = jnp.dot(out_proj, mixed, preferred_element_type=F32).astype(BF16)  8.34 us
    all_to_all x1, starting transfers between devices, shards(): packed = lax.all_to_all(packed, 'seq', 0, 0)  7.12 us
    pallas_call x1, Pallas kernels, prepare(): pl.pallas_call(prepare_kernel, grid=(channels // wide,), in_specs=[block]...  5.79 us
    pallas_call x1, Pallas kernels, convolve(): pl.pallas_call(conv_kernel, in_specs=[pl.BlockSpec(memory_space=pltpu.VME...  5.32 us
    reduce_sum x1, other arithmetic, shards(): return jnp.sum(shares.astype(F32), axis=0).T.astype(BF16)  4 us
  transfers between devices with their start and end apart: 1, of which 1 were waited for; matrix products, arithmetic and copies ran while one was open for 0% of the time, Pallas kernels for 0%

profile of v1, /device:TPU:0, one launch (start us, length us, event | category | flops | bytes accessed | tf_op | source)
XLA Modules:
  0.0 122.0 jit_solution(3246463566161892731)
XLA Ops:
  0.0 0.0 copy-start
  0.0 5.8 %prepare.1 = (bf16[16,128,256]{2,1,0:T(8,128)(2,1)}, bf16[1024,256]{1,0:T(8,128)(2,1)}) custom-call(bf16[256,1024]{1,0:T(8,128)(2,1)} %in_gate.1, bf16[256,1024]{1,0:T(8,128)(2,1)} %signal.1, bf16[256,1024]{1,0:T(8,128)(2,1)} %taps.1, bf16[256,1024]{1,0:T(8,128)(2,1)} %out_gate.1), custom_call_target="tpu_custom_call" | custom-call | tf_op jit(solution)/shard_map/prepare/pallas_call | solution.py:41
  5.8 7.1 %all-to-all-start = ((bf16[16,128,256]{2,1,0:T(8,128)(2,1)}), bf16[16,128,256]{2,1,0:T(8,128)(2,1)S(1)}, u32[]{:S(2)}, u32[]{:S(2)}) async-start(bf16[16,128,256]{2,1,0:T(8,128)(2,1)} %get-tuple-element.8), calls=%async_computation | async-start | bytes 2097152 | tf_op jit(solution)/shard_map/all_to_all | solution.py:141
  12.9 0.0 copy-done
  12.9 0.1 dynamic-slice_bitcast_fusion
  13.0 0.1 copy.12.skip
  13.1 17.8 %all-to-all-done.packed = bf16[16,128,256]{2,1,0:T(8,128)(2,1)S(1)} async-done(((bf16[16,128,256]{2,1,0:T(8,128)(2,1)}), bf16[16,128,256]{2,1,0:T(8,128)(2,1)S(1)}, u32[]{:S(2)}, u32[]{:S(2)}) %all-to-all-start) | async-done | bytes 1048608 | tf_op jit(solution)/shard_map/all_to_all | solution.py:141
  30.9 0.0 copy-start.1
  30.9 0.9 copy-done.1
  31.9 0.0 copy-start.2
  31.9 0.9 copy-done.2
  32.8 0.0 copy-start.3
  32.8 0.9 copy-done.3
  33.8 0.0 copy-start.4
  33.8 0.9 copy-done.4
  34.7 5.3 %convolve.1 = bf16[16,64,256]{2,1,0:T(8,128)(2,1)S(1)} custom-call(bf16[16,128,256]{2,1,0:T(8,128)(2,1)S(1)} %all-to-all-done.packed, bf16[256,512]{1,0:T(8,128)(2,1)S(1)} %copy-done.4, bf16[256,512]{1,0:T(8,128)(2,1)S(1)} %copy-done.3, bf16[512,256]{1,0:T(8,128)(2,1)S(1)} %copy-done.2, bf16[512,256]{1,0:T(8,128)(2,1)S(1)} %copy-done.1, f32[64,1]{1,0:T(8,128)S(1)} %copy.12.skip), custom_call_target="tpu_custom_call" | custom-call | tf_op jit(solution)/shard_map/convolve/pallas_call | solution.py:120
  40.1 15.0 %all_to_all.15 = bf16[16,64,256]{2,1,0:T(8,128)(2,1)S(1)} all-to-all(bf16[16,64,256]{2,1,0:T(8,128)(2,1)S(1)} %convolve.1), channel_id=1, replica_groups=mesh['seq'=16,'chan'=8] {'seq'}, dimensions={0} | all-to-all | bytes 1048576 | tf_op jit(solution)/shard_map/all_to_all | solution.py:144
  55.1 8.3 %convolution_convert_fusion = bf16[256,8192]{1,0:T(8,128)(2,1)S(1)} fusion(bf16[8192,1024]{1,0:T(8,128)(2,1)} %param.15, bf16[1024,256]{1,0:T(8,128)(2,1)S(1)} %bitcast.13, bf16[1024,256]{1,0:T(8,128)(2,1)} %get-tuple-element.7), kind=kOutput, calls=%fused_computation | convolution fusion | flops 4298113024 | bytes 22020096 | tf_op jit(solution)/shard_map/dot_general | solution.py:146
  63.4 0.4 copy.16
  63.9 54.2 %all_to_all.16 = bf16[8,1024,256]{1,2,0:T(8,128)(2,1)} all-to-all(bf16[8,1024,256]{1,2,0:T(8,128)(2,1)S(1)} %bitcast.11), channel_id=1, replica_groups=mesh['seq'=16,'chan'=8] {'chan'}, dimensions={0} | all-to-all | bytes 8388608 | tf_op jit(solution)/shard_map/all_to_all | solution.py:147
  118.0 4.0 %reduce_sum.12 = bf16[1024,256]{0,1:T(8,128)(2,1)} reduce(bf16[8,1024,256]{1,2,0:T(8,128)(2,1)} %all_to_all.16, bf16[]{:T(256)} %constant.22.clone.1), dimensions={0}, to_apply=%region_0.0 | reduce | flops 1835008 | bytes 4718594 | tf_op jit(solution)/shard_map/reduce_sum | solution.py:148
Async XLA Ops:
  0.0 12.9 %copy-start = (f32[1024]{0:T(1024)S(1)}, f32[1024]{0:T(1024)}, u32[]{:S(2)}) copy-start(f32[1024]{0:T(1024)} %param.14) | copy-start | bytes 12292
  5.8 25.1 %all-to-all-start = ((bf16[16,128,256]{2,1,0:T(8,128)(2,1)}), bf16[16,128,256]{2,1,0:T(8,128)(2,1)S(1)}, u32[]{:S(2)}, u32[]{:S(2)}) async-start(bf16[16,128,256]{2,1,0:T(8,128)(2,1)} %get-tuple-element.8), calls=%async_computation | async-start | bytes 2097152 | tf_op jit(solution)/shard_map/all_to_all | solution.py:141
  30.9 1.0 copy-start.1
  31.9 0.9 copy-start.2
  32.8 0.9 copy-start.3
  33.8 0.9 copy-start.4

commit v2 on v1

--- a/solution.py
+++ b/solution.py
@@ -16,12 +16,12 @@
     return high, low
 
 
-def transform_tables(n):
+def transform_table(n):
     freq = np.arange(n, dtype=np.float64) + 0.5
     angle = np.pi / n * np.outer(np.arange(n, dtype=np.float64), freq)
     forward = np.concatenate([np.cos(angle), -np.sin(angle)], axis=1)
-    inverse = np.concatenate([np.cos(angle).T, -np.sin(angle).T], axis=0) / n
-    return split_bf16(forward) + split_bf16(inverse)
+    high, low = split_bf16(forward)
+    return np.concatenate([high, low], axis=0)
 
 
 def prepare_kernel(in_gate, signal, taps, out_gate, packed, out_gate_t):
@@ -54,16 +54,19 @@
     )(in_gate, signal, taps, out_gate)
 
 
-def conv_kernel(packed, fwd_high, fwd_low, inv_high, inv_low, skip, out, g_spec, p_spec, acc_high, acc_low):
+def conv_kernel(packed, table, skip, out, g_spec, p_spec, acc_high, acc_low):
     blocks, both, n = packed.shape
     ch = both // 2
     lane = lax.broadcasted_iota(jnp.int32, (1, n), 1)
     sign = jnp.where(lane % 2 == 0, 1.0, -1.0).astype(F32)
 
     def transform(rows):
-        return jnp.dot(rows, fwd_high[...], preferred_element_type=F32) + jnp.dot(
-            rows, fwd_low[...], preferred_element_type=F32
+        return jnp.dot(rows, table[:n], preferred_element_type=F32) + jnp.dot(
+            rows, table[n:], preferred_element_type=F32
         )
+
+    def inverse(spectra, part):
+        return lax.dot_general(spectra, part, (((1,), (1,)), ((), ())), preferred_element_type=F32)
 
     group = 4
     tail = None
@@ -104,11 +107,8 @@
     for b in range(0, blocks, group):
         high = acc_high[b : b + group].reshape(group * ch, 2 * n)
         low = acc_low[b : b + group].reshape(group * ch, 2 * n)
-        conv = (
-            jnp.dot(high, inv_high[...], preferred_element_type=F32)
-            + jnp.dot(low, inv_high[...], preferred_element_type=F32)
-            + jnp.dot(high, inv_low[...], preferred_element_type=F32)
-        ).reshape(group, ch, n)
+        conv = inverse(high, table[:n]) + inverse(low, table[:n]) + inverse(high, table[n:])
+        conv = (conv * (1.0 / n)).reshape(group, ch, n)
         gated = packed[b : b + group, :ch, :].astype(F32)
         out[b : b + group] = (conv + skip[...][None] * gated).astype(BF16)
 
@@ -116,10 +116,9 @@
 def convolve(packed, skip):
     blocks, both, n = packed.shape
     ch = both // 2
-    tables = transform_tables(n)
     return pl.pallas_call(
         conv_kernel,
-        in_specs=[pl.BlockSpec(memory_space=pltpu.VMEM)] * 6,
+        in_specs=[pl.BlockSpec(memory_space=pltpu.VMEM)] * 3,
         out_specs=pl.BlockSpec(memory_space=pltpu.VMEM),
         out_shape=jax.ShapeDtypeStruct((blocks, ch, n), BF16),
         scratch_shapes=[
@@ -130,7 +129,65 @@
         ],
         compiler_params=pltpu.CompilerParams(vmem_limit_bytes=40 * 2**20),
         name="convolve",
-    )(packed, *(jnp.asarray(t) for t in tables), skip)
+    )(packed, jnp.asarray(transform_table(n)), skip)
+
+
+def project_kernel(order, weight, gate, conv, out, mixed):
+    @pl.when(pl.program_id(0) == 0)
+    def _():
+        mixed[...] = (gate[...].astype(F32) * conv[...].astype(F32)).astype(BF16)
+
+    out[0] = jnp.dot(weight[...], mixed[...], preferred_element_type=F32).astype(BF16)
+
+
+def project(weight, gate, conv, starts, rows):
+    channels, tokens = conv.shape
+    count = len(starts)
+    whole = pl.BlockSpec((channels, tokens), lambda i, order: (0, 0))
+    return pl.pallas_call(
+        project_kernel,
+        grid_spec=pltpu.PrefetchScalarGridSpec(
+            num_scalar_prefetch=1,
+            grid=(count,),
+            in_specs=[
+                pl.BlockSpec((pl.Element(rows), pl.Element(channels)), lambda i, order: (pl.multiple_of(order[i], 16), 0)),
+                whole,
+                whole,
+            ],
+            out_specs=pl.BlockSpec((1, rows, tokens), lambda i, order: (i, 0, 0)),
+            scratch_shapes=[pltpu.VMEM((channels, tokens), BF16)],
+        ),
+        out_shape=jax.ShapeDtypeStruct((count, rows, tokens), BF16),
+        cost_estimate=pl.CostEstimate(
+            flops=2 * count * rows * channels * tokens,
+            bytes_accessed=2 * (count * rows * (channels + tokens) + 2 * channels * tokens),
+            transcendentals=0,
+        ),
+        name="project",
+    )(jnp.stack(starts).astype(jnp.int32), weight, gate, conv)
+
+
+Z = 4
+
+
+def to_z(block, step):
+    n = lax.axis_size("chan")
+    return lax.ppermute(block, "chan", [(i, i // Z * Z + (i + step) % Z) for i in range(n)])
+
+
+def to_other_x(block):
+    n = lax.axis_size("chan")
+    return lax.ppermute(block, "chan", [(i, (i + Z) % n) for i in range(n)])
+
+
+def reduce_z(plus, minus, keep_plus, keep_minus, own_first, own_second):
+    from_below, from_above = to_z(plus, 1), to_z(minus, -1)
+    k = keep_plus.shape[0]
+    up = to_z((keep_plus.astype(F32) + from_below[:k].astype(F32)).astype(BF16), 1)
+    down = to_z((keep_minus.astype(F32) + from_above[:k].astype(F32)).astype(BF16), -1)
+    first = own_first.astype(F32) + from_above[k:].astype(F32) + up.astype(F32)
+    second = own_second.astype(F32) + from_below[k:].astype(F32) + down.astype(F32)
+    return first, second
 
 
 def shards(out_gate, in_gate, signal, filter_taps, skip_gain, out_proj):
@@ -142,10 +199,39 @@
     skip = lax.dynamic_slice_in_dim(skip_gain, lax.axis_index("seq") * per_part, per_part, 0)
     conv = convolve(packed, skip[:, None])
     conv = lax.all_to_all(conv, "seq", 0, 0).reshape(channels, tokens)
-    mixed = (out_gate_t.astype(F32) * conv.astype(F32)).astype(BF16)
-    partial = jnp.dot(out_proj, mixed, preferred_element_type=F32).astype(BF16)
-    shares = lax.all_to_all(partial.reshape(chans, -1, tokens), "chan", 0, 0)
-    return jnp.sum(shares.astype(F32), axis=0).T.astype(BF16)
+
+    me = lax.axis_index("chan")
+    x, z = me // Z, me % Z
+    chunk = out_proj.shape[0] // chans
+    half_a = 192
+    half_b = chunk // 2 - half_a
+
+    def at(flip, step, offset):
+        return (((x + flip) % 2) * Z + (z + step) % Z) * chunk + offset
+
+    a1, a2, b1, b2 = 0, half_a, 2 * half_a, 2 * half_a + half_b
+    order = [(2, 0), (1, 1), (2, 1), (3, 0), (1, 0), (3, 1), (0, 0), (0, 1)]
+    rows_a = lambda flip: [at(flip, s, (a1, a2)[h]) for s, h in order]
+    rows_b = [at(flip, s, (b1, b2)[h]) for s, h in order for flip in (0, 1)]
+    run = lambda starts, rows: project(out_proj, out_gate_t, conv, starts, rows)
+
+    from_x = to_other_x(run(rows_a(1), half_a))
+    plus_b = run(rows_b[:4], half_b)
+    minus_b = run(rows_b[4:8], half_b)
+    rest_b = run(rows_b[8:], half_b)
+    own_a = run(rows_a(0), half_a)
+
+    def summed_a(lo, hi):
+        return own_a[lo:hi].astype(F32) + from_x[lo:hi].astype(F32)
+
+    b_first, b_second = reduce_z(plus_b, minus_b, rest_b[:2], rest_b[2:4], rest_b[4:6], rest_b[6:8])
+    other_b = to_other_x(jnp.stack([b_first[1], b_second[1]]).astype(BF16)).astype(F32)
+    a_first, a_second = reduce_z(
+        summed_a(0, 2).astype(BF16), summed_a(2, 4).astype(BF16),
+        summed_a(4, 5), summed_a(5, 6), summed_a(6, 7), summed_a(7, 8),
+    )
+    rows = [a_first[0], a_second[0], b_first[0] + other_b[0], b_second[0] + other_b[1]]
+    return jnp.concatenate([r.astype(BF16) for r in rows], axis=0).T
 
 
 def solution(mesh):

time: 123 us -> 128 us (1.041)
  blocking collectives: 69.1 us -> 0 us
  Pallas kernels: 11.1 us -> 46.6 us
  waiting for transfers between devices: 17.8 us -> 51.1 us
  starting transfers between devices: 7.12 us -> 22.1 us
  matrix products: 8.34 us -> 0 us
    all_to_all x2 -> x0, blocking collectives: 69.1 us -> none  [the longest x1 54.2 us: shards(): shares = lax.all_to_all(partial.reshape(chans, -1, tokens), 'chan', 0, 0)]
    pallas_call x0 -> x5, Pallas kernels: none -> 34.6 us  [project(): pl.pallas_call(project_kernel, grid_spec=pltpu.PrefetchScalarGridSpec(num...]
    ppermute x0 -> x10, waiting for transfers between devices: none -> 21.6 us  [the longest x8 16 us: to_z(): lax.ppermute(block, 'chan', [(i, i // Z * Z + (i + step) % Z) for i in ra...]
    all_to_all x0 -> x1, waiting for transfers between devices: none -> 11.6 us  [shards(): conv = lax.all_to_all(conv, 'seq', 0, 0).reshape(channels, tokens)]
    ppermute x0 -> x10, starting transfers between devices: none -> 11.2 us  [the longest x8 9.12 us: to_z(): lax.ppermute(block, 'chan', [(i, i // Z * Z + (i + step) % Z) for i in ra...]
    dot_general x1 -> x0, matrix products: 8.34 us -> none  [shards(): partial = jnp.dot(out_proj, mixed, preferred_element_type=F32).astype(BF16)]
    reduce_sum x1 -> x0, other arithmetic: 4 us -> none  [shards(): return jnp.sum(shares.astype(F32), axis=0).T.astype(BF16)]
    all_to_all x0 -> x1, starting transfers between devices: none -> 3.57 us  [shards(): conv = lax.all_to_all(conv, 'seq', 0, 0).reshape(channels, tokens)]
  transfers between devices with their start and end apart: 1 -> 12, of which waited for: 1 -> 6; matrix products, arithmetic and copies ran while one was open for 0% -> 4% of each run, Pallas kernels for 0% -> 21%
where the time goes in v2:
time: 128 us; the launch traced here: 127 us
  waiting for transfers between devices  51.1 us (40%)
  Pallas kernels  46.6 us (36%)
  starting transfers between devices  22.1 us (17%)
  local copies, waits for them, and re-layouts  3.97 us (3%)
  other arithmetic  3.23 us (3%)
    pallas_call x5, Pallas kernels, project(): pl.pallas_call(project_kernel, grid_spec=pltpu.PrefetchScalarGridSpec(num...  34.6 us
    all_to_all x1, waiting for transfers between devices, shards(): packed = lax.all_to_all(packed, 'seq', 0, 0)  17.8 us
    ppermute x8, waiting for transfers between devices, to_z(): lax.ppermute(block, 'chan', [(i, i // Z * Z + (i + step) % Z) for i in ra...  16 us
    all_to_all x1, waiting for transfers between devices, shards(): conv = lax.all_to_all(conv, 'seq', 0, 0).reshape(channels, tokens)  11.6 us
    ppermute x8, starting transfers between devices, to_z(): lax.ppermute(block, 'chan', [(i, i // Z * Z + (i + step) % Z) for i in ra...  9.12 us
    all_to_all x1, starting transfers between devices, shards(): packed = lax.all_to_all(packed, 'seq', 0, 0)  7.25 us
    pallas_call x1, Pallas kernels, convolve(): pl.pallas_call(conv_kernel, in_specs=[pl.BlockSpec(memory_space=pltpu.VME...  6.21 us
    pallas_call x1, Pallas kernels, prepare(): pl.pallas_call(prepare_kernel, grid=(channels // wide,), in_specs=[block]...  5.79 us
  transfers between devices with their start and end apart: 12, of which 6 were waited for; matrix products, arithmetic and copies ran while one was open for 4% of the time, Pallas kernels for 21%

profile of v2, /device:TPU:0, one launch (start us, length us, event | category | flops | bytes accessed | tf_op | source)
XLA Modules:
  0.0 127.2 jit_solution(5031582220791526342)
XLA Ops:
  0.0 5.8 %prepare.1 = (bf16[16,128,256]{2,1,0:T(8,128)(2,1)}, bf16[1024,256]{1,0:T(8,128)(2,1)}) custom-call(bf16[256,1024]{1,0:T(8,128)(2,1)} %in_gate.1, bf16[256,1024]{1,0:T(8,128)(2,1)} %signal.1, bf16[256,1024]{1,0:T(8,128)(2,1)} %taps.1, bf16[256,1024]{1,0:T(8,128)(2,1)} %out_gate.1), custom_call_target="tpu_custom_call" | custom-call | tf_op jit(solution)/shard_map/prepare/pallas_call | solution.py:41
  5.8 7.2 %all-to-all-start = ((bf16[16,128,256]{2,1,0:T(8,128)(2,1)}), bf16[16,128,256]{2,1,0:T(8,128)(2,1)S(1)}, u32[]{:S(2)}, u32[]{:S(2)}) async-start(bf16[16,128,256]{2,1,0:T(8,128)(2,1)} %get-tuple-element.8), calls=%async_computation | async-start | bytes 2097152 | tf_op jit(solution)/shard_map/all_to_all | solution.py:198
  13.1 0.1 dynamic-slice_bitcast_fusion
  13.1 0.1 copy.8.skip
  13.2 17.8 %all-to-all-done.packed = bf16[16,128,256]{2,1,0:T(8,128)(2,1)S(1)} async-done(((bf16[16,128,256]{2,1,0:T(8,128)(2,1)}), bf16[16,128,256]{2,1,0:T(8,128)(2,1)S(1)}, u32[]{:S(2)}, u32[]{:S(2)}) %all-to-all-start) | async-done | bytes 1048608 | tf_op jit(solution)/shard_map/all_to_all | solution.py:198
  31.1 6.2 %convolve.1 = bf16[16,64,256]{2,1,0:T(8,128)(2,1)} custom-call(bf16[16,128,256]{2,1,0:T(8,128)(2,1)S(1)} %all-to-all-done.packed, bf16[512,512]{1,0:T(8,128)(2,1)S(1)} %copy-done.1, f32[64,1]{1,0:T(8,128)S(1)} %copy.8.skip), custom_call_target="tpu_custom_call" | custom-call | tf_op jit(solution)/shard_map/convolve/pallas_call | solution.py:119
  37.3 3.6 %all-to-all-start.1 = ((bf16[16,64,256]{2,1,0:T(8,128)(2,1)}), bf16[16,64,256]{2,1,0:T(8,128)(2,1)S(1)}, u32[]{:S(2)}, u32[]{:S(2)}) async-start(bf16[16,64,256]{2,1,0:T(8,128)(2,1)} %convolve.1), calls=%async_computation.1 | async-start | bytes 1048576 | tf_op jit(solution)/shard_map/all_to_all | solution.py:201
  41.0 0.6 stack.132.order
  41.6 11.6 %all-to-all-done.1 = bf16[16,64,256]{2,1,0:T(8,128)(2,1)S(1)} async-done(((bf16[16,64,256]{2,1,0:T(8,128)(2,1)}), bf16[16,64,256]{2,1,0:T(8,128)(2,1)S(1)}, u32[]{:S(2)}, u32[]{:S(2)}) %all-to-all-start.1) | async-done | bytes 524320 | tf_op jit(solution)/shard_map/all_to_all | solution.py:201
  53.2 0.8 copy-done.2
  54.0 7.7 %project.6 = bf16[8,192,256]{2,1,0:T(8,128)(2,1)} custom-call(s32[8]{0:T(128)} %stack.132.order, bf16[8192,1024]{1,0:T(8,128)(2,1)} %weight.9, bf16[1024,256]{1,0:T(8,128)(2,1)} %get-tuple-element.7.gate, bf16[1024,256]{1,0:T(8,128)(2,1)} %bitcast.45), custom_call_target="tpu_custom_call" | custom-call | flops 805306368 | bytes 4980736 | tf_op jit(solution)/shard_map/project/pallas_call | solution.py:147
  61.7 0.6 collective-permute-start
  62.3 0.6 pad_add_fusion.1.order
  62.9 5.4 %project.9 = bf16[4,320,256]{2,1,0:T(8,128)(2,1)} custom-call(s32[4]{0:T(128)} %pad_add_fusion.1.order, bf16[8192,1024]{1,0:T(8,128)(2,1)} %weight.9, bf16[1024,256]{1,0:T(8,128)(2,1)} %get-tuple-element.7.gate, bf16[1024,256]{1,0:T(8,128)(2,1)} %bitcast.46), custom_call_target="tpu_custom_call" | custom-call | flops 671088640 | bytes 4325376 | tf_op jit(solution)/shard_map/project/pallas_call | solution.py:147
  68.3 1.9 %collective-permute-start.6 = (bf16[4,320,256]{2,1,0:T(8,128)(2,1)}, bf16[4,320,256]{2,1,0:T(8,128)(2,1)S(1)}, u32[]{:S(2)}, u32[]{:S(2)}) collective-permute-start(bf16[4,320,256]{2,1,0:T(8,128)(2,1)} %project.9), channel_id=1, source_target_pairs={{0,1},{1,2},{2,3},{3,0},{4,5},{5,6},{6,7},{7,4},{8,9},{9,10},{10,1... | collective-permute-start | bytes 1966088 | tf_op jit(solution)/shard_map/ppermute | solution.py:175
  70.2 0.7 stack.123.order
  70.9 0.6 stack.141.order
  71.5 0.6 pad_add_fusion.order
  72.1 5.3 %project.8 = bf16[4,320,256]{2,1,0:T(8,128)(2,1)} custom-call(s32[4]{0:T(128)} %pad_add_fusion.order, bf16[8192,1024]{1,0:T(8,128)(2,1)} %weight.9, bf16[1024,256]{1,0:T(8,128)(2,1)} %get-tuple-element.7.gate, bf16[1024,256]{1,0:T(8,128)(2,1)} %bitcast.47), custom_call_target="tpu_custom_call" | custom-call | flops 671088640 | bytes 4325376 | tf_op jit(solution)/shard_map/project/pallas_call | solution.py:147
  77.5 2.1 %collective-permute-start.5 = (bf16[4,320,256]{2,1,0:T(8,128)(2,1)}, bf16[4,320,256]{2,1,0:T(8,128)(2,1)S(1)}, u32[]{:S(2)}, u32[]{:S(2)}) collective-permute-start(bf16[4,320,256]{2,1,0:T(8,128)(2,1)} %project.8), channel_id=1, source_target_pairs={{0,3},{1,0},{2,1},{3,2},{4,7},{5,4},{6,5},{7,6},{8,11},{9,8},{10,9... | collective-permute-start | bytes 1966088 | tf_op jit(solution)/shard_map/ppermute | solution.py:175
  79.6 7.7 %project.5 = bf16[8,192,256]{2,1,0:T(8,128)(2,1)} custom-call(s32[8]{0:T(128)} %stack.123.order, bf16[8192,1024]{1,0:T(8,128)(2,1)} %weight.9, bf16[1024,256]{1,0:T(8,128)(2,1)} %get-tuple-element.7.gate, bf16[1024,256]{1,0:T(8,128)(2,1)} %bitcast.48), custom_call_target="tpu_custom_call" | custom-call | flops 805306368 | bytes 4980736 | tf_op jit(solution)/shard_map/project/pallas_call | solution.py:147
  87.3 8.6 %project.7 = bf16[8,320,256]{2,1,0:T(8,128)(2,1)} custom-call(s32[8]{0:T(128)} %stack.141.order, bf16[8192,1024]{1,0:T(8,128)(2,1)} %weight.9, bf16[1024,256]{1,0:T(8,128)(2,1)} %get-tuple-element.7.gate, bf16[1024,256]{1,0:T(8,128)(2,1)} %bitcast.49), custom_call_target="tpu_custom_call" | custom-call | flops 1342177280 | bytes 7602176 | tf_op jit(solution)/shard_map/project/pallas_call | solution.py:147
  95.8 0.0 collective-permute-done
  95.8 0.1 add_convert_fusion.2
  95.9 0.1 collective-permute-start.2
  96.0 0.0 collective-permute-done.6
  96.0 1.2 add_convert_fusion.1
  97.2 1.8 %collective-permute-start.7 = (bf16[2,320,256]{2,1,0:T(8,128)(2,1)S(1)}, bf16[2,320,256]{2,1,0:T(8,128)(2,1)S(1)}, u32[]{:S(2)}, u32[]{:S(2)}) collective-permute-start(bf16[2,320,256]{2,1,0:T(8,128)(2,1)S(1)} %add_convert_fusion.1), channel_id=1, source_target_pairs={{0,1},{1,2},{2,3},{3,0},{4,5},{5,6},{6,7},{7,4},{8,9},{9,10},{10,1... | collective-permute-start | bytes 983048 | tf_op jit(solution)/shard_map/ppermute | solution.py:175
  99.0 1.5 %collective-permute-start.1 = (bf16[2,192,256]{2,1,0:T(8,128)(2,1)S(1)}, bf16[2,192,256]{2,1,0:T(8,128)(2,1)S(1)}, u32[]{:S(2)}, u32[]{:S(2)}) collective-permute-start(bf16[2,192,256]{2,1,0:T(8,128)(2,1)S(1)} %get-tuple-element.14), channel_id=1, source_target_pairs={{0,3},{1,0},{2,1},{3,2},{4,7},{5,4},{6,5},{7,6},{8,11},{9,8},{10,9... | collective-permute-start | bytes 589832 | tf_op jit(solution)/shard_map/ppermute | solution.py:175
  100.5 4.6 %collective-permute-done.2 = bf16[2,192,256]{2,1,0:T(8,128)(2,1)S(1)} collective-permute-done((bf16[2,192,256]{2,1,0:T(8,128)(2,1)S(1)}, bf16[2,192,256]{2,1,0:T(8,128)(2,1)S(1)}, u32[]{:S(2)}, u32[]{:S(2)}) %collective-permute-start.2) | collective-permute-done | bytes 196640 | tf_op jit(solution)/shard_map/ppermute | solution.py:175
  105.1 0.1 collective-permute-start.3
  105.2 0.0 collective-permute-done.5
  105.2 5.7 %collective-permute-done.7 = bf16[2,320,256]{2,1,0:T(8,128)(2,1)S(1)} collective-permute-done((bf16[2,320,256]{2,1,0:T(8,128)(2,1)S(1)}, bf16[2,320,256]{2,1,0:T(8,128)(2,1)S(1)}, u32[]{:S(2)}, u32[]{:S(2)}) %collective-permute-start.7) | collective-permute-done | bytes 327712 | tf_op jit(solution)/shard_map/ppermute | solution.py:175
  110.9 0.0 copy-done.3
  110.9 0.2 convert_add_fusion.1
  111.1 0.8 collective-permute-start.8
  111.9 0.0 collective-permute-done.1
  111.9 0.0 collective-permute-done.3
  112.0 0.1 fusion.4
  112.1 0.8 collective-permute-start.4
  112.9 5.8 %collective-permute-done.8 = bf16[2,320,256]{2,1,0:T(8,128)(2,1)S(1)} collective-permute-done((bf16[2,320,256]{2,1,0:T(8,128)(2,1)S(1)}, bf16[2,320,256]{2,1,0:T(8,128)(2,1)S(1)}, u32[]{:S(2)}, u32[]{:S(2)}) %collective-permute-start.8) | collective-permute-done | bytes 327712 | tf_op jit(solution)/shard_map/ppermute | solution.py:175
  118.6 0.1 convert_add_fusion
  118.8 1.5 %collective-permute-start.9 = (bf16[2,320,256]{2,1,0:T(8,128)(2,1)S(1)}, bf16[2,320,256]{2,1,0:T(8,128)(2,1)S(1)}, u32[]{:S(2)}, u32[]{:S(2)}) collective-permute-start(bf16[2,320,256]{2,1,0:T(8,128)(2,1)S(1)} %pad_maximum_fusion), channel_id=1, source_target_pairs={{0,4},{1,5},{2,6},{3,7},{4,0},{5,1},{6,2},{7,3},{8,12},{9,13},{10,... | collective-permute-start | bytes 983048 | tf_op jit(solution)/shard_map/ppermute | solution.py:180
  120.3 0.0 collective-permute-done.4
  120.3 0.1 fusion.5
  120.3 5.6 %collective-permute-done.9 = bf16[2,320,256]{2,1,0:T(8,128)(2,1)S(1)} collective-permute-done((bf16[2,320,256]{2,1,0:T(8,128)(2,1)S(1)}, bf16[2,320,256]{2,1,0:T(8,128)(2,1)S(1)}, u32[]{:S(2)}, u32[]{:S(2)}) %collective-permute-start.9) | collective-permute-done | bytes 327712 | tf_op jit(solution)/shard_map/ppermute | solution.py:180
  126.0 0.1 fusion.2
  126.2 1.0 copy.9
  (14 shorter events, 0.2 us)
Async XLA Ops:
  0.0 13.1 %copy-start = (f32[1024]{0:T(1024)S(1)}, f32[1024]{0:T(1024)}, u32[]{:S(2)}) copy-start(f32[1024]{0:T(1024)} %param.11) | copy-start | bytes 12292
  5.8 25.3 %copy-start.1 = (bf16[512,512]{1,0:T(8,128)(2,1)S(1)}, bf16[512,512]{1,0:T(8,128)(2,1)}, u32[]{:S(2)}) copy-start(bf16[512,512]{1,0:T(8,128)(2,1)} %constant.194.clone.table) | copy-start | bytes 1572868
  5.8 25.3 %all-to-all-start = ((bf16[16,128,256]{2,1,0:T(8,128)(2,1)}), bf16[16,128,256]{2,1,0:T(8,128)(2,1)S(1)}, u32[]{:S(2)}, u32[]{:S(2)}) async-start(bf16[16,128,256]{2,1,0:T(8,128)(2,1)} %get-tuple-element.8), calls=%async_computation | async-start | bytes 2097152 | tf_op jit(solution)/shard_map/all_to_all | solution.py:198
  37.3 15.9 %all-to-all-start.1 = ((bf16[16,64,256]{2,1,0:T(8,128)(2,1)}), bf16[16,64,256]{2,1,0:T(8,128)(2,1)S(1)}, u32[]{:S(2)}, u32[]{:S(2)}) async-start(bf16[16,64,256]{2,1,0:T(8,128)(2,1)} %convolve.1), calls=%async_computation.1 | async-start | bytes 1048576 | tf_op jit(solution)/shard_map/all_to_all | solution.py:201
  53.2 0.8 copy-start.2
  61.7 34.2 %collective-permute-start = (bf16[8,192,256]{2,1,0:T(8,128)(2,1)}, bf16[8,192,256]{2,1,0:T(8,128)(2,1)S(1)}, u32[]{:S(2)}, u32[]{:S(2)}) collective-permute-start(bf16[8,192,256]{2,1,0:T(8,128)(2,1)} %project.6), channel_id=1, source_target_pairs={{0,4},{1,5},{2,6},{3,7},{4,0},{5,1},{6,2},{7,3},{8,12},{9,13},{10,... | collective-permute-start | bytes 2359304 | tf_op jit(solution)/shard_map/ppermute | solution.py:180
  68.3 27.7 %collective-permute-start.6 = (bf16[4,320,256]{2,1,0:T(8,128)(2,1)}, bf16[4,320,256]{2,1,0:T(8,128)(2,1)S(1)}, u32[]{:S(2)}, u32[]{:S(2)}) collective-permute-start(bf16[4,320,256]{2,1,0:T(8,128)(2,1)} %project.9), channel_id=1, source_target_pairs={{0,1},{1,2},{2,3},{3,0},{4,5},{5,6},{6,7},{7,4},{8,9},{9,10},{10,1... | collective-permute-start | bytes 1966088 | tf_op jit(solution)/shard_map/ppermute | solution.py:175
  77.5 27.7 %collective-permute-start.5 = (bf16[4,320,256]{2,1,0:T(8,128)(2,1)}, bf16[4,320,256]{2,1,0:T(8,128)(2,1)S(1)}, u32[]{:S(2)}, u32[]{:S(2)}) collective-permute-start(bf16[4,320,256]{2,1,0:T(8,128)(2,1)} %project.8), channel_id=1, source_target_pairs={{0,3},{1,0},{2,1},{3,2},{4,7},{5,4},{6,5},{7,6},{8,11},{9,8},{10,9... | collective-permute-start | bytes 1966088 | tf_op jit(solution)/shard_map/ppermute | solution.py:175
  87.2 8.6 %copy-start.4 = (bf16[8,192,256]{2,1,0:T(8,128)(2,1)S(1)}, bf16[8,192,256]{2,1,0:T(8,128)(2,1)}, u32[]{:S(2)}) copy-start(bf16[8,192,256]{2,1,0:T(8,128)(2,1)} %project.5) | copy-start | bytes 2359300
  95.8 15.1 %copy-start.3 = (bf16[8,320,256]{2,1,0:T(8,128)(2,1)S(1)}, bf16[8,320,256]{2,1,0:T(8,128)(2,1)}, u32[]{:S(2)}) copy-start(bf16[8,320,256]{2,1,0:T(8,128)(2,1)} %project.7) | copy-start | bytes 3932164
  95.9 9.1 %collective-permute-start.2 = (bf16[2,192,256]{2,1,0:T(8,128)(2,1)S(1)}, bf16[2,192,256]{2,1,0:T(8,128)(2,1)S(1)}, u32[]{:S(2)}, u32[]{:S(2)}) collective-permute-start(bf16[2,192,256]{2,1,0:T(8,128)(2,1)S(1)} %get-tuple-element.13), channel_id=1, source_target_pairs={{0,1},{1,2},{2,3},{3,0},{4,5},{5,6},{6,7},{7,4},{8,9},{9,10},{10,1... | collective-permute-start | bytes 589832 | tf_op jit(solution)/shard_map/ppermute | solution.py:175
  97.2 13.7 %collective-permute-start.7 = (bf16[2,320,256]{2,1,0:T(8,128)(2,1)S(1)}, bf16[2,320,256]{2,1,0:T(8,128)(2,1)S(1)}, u32[]{:S(2)}, u32[]{:S(2)}) collective-permute-start(bf16[2,320,256]{2,1,0:T(8,128)(2,1)S(1)} %add_convert_fusion.1), channel_id=1, source_target_pairs={{0,1},{1,2},{2,3},{3,0},{4,5},{5,6},{6,7},{7,4},{8,9},{9,10},{10,1... | collective-permute-start | bytes 983048 | tf_op jit(solution)/shard_map/ppermute | solution.py:175
  99.0 13.0 %collective-permute-start.1 = (bf16[2,192,256]{2,1,0:T(8,128)(2,1)S(1)}, bf16[2,192,256]{2,1,0:T(8,128)(2,1)S(1)}, u32[]{:S(2)}, u32[]{:S(2)}) collective-permute-start(bf16[2,192,256]{2,1,0:T(8,128)(2,1)S(1)} %get-tuple-element.14), channel_id=1, source_target_pairs={{0,3},{1,0},{2,1},{3,2},{4,7},{5,4},{6,5},{7,6},{8,11},{9,8},{10,9... | collective-permute-start | bytes 589832 | tf_op jit(solution)/shard_map/ppermute | solution.py:175
  105.1 6.9 %collective-permute-start.3 = (bf16[1,192,256]{2,1,0:T(8,128)(2,1)S(1)}, bf16[1,192,256]{2,1,0:T(8,128)(2,1)S(1)}, u32[]{:S(2)}, u32[]{:S(2)}) collective-permute-start(bf16[1,192,256]{2,1,0:T(8,128)(2,1)S(1)} %add_convert_fusion.7), channel_id=1, source_target_pairs={{0,1},{1,2},{2,3},{3,0},{4,5},{5,6},{6,7},{7,4},{8,9},{9,10},{10,1... | collective-permute-start | bytes 294920 | tf_op jit(solution)/shard_map/ppermute | solution.py:175
  111.1 7.5 %collective-permute-start.8 = (bf16[2,320,256]{2,1,0:T(8,128)(2,1)S(1)}, bf16[2,320,256]{2,1,0:T(8,128)(2,1)S(1)}, u32[]{:S(2)}, u32[]{:S(2)}) collective-permute-start(bf16[2,320,256]{2,1,0:T(8,128)(2,1)S(1)} %get-tuple-element.10), channel_id=1, source_target_pairs={{0,3},{1,0},{2,1},{3,2},{4,7},{5,4},{6,5},{7,6},{8,11},{9,8},{10,9... | collective-permute-start | bytes 983048 | tf_op jit(solution)/shard_map/ppermute | solution.py:175
  112.1 8.2 %collective-permute-start.4 = (bf16[1,192,256]{2,1,0:T(8,128)(2,1)S(1)}, bf16[1,192,256]{2,1,0:T(8,128)(2,1)S(1)}, u32[]{:S(2)}, u32[]{:S(2)}) collective-permute-start(bf16[1,192,256]{2,1,0:T(8,128)(2,1)S(1)} %get-tuple-element.12), channel_id=1, source_target_pairs={{0,3},{1,0},{2,1},{3,2},{4,7},{5,4},{6,5},{7,6},{8,11},{9,8},{10,9... | collective-permute-start | bytes 294920 | tf_op jit(solution)/shard_map/ppermute | solution.py:175
  118.8 7.2 %collective-permute-start.9 = (bf16[2,320,256]{2,1,0:T(8,128)(2,1)S(1)}, bf16[2,320,256]{2,1,0:T(8,128)(2,1)S(1)}, u32[]{:S(2)}, u32[]{:S(2)}) collective-permute-start(bf16[2,320,256]{2,1,0:T(8,128)(2,1)S(1)} %pad_maximum_fusion), channel_id=1, source_target_pairs={{0,4},{1,5},{2,6},{3,7},{4,0},{5,1},{6,2},{7,3},{8,12},{9,13},{10,... | collective-permute-start | bytes 983048 | tf_op jit(solution)/shard_map/ppermute | solution.py:180

commit v3 on v2

v3 whole, which is shorter than its diff:
```python
import functools

import numpy as np

import jax
import jax.numpy as jnp
from jax import lax
from jax.experimental import pallas as pl
from jax.experimental.pallas import tpu as pltpu
from jax.sharding import PartitionSpec as P

F32, BF16 = jnp.float32, jnp.bfloat16


def split_bf16(table):
    high = table.astype(BF16)
    low = (table - high.astype(np.float64)).astype(BF16)
    return high, low


def transform_table(n):
    freq = np.arange(n, dtype=np.float64) + 0.5
    angle = np.pi / n * np.outer(np.arange(n, dtype=np.float64), freq)
    forward = np.concatenate([np.cos(angle), -np.sin(angle)], axis=1)
    high, low = split_bf16(forward)
    inverse = [part.T.astype(np.float64) / n for part in (high, low)]
    return np.concatenate([high, low, np.concatenate(inverse, axis=1).astype(BF16)], axis=0)


def prepare_kernel(in_gate, signal, taps, packed, gate_buf, signal_buf, taps_buf, sems):
    parts, both, tokens = packed.shape
    half = both // 2
    steps, wide = gate_buf.shape[0], gate_buf.shape[2]
    copies = [
        [
            pltpu.make_async_copy(source.at[:, i * wide : (i + 1) * wide], buf.at[i], sems.at[i, j])
            for j, (source, buf) in enumerate(((in_gate, gate_buf), (signal, signal_buf), (taps, taps_buf)))
        ]
        for i in range(steps)
    ]
    for step in copies:
        for copy in step:
            copy.start()
    count = wide // half
    for i, step in enumerate(copies):
        for copy in step:
            copy.wait()
        gated = (gate_buf[i].astype(F32) * signal_buf[i].astype(F32)).astype(BF16)
        packed[i * count : (i + 1) * count, :half] = gated.T.reshape(count, half, tokens)
        packed[i * count : (i + 1) * count, half:] = taps_buf[i].T.reshape(count, half, tokens)


def prepare(in_gate, signal, taps, parts):
    tokens, channels = in_gate.shape
    steps = 4
    wide = channels // steps
    return pl.pallas_call(
        prepare_kernel,
        in_specs=[pl.BlockSpec(memory_space=pltpu.HBM)] * 3,
        out_specs=pl.BlockSpec(memory_space=pltpu.VMEM),
        out_shape=jax.ShapeDtypeStruct((parts, 2 * channels // parts, tokens), BF16),
        scratch_shapes=[pltpu.VMEM((steps, tokens, wide), BF16)] * 3 + [pltpu.SemaphoreType.DMA((steps, 3))],
        compiler_params=pltpu.CompilerParams(vmem_limit_bytes=60 * 2**20),
        name="prepare",
    )(in_gate, signal, taps)


def conv_kernel(
    packed, skip, table_far, gate_far, weight_far, out, gate_t, weight, table, gate, g_spec, p_spec, acc_high, acc_low, sems
):
    copies = [
        pltpu.make_async_copy(source, target, sems.at[i])
        for i, (source, target) in enumerate(((table_far, table), (gate_far, gate), (weight_far, weight)))
    ]
    for copy in copies:
        copy.start()
    copies[0].wait()
    copies[1].wait()
    gate_t[...] = gate[...].T
    blocks, both, n = packed.shape
    ch = both // 2
    lane = lax.broadcasted_iota(jnp.int32, (1, n), 1)
    sign = jnp.where(lane % 2 == 0, 1.0, -1.0).astype(F32)

    def transform(rows):
        return jnp.dot(rows, table[:n], preferred_element_type=F32) + jnp.dot(
            rows, table[n : 2 * n], preferred_element_type=F32
        )

    def inverse(spectra, part):
        return jnp.dot(spectra, table[2 * n :, part * n : (part + 1) * n], preferred_element_type=F32)

    group = 4
    tail = None
    for b in range(0, blocks, group):
        rows = packed[b : b + group]
        g_spec[b : b + group] = transform(rows[:, :ch].reshape(group * ch, n)).reshape(group, ch, 2 * n)
        h = transform(rows[:, ch:].reshape(group * ch, n)).reshape(group, ch, 2 * n)
        for j in range(group):
            if tail is None:
                p_spec[b + j] = h[j]
            else:
                p_spec[b + j, :, :n] = h[j, :, :n] - sign * tail[:, n:]
                p_spec[b + j, :, n:] = h[j, :, n:] + sign * tail[:, :n]
            tail = h[j]

    lanes, subs = 128, 16

    def products(step, carry):
        rows = pl.ds(pl.multiple_of(step * subs, subs), subs)
        for f in range(0, n, lanes):
            re, im = slice(f, f + lanes), slice(n + f, n + f + lanes)
            for i in range(blocks):
                acc_re = acc_im = None
                for a in range(i + 1):
                    gr, gi = g_spec[a, rows, re], g_spec[a, rows, im]
                    pr, pi = p_spec[i - a, rows, re], p_spec[i - a, rows, im]
                    t_re, t_im = gr * pr - gi * pi, gr * pi + gi * pr
                    acc_re = t_re if acc_re is None else acc_re + t_re
                    acc_im = t_im if acc_im is None else acc_im + t_im
                for value, cols in ((acc_re, re), (acc_im, im)):
                    high = value.astype(BF16)
                    acc_high[i, rows, cols] = high
                    acc_low[i, rows, cols] = (value - high.astype(F32)).astype(BF16)
        return carry

    lax.fori_loop(0, ch // subs, products, 0)

    for b in range(0, blocks, group):
        high = acc_high[b : b + group].reshape(group * ch, 2 * n)
        low = acc_low[b : b + group].reshape(group * ch, 2 * n)
        conv = (inverse(high, 0) + inverse(low, 0) + inverse(high, 1)).reshape(group, ch, n)
        gated = packed[b : b + group, :ch, :].astype(F32)
        out[b : b + group] = (conv + skip[...][None] * gated).astype(BF16)
    copies[2].wait()


def convolve(packed, skip, table, gate, weight):
    blocks, both, n = packed.shape
    ch = both // 2
    near, far = pl.BlockSpec(memory_space=pltpu.VMEM), pl.BlockSpec(memory_space=pltpu.HBM)
    return pl.pallas_call(
        conv_kernel,
        in_specs=[near, near, far, far, far],
        out_specs=[near] * 3,
        out_shape=[
            jax.ShapeDtypeStruct((blocks, ch, n), BF16),
            jax.ShapeDtypeStruct(gate.shape[::-1], BF16),
            jax.ShapeDtypeStruct(weight.shape, BF16),
        ],
        scratch_shapes=[
            pltpu.VMEM(table.shape, BF16),
            pltpu.VMEM(gate.shape, BF16),
            pltpu.VMEM((blocks, ch, 2 * n), F32),
            pltpu.VMEM((blocks, ch, 2 * n), F32),
            pltpu.VMEM((blocks, ch, 2 * n), BF16),
            pltpu.VMEM((blocks, ch, 2 * n), BF16),
            pltpu.SemaphoreType.DMA((3,)),
        ],
        compiler_params=pltpu.CompilerParams(vmem_limit_bytes=28 * 2**20),
        name="convolve",
    )(packed, skip, table, gate, weight)


def project_kernel(weight, mixed, out, *, pieces, chunk):
    me = lax.axis_index("chan")
    rows = out.shape[1]
    for i, (flip, step, offset) in enumerate(pieces):
        start = ((me // Z + flip) % 2 * Z + (me % Z + step) % Z) * chunk + offset
        block = weight[pl.ds(pl.multiple_of(start, 16), rows), :]
        out[i] = jnp.dot(block, mixed[...], preferred_element_type=F32).astype(BF16)


def project(weight, mixed, pieces, rows, chunk):
    channels, tokens = mixed.shape
    count = len(pieces)
    in_vmem = pl.BlockSpec(memory_space=pltpu.VMEM)
    return pl.pallas_call(
        functools.partial(project_kernel, pieces=pieces, chunk=chunk),
        in_specs=[in_vmem] * 2,
        out_specs=in_vmem,
        out_shape=jax.ShapeDtypeStruct((count, rows, tokens), BF16),
        compiler_params=pltpu.CompilerParams(vmem_limit_bytes=8 * 2**20),
        cost_estimate=pl.CostEstimate(
            flops=2 * count * rows * channels * tokens,
            bytes_accessed=2 * count * rows * tokens,
            transcendentals=0,
        ),
        name="project",
    )(weight, mixed)


Z = 4


def to_z(block, step):
    n = lax.axis_size("chan")
    return lax.ppermute(block, "chan", [(i, i // Z * Z + (i + step) % Z) for i in range(n)])


def to_other_x(block):
    n = lax.axis_size("chan")
    return lax.ppermute(block, "chan", [(i, (i + Z) % n) for i in range(n)])


def reduce_z(plus, minus, keep_plus, keep_minus, own_first, own_second):
    from_below, from_above = to_z(plus, 1), to_z(minus, -1)
    k = keep_plus.shape[0]
    up = to_z((keep_plus.astype(F32) + from_below[:k].astype(F32)).astype(BF16), 1)
    down = to_z((keep_minus.astype(F32) + from_above[:k].astype(F32)).astype(BF16), -1)
    first = own_first.astype(F32) + from_above[k:].astype(F32) + up.astype(F32)
    second = own_second.astype(F32) + from_below[k:].astype(F32) + down.astype(F32)
    return first, second


def shards(out_gate, in_gate, signal, filter_taps, skip_gain, out_proj):
    tokens, channels = out_gate.shape
    parts, chans = lax.axis_size("seq"), lax.axis_size("chan")
    per_part = channels // parts
    packed = prepare(in_gate, signal, filter_taps, parts)
    packed = lax.all_to_all(packed, "seq", 0, 0)
    skip = lax.dynamic_slice_in_dim(skip_gain, lax.axis_index("seq") * per_part, per_part, 0)
    table = jnp.asarray(transform_table(tokens))
    conv, out_gate_t, out_proj = convolve(packed, skip[:, None], table, out_gate, out_proj)
    conv = lax.all_to_all(conv, "seq", 0, 0).reshape(channels, tokens)

    mixed = (out_gate_t.astype(F32) * conv.astype(F32)).astype(BF16)
    chunk = out_proj.shape[0] // chans
    half_a = 192
    half_b = chunk // 2 - half_a
    order = [(2, 0), (1, 1), (2, 1), (3, 0), (1, 0), (3, 1), (0, 0), (0, 1)]
    rows_a = [[(flip, s, h * half_a) for s, h in order] for flip in (0, 1)]
    rows_b = [(flip, s, 2 * half_a + h * half_b) for s, h in order for flip in (0, 1)]

    from_x = to_other_x(project(out_proj, mixed, rows_a[1], half_a, chunk))
    plus_b = project(out_proj, mixed, rows_b[:4], half_b, chunk)
    minus_b = project(out_proj, mixed, rows_b[4:8], half_b, chunk)
    own_a = project(out_proj, mixed, rows_a[0], half_a, chunk)
    rest_b = project(out_proj, mixed, rows_b[8:], half_b, chunk)

    def summed_a(lo, hi):
        return own_a[lo:hi].astype(F32) + from_x[lo:hi].astype(F32)

    b_first, b_second = reduce_z(plus_b, minus_b, rest_b[:2], rest_b[2:4], rest_b[4:6], rest_b[6:8])
    other_b = to_other_x(jnp.stack([b_first[1], b_second[1]]).astype(BF16)).astype(F32)
    a_first, a_second = reduce_z(
        summed_a(0, 2).astype(BF16), summed_a(2, 4).astype(BF16),
        summed_a(4, 5), summed_a(5, 6), summed_a(6, 7), summed_a(7, 8),
    )
    rows = [a_first[0], a_second[0], b_first[0] + other_b[0], b_second[0] + other_b[1]]
    return jnp.concatenate([r.astype(BF16) for r in rows], axis=0).T


def solution(mesh):
    return jax.shard_map(
        shards,
        mesh=mesh,
        in_specs=(
            P("seq", "chan"),
            P("seq", "chan"),
            P("seq", "chan"),
            P("seq", "chan"),
            P("chan"),
            P(None, "chan"),
        ),
        out_specs=P("seq", "chan"),
        check_vma=False,
    )
```

time: 128 us -> 102 us (0.80)
  Pallas kernels: 46.6 us -> 13.8 us
  blocking collectives: 0 us -> 15 us
  local copies, waits for them, and re-layouts: 3.97 us -> 1.23 us
  waiting for transfers between devices: 51.1 us -> 48.8 us
  other arithmetic: 3.23 us -> 1.05 us
    pallas_call x7, Pallas kernels: 46.6 us -> 13.8 us  [the longest x1 5.9 us: convolve(): pl.pallas_call(conv_kernel, in_specs=[near, near, far, far, far], out_spe...]
    all_to_all x0 -> x1, blocking collectives: none -> 15 us  [shards(): conv = lax.all_to_all(conv, 'seq', 0, 0).reshape(channels, tokens)]
    all_to_all x1 -> x0, waiting for transfers between devices: 11.6 us -> none  [shards(): conv = lax.all_to_all(conv, 'seq', 0, 0).reshape(channels, tokens)]
    ppermute x2, waiting for transfers between devices: 5.63 us -> 16 us  [to_other_x(): return lax.ppermute(block, 'chan', [(i, (i + Z) % n) for i in range(n)])]
    all_to_all x1 -> x0, starting transfers between devices: 3.57 us -> none  [shards(): conv = lax.all_to_all(conv, 'seq', 0, 0).reshape(channels, tokens)]
    ppermute x8, starting transfers between devices: 9.12 us -> 12.2 us  [to_z(): lax.ppermute(block, 'chan', [(i, i // Z * Z + (i + step) % Z) for i in ra...]
    another operation x3 -> x0, local copies, waits for them, and re-layouts: 1.93 us -> none  [project(): jnp.stack(starts).astype(jnp.int32)]
  transfers between devices with their start and end apart: 12 -> 11, of which waited for: 6 -> 7; matrix products, arithmetic and copies ran while one was open for 4% -> 1% of each run, Pallas kernels for 21% -> 4%
where the time goes in v3:
time: 102 us; the launch traced here: 101 us
  waiting for transfers between devices  48.8 us (48%)
  starting transfers between devices  20.9 us (20%)
  blocking collectives  15 us (15%)
  Pallas kernels  13.8 us (14%)
  local copies, waits for them, and re-layouts  1.23 us (1%)
  other arithmetic  1.05 us (1%)
    all_to_all x1, waiting for transfers between devices, shards(): packed = lax.all_to_all(packed, 'seq', 0, 0)  17.8 us
    ppermute x2, waiting for transfers between devices, to_other_x(): return lax.ppermute(block, 'chan', [(i, (i + Z) % n) for i in range(n)])  16 us
    ppermute x8, waiting for transfers between devices, to_z(): lax.ppermute(block, 'chan', [(i, i // Z * Z + (i + step) % Z) for i in ra...  15 us
    all_to_all x1, blocking collectives, shards(): conv = lax.all_to_all(conv, 'seq', 0, 0).reshape(channels, tokens)  15 us
    ppermute x8, starting transfers between devices, to_z(): lax.ppermute(block, 'chan', [(i, i // Z * Z + (i + step) % Z) for i in ra...  12.2 us
    all_to_all x1, starting transfers between devices, shards(): packed = lax.all_to_all(packed, 'seq', 0, 0)  7.26 us
    pallas_call x1, Pallas kernels, convolve(): pl.pallas_call(conv_kernel, in_specs=[near, near, far, far, far], out_spe...  5.9 us
    pallas_call x5, Pallas kernels, project(): pl.pallas_call(functools.partial(project_kernel, pieces=pieces, chunk=chu...  5.18 us
  transfers between devices with their start and end apart: 11, of which 7 were waited for; matrix products, arithmetic and copies ran while one was open for 1% of the time, Pallas kernels for 4%

profile of v3, /device:TPU:0, one launch (start us, length us, event | category | flops | bytes accessed | tf_op | source)
XLA Modules:
  0.0 100.9 jit_solution(10200532438403169332)
XLA Ops:
  0.0 0.0 copy-start
  0.0 2.7 %prepare.1 = bf16[16,128,256]{2,1,0:T(8,128)(2,1)} custom-call(bf16[256,1024]{1,0:T(8,128)(2,1)} %in_gate.1, bf16[256,1024]{1,0:T(8,128)(2,1)} %signal.1, bf16[256,1024]{1,0:T(8,128)(2,1)} %taps.1), custom_call_target="tpu_custom_call" | custom-call | tf_op jit(solution)/shard_map/prepare/pallas_call | solution.py:57
  2.7 0.0 copy-start.1
  2.7 0.0 copy-start.2
  2.7 7.3 %all-to-all-start = ((bf16[16,128,256]{2,1,0:T(8,128)(2,1)}), bf16[16,128,256]{2,1,0:T(8,128)(2,1)S(1)}, u32[]{:S(2)}, u32[]{:S(2)}) async-start(bf16[16,128,256]{2,1,0:T(8,128)(2,1)} %prepare.1), calls=%async_computation | async-start | bytes 2097152 | tf_op jit(solution)/shard_map/all_to_all | solution.py:221
  10.0 0.0 copy-done
  10.0 0.1 dynamic-slice_bitcast_fusion
  10.1 0.1 copy.8.skip
  10.2 17.8 %all-to-all-done.packed = bf16[16,128,256]{2,1,0:T(8,128)(2,1)S(1)} async-done(((bf16[16,128,256]{2,1,0:T(8,128)(2,1)}), bf16[16,128,256]{2,1,0:T(8,128)(2,1)S(1)}, u32[]{:S(2)}, u32[]{:S(2)}) %all-to-all-start) | async-done | bytes 1048608 | tf_op jit(solution)/shard_map/all_to_all | solution.py:221
  28.0 0.0 copy-done.1
  28.0 0.0 copy-done.2
  28.0 5.9 %convolve.1 = (bf16[16,64,256]{2,1,0:T(8,128)(2,1)S(1)}, bf16[1024,256]{1,0:T(8,128)(2,1)S(1)}, bf16[8192,1024]{1,0:T(8,128)(2,1)S(1)}) custom-call(bf16[16,128,256]{2,1,0:T(8,128)(2,1)S(1)} %all-to-all-done.packed, f32[64,1]{1,0:T(8,128)S(1)} %copy.8.skip, bf16[1024,512]{1,0:T(8,128)(2,1)S(1)} %copy-done.1, bf16[256,1024]{1,0:T(8,128)(2,1)S(1)} %copy-done.2, ...), custom_call_target="tpu_custom_call" | custom-call | tf_op jit(solution)/shard_map/convolve/pallas_call | solution.py:142
  33.9 15.0 %all_to_all.10 = bf16[16,64,256]{2,1,0:T(8,128)(2,1)S(1)} all-to-all(bf16[16,64,256]{2,1,0:T(8,128)(2,1)S(1)} %get-tuple-element.10), channel_id=1, replica_groups=mesh['seq'=16,'chan'=8] {'seq'}, dimensions={0} | all-to-all | bytes 1048576 | tf_op jit(solution)/shard_map/all_to_all | solution.py:225
  48.9 0.2 fusion.mixed
  49.1 1.0 project.6
  50.1 0.7 collective-permute-start
  50.8 0.8 project.9
  51.6 2.0 %collective-permute-start.6 = (bf16[4,320,256]{2,1,0:T(8,128)(2,1)S(1)}, bf16[4,320,256]{2,1,0:T(8,128)(2,1)S(1)}, u32[]{:S(2)}, u32[]{:S(2)}) collective-permute-start(bf16[4,320,256]{2,1,0:T(8,128)(2,1)S(1)} %project.9), channel_id=1, source_target_pairs={{0,1},{1,2},{2,3},{3,0},{4,5},{5,6},{6,7},{7,4},{8,9},{9,10},{10,1... | collective-permute-start | bytes 1966088 | tf_op jit(solution)/shard_map/ppermute | solution.py:198
  53.6 0.8 project.8
  54.5 2.2 %collective-permute-start.5 = (bf16[4,320,256]{2,1,0:T(8,128)(2,1)S(1)}, bf16[4,320,256]{2,1,0:T(8,128)(2,1)S(1)}, u32[]{:S(2)}, u32[]{:S(2)}) collective-permute-start(bf16[4,320,256]{2,1,0:T(8,128)(2,1)S(1)} %project.8), channel_id=1, source_target_pairs={{0,3},{1,0},{2,1},{3,2},{4,7},{5,4},{6,5},{7,6},{8,11},{9,8},{10,9... | collective-permute-start | bytes 1966088 | tf_op jit(solution)/shard_map/ppermute | solution.py:198
  56.7 1.0 project.5
  57.7 1.5 %project.7 = bf16[8,320,256]{2,1,0:T(8,128)(2,1)S(1)} custom-call(bf16[8192,1024]{1,0:T(8,128)(2,1)S(1)} %get-tuple-element.8.weight, bf16[1024,256]{1,0:T(8,128)(2,1)S(1)} %fusion.mixed), custom_call_target="tpu_custom_call" | custom-call | flops 1342177280 | bytes 1310720 | tf_op jit(solution)/shard_map/project/pallas_call | solution.py:178
  59.2 9.7 %collective-permute-done = bf16[8,192,256]{2,1,0:T(8,128)(2,1)S(1)} collective-permute-done((bf16[8,192,256]{2,1,0:T(8,128)(2,1)S(1)}, bf16[8,192,256]{2,1,0:T(8,128)(2,1)S(1)}, u32[]{:S(2)}, u32[]{:S(2)}) %collective-permute-start) | collective-permute-done | bytes 786464 | tf_op jit(solution)/shard_map/ppermute | solution.py:203
  68.9 0.1 add_convert_fusion.2
  69.0 2.0 %collective-permute-start.2 = (bf16[2,192,256]{2,1,0:T(8,128)(2,1)S(1)}, bf16[2,192,256]{2,1,0:T(8,128)(2,1)S(1)}, u32[]{:S(2)}, u32[]{:S(2)}) collective-permute-start(bf16[2,192,256]{2,1,0:T(8,128)(2,1)S(1)} %get-tuple-element.15), channel_id=1, source_target_pairs={{0,1},{1,2},{2,3},{3,0},{4,5},{5,6},{6,7},{7,4},{8,9},{9,10},{10,1... | collective-permute-start | bytes 589832 | tf_op jit(solution)/shard_map/ppermute | solution.py:198
  71.0 0.0 collective-permute-done.6
  71.0 0.1 add_convert_fusion.1
  71.1 2.0 %collective-permute-start.7 = (bf16[2,320,256]{2,1,0:T(8,128)(2,1)S(1)}, bf16[2,320,256]{2,1,0:T(8,128)(2,1)S(1)}, u32[]{:S(2)}, u32[]{:S(2)}) collective-permute-start(bf16[2,320,256]{2,1,0:T(8,128)(2,1)S(1)} %add_convert_fusion.1), channel_id=1, source_target_pairs={{0,1},{1,2},{2,3},{3,0},{4,5},{5,6},{6,7},{7,4},{8,9},{9,10},{10,1... | collective-permute-start | bytes 983048 | tf_op jit(solution)/shard_map/ppermute | solution.py:198
  73.1 1.3 %collective-permute-start.1 = (bf16[2,192,256]{2,1,0:T(8,128)(2,1)S(1)}, bf16[2,192,256]{2,1,0:T(8,128)(2,1)S(1)}, u32[]{:S(2)}, u32[]{:S(2)}) collective-permute-start(bf16[2,192,256]{2,1,0:T(8,128)(2,1)S(1)} %get-tuple-element.16), channel_id=1, source_target_pairs={{0,3},{1,0},{2,1},{3,2},{4,7},{5,4},{6,5},{7,6},{8,11},{9,8},{10,9... | collective-permute-start | bytes 589832 | tf_op jit(solution)/shard_map/ppermute | solution.py:198
  74.4 4.5 %collective-permute-done.2 = bf16[2,192,256]{2,1,0:T(8,128)(2,1)S(1)} collective-permute-done((bf16[2,192,256]{2,1,0:T(8,128)(2,1)S(1)}, bf16[2,192,256]{2,1,0:T(8,128)(2,1)S(1)}, u32[]{:S(2)}, u32[]{:S(2)}) %collective-permute-start.2) | collective-permute-done | bytes 196640 | tf_op jit(solution)/shard_map/ppermute | solution.py:198
  79.0 0.1 collective-permute-start.3
  79.1 0.0 collective-permute-done.5
  79.1 5.6 %collective-permute-done.7 = bf16[2,320,256]{2,1,0:T(8,128)(2,1)S(1)} collective-permute-done((bf16[2,320,256]{2,1,0:T(8,128)(2,1)S(1)}, bf16[2,320,256]{2,1,0:T(8,128)(2,1)S(1)}, u32[]{:S(2)}, u32[]{:S(2)}) %collective-permute-start.7) | collective-permute-done | bytes 327712 | tf_op jit(solution)/shard_map/ppermute | solution.py:198
  84.7 0.2 convert_add_fusion.1
  84.9 1.8 %collective-permute-start.8 = (bf16[2,320,256]{2,1,0:T(8,128)(2,1)S(1)}, bf16[2,320,256]{2,1,0:T(8,128)(2,1)S(1)}, u32[]{:S(2)}, u32[]{:S(2)}) collective-permute-start(bf16[2,320,256]{2,1,0:T(8,128)(2,1)S(1)} %get-tuple-element.12), channel_id=1, source_target_pairs={{0,3},{1,0},{2,1},{3,2},{4,7},{5,4},{6,5},{7,6},{8,11},{9,8},{10,9... | collective-permute-start | bytes 983048 | tf_op jit(solution)/shard_map/ppermute | solution.py:198
  86.7 0.0 collective-permute-done.1
  86.8 0.0 collective-permute-done.3
  86.8 0.1 fusion.5
  86.9 0.8 collective-permute-start.4
  87.7 4.7 %collective-permute-done.8 = bf16[2,320,256]{2,1,0:T(8,128)(2,1)S(1)} collective-permute-done((bf16[2,320,256]{2,1,0:T(8,128)(2,1)S(1)}, bf16[2,320,256]{2,1,0:T(8,128)(2,1)S(1)}, u32[]{:S(2)}, u32[]{:S(2)}) %collective-permute-start.8) | collective-permute-done | bytes 327712 | tf_op jit(solution)/shard_map/ppermute | solution.py:198
  92.4 0.1 convert_add_fusion
  92.6 0.7 collective-permute-start.9
  93.3 0.1 collective-permute-done.4
  93.4 0.1 fusion.6
  93.5 6.2 %collective-permute-done.9 = bf16[2,320,256]{2,1,0:T(8,128)(2,1)S(1)} collective-permute-done((bf16[2,320,256]{2,1,0:T(8,128)(2,1)S(1)}, bf16[2,320,256]{2,1,0:T(8,128)(2,1)S(1)}, u32[]{:S(2)}, u32[]{:S(2)}) %collective-permute-start.9) | collective-permute-done | bytes 327712 | tf_op jit(solution)/shard_map/ppermute | solution.py:203
  99.8 0.1 fusion.3
  99.9 1.0 copy.9
  (6 shorter events, 0.2 us)
Async XLA Ops:
  0.0 10.0 %copy-start = (f32[1024]{0:T(1024)S(1)}, f32[1024]{0:T(1024)}, u32[]{:S(2)}) copy-start(f32[1024]{0:T(1024)} %param.11) | copy-start | bytes 12292
  2.7 25.3 %copy-start.1 = (bf16[1024,512]{1,0:T(8,128)(2,1)S(1)}, bf16[1024,512]{1,0:T(8,128)(2,1)}, u32[]{:S(2)}) copy-start(bf16[1024,512]{1,0:T(8,128)(2,1)} %constant.14.clone.table_far) | copy-start | bytes 3145732
  2.7 25.3 %copy-start.2 = (bf16[256,1024]{1,0:T(8,128)(2,1)S(1)}, bf16[256,1024]{1,0:T(8,128)(2,1)}, u32[]{:S(2)}) copy-start(bf16[256,1024]{1,0:T(8,128)(2,1)} %gate_far.1) | copy-start | bytes 1572868
  2.7 25.3 %all-to-all-start = ((bf16[16,128,256]{2,1,0:T(8,128)(2,1)}), bf16[16,128,256]{2,1,0:T(8,128)(2,1)S(1)}, u32[]{:S(2)}, u32[]{:S(2)}) async-start(bf16[16,128,256]{2,1,0:T(8,128)(2,1)} %prepare.1), calls=%async_computation | async-start | bytes 2097152 | tf_op jit(solution)/shard_map/all_to_all | solution.py:221
  50.1 18.9 %collective-permute-start = (bf16[8,192,256]{2,1,0:T(8,128)(2,1)S(1)}, bf16[8,192,256]{2,1,0:T(8,128)(2,1)S(1)}, u32[]{:S(2)}, u32[]{:S(2)}) collective-permute-start(bf16[8,192,256]{2,1,0:T(8,128)(2,1)S(1)} %project.6), channel_id=1, source_target_pairs={{0,4},{1,5},{2,6},{3,7},{4,0},{5,1},{6,2},{7,3},{8,12},{9,13},{10,... | collective-permute-start | bytes 2359304 | tf_op jit(solution)/shard_map/ppermute | solution.py:203
  51.6 19.4 %collective-permute-start.6 = (bf16[4,320,256]{2,1,0:T(8,128)(2,1)S(1)}, bf16[4,320,256]{2,1,0:T(8,128)(2,1)S(1)}, u32[]{:S(2)}, u32[]{:S(2)}) collective-permute-start(bf16[4,320,256]{2,1,0:T(8,128)(2,1)S(1)} %project.9), channel_id=1, source_target_pairs={{0,1},{1,2},{2,3},{3,0},{4,5},{5,6},{6,7},{7,4},{8,9},{9,10},{10,1... | collective-permute-start | bytes 1966088 | tf_op jit(solution)/shard_map/ppermute | solution.py:198
  54.5 24.6 %collective-permute-start.5 = (bf16[4,320,256]{2,1,0:T(8,128)(2,1)S(1)}, bf16[4,320,256]{2,1,0:T(8,128)(2,1)S(1)}, u32[]{:S(2)}, u32[]{:S(2)}) collective-permute-start(bf16[4,320,256]{2,1,0:T(8,128)(2,1)S(1)} %project.8), channel_id=1, source_target_pairs={{0,3},{1,0},{2,1},{3,2},{4,7},{5,4},{6,5},{7,6},{8,11},{9,8},{10,9... | collective-permute-start | bytes 1966088 | tf_op jit(solution)/shard_map/ppermute | solution.py:198
  69.0 9.9 %collective-permute-start.2 = (bf16[2,192,256]{2,1,0:T(8,128)(2,1)S(1)}, bf16[2,192,256]{2,1,0:T(8,128)(2,1)S(1)}, u32[]{:S(2)}, u32[]{:S(2)}) collective-permute-start(bf16[2,192,256]{2,1,0:T(8,128)(2,1)S(1)} %get-tuple-element.15), channel_id=1, source_target_pairs={{0,1},{1,2},{2,3},{3,0},{4,5},{5,6},{6,7},{7,4},{8,9},{9,10},{10,1... | collective-permute-start | bytes 589832 | tf_op jit(solution)/shard_map/ppermute | solution.py:198
  71.1 13.6 %collective-permute-start.7 = (bf16[2,320,256]{2,1,0:T(8,128)(2,1)S(1)}, bf16[2,320,256]{2,1,0:T(8,128)(2,1)S(1)}, u32[]{:S(2)}, u32[]{:S(2)}) collective-permute-start(bf16[2,320,256]{2,1,0:T(8,128)(2,1)S(1)} %add_convert_fusion.1), channel_id=1, source_target_pairs={{0,1},{1,2},{2,3},{3,0},{4,5},{5,6},{6,7},{7,4},{8,9},{9,10},{10,1... | collective-permute-start | bytes 983048 | tf_op jit(solution)/shard_map/ppermute | solution.py:198
  73.1 13.6 %collective-permute-start.1 = (bf16[2,192,256]{2,1,0:T(8,128)(2,1)S(1)}, bf16[2,192,256]{2,1,0:T(8,128)(2,1)S(1)}, u32[]{:S(2)}, u32[]{:S(2)}) collective-permute-start(bf16[2,192,256]{2,1,0:T(8,128)(2,1)S(1)} %get-tuple-element.16), channel_id=1, source_target_pairs={{0,3},{1,0},{2,1},{3,2},{4,7},{5,4},{6,5},{7,6},{8,11},{9,8},{10,9... | collective-permute-start | bytes 589832 | tf_op jit(solution)/shard_map/ppermute | solution.py:198
  79.0 7.7 %collective-permute-start.3 = (bf16[1,192,256]{2,1,0:T(8,128)(2,1)S(1)}, bf16[1,192,256]{2,1,0:T(8,128)(2,1)S(1)}, u32[]{:S(2)}, u32[]{:S(2)}) collective-permute-start(bf16[1,192,256]{2,1,0:T(8,128)(2,1)S(1)} %add_convert_fusion.7), channel_id=1, source_target_pairs={{0,1},{1,2},{2,3},{3,0},{4,5},{5,6},{6,7},{7,4},{8,9},{9,10},{10,1... | collective-permute-start | bytes 294920 | tf_op jit(solution)/shard_map/ppermute | solution.py:198
  84.9 7.5 %collective-permute-start.8 = (bf16[2,320,256]{2,1,0:T(8,128)(2,1)S(1)}, bf16[2,320,256]{2,1,0:T(8,128)(2,1)S(1)}, u32[]{:S(2)}, u32[]{:S(2)}) collective-permute-start(bf16[2,320,256]{2,1,0:T(8,128)(2,1)S(1)} %get-tuple-element.12), channel_id=1, source_target_pairs={{0,3},{1,0},{2,1},{3,2},{4,7},{5,4},{6,5},{7,6},{8,11},{9,8},{10,9... | collective-permute-start | bytes 983048 | tf_op jit(solution)/shard_map/ppermute | solution.py:198
  86.9 6.6 %collective-permute-start.4 = (bf16[1,192,256]{2,1,0:T(8,128)(2,1)S(1)}, bf16[1,192,256]{2,1,0:T(8,128)(2,1)S(1)}, u32[]{:S(2)}, u32[]{:S(2)}) collective-permute-start(bf16[1,192,256]{2,1,0:T(8,128)(2,1)S(1)} %get-tuple-element.14), channel_id=1, source_target_pairs={{0,3},{1,0},{2,1},{3,2},{4,7},{5,4},{6,5},{7,6},{8,11},{9,8},{10,9... | collective-permute-start | bytes 294920 | tf_op jit(solution)/shard_map/ppermute | solution.py:198
  92.6 7.2 %collective-permute-start.9 = (bf16[2,320,256]{2,1,0:T(8,128)(2,1)S(1)}, bf16[2,320,256]{2,1,0:T(8,128)(2,1)S(1)}, u32[]{:S(2)}, u32[]{:S(2)}) collective-permute-start(bf16[2,320,256]{2,1,0:T(8,128)(2,1)S(1)} %pad_maximum_fusion), channel_id=1, source_target_pairs={{0,4},{1,5},{2,6},{3,7},{4,0},{5,1},{6,2},{7,3},{8,12},{9,13},{10,... | collective-permute-start | bytes 983048 | tf_op jit(solution)/shard_map/ppermute | solution.py:203

commit v4 on v3

--- a/solution.py
+++ b/solution.py
@@ -1,5 +1,3 @@
-import functools
-
 import numpy as np
 
 import jax
@@ -66,7 +64,7 @@
 
 
 def conv_kernel(
-    packed, skip, table_far, gate_far, weight_far, out, gate_t, weight, table, gate, g_spec, p_spec, acc_high, acc_low, sems
+    packed, skip, gate_other, table_far, gate_far, weight_far, out, gate_t, weight, table, gate, g_spec, p_spec, acc_high, acc_low, sems
 ):
     copies = [
         pltpu.make_async_copy(source, target, sems.at[i])
@@ -76,8 +74,9 @@
         copy.start()
     copies[0].wait()
     copies[1].wait()
-    gate_t[...] = gate[...].T
     blocks, both, n = packed.shape
+    gate_t[:, :n] = gate[...].T
+    gate_t[:, n:] = gate_other[...].T
     ch = both // 2
     lane = lax.broadcasted_iota(jnp.int32, (1, n), 1)
     sign = jnp.where(lane % 2 == 0, 1.0, -1.0).astype(F32)
@@ -131,21 +130,24 @@
         low = acc_low[b : b + group].reshape(group * ch, 2 * n)
         conv = (inverse(high, 0) + inverse(low, 0) + inverse(high, 1)).reshape(group, ch, n)
         gated = packed[b : b + group, :ch, :].astype(F32)
-        out[b : b + group] = (conv + skip[...][None] * gated).astype(BF16)
+        rows = (conv + skip[...][None] * gated).astype(BF16)
+        out[b : b + group, :, :n] = rows
+        other = (b + blocks // 2) % blocks
+        out[other : other + group, :, n:] = rows[:, :, : n // 2]
     copies[2].wait()
 
 
-def convolve(packed, skip, table, gate, weight):
+def convolve(packed, skip, table, gate, gate_other, weight):
     blocks, both, n = packed.shape
     ch = both // 2
     near, far = pl.BlockSpec(memory_space=pltpu.VMEM), pl.BlockSpec(memory_space=pltpu.HBM)
     return pl.pallas_call(
         conv_kernel,
-        in_specs=[near, near, far, far, far],
+        in_specs=[near, near, near, far, far, far],
         out_specs=[near] * 3,
         out_shape=[
-            jax.ShapeDtypeStruct((blocks, ch, n), BF16),
-            jax.ShapeDtypeStruct(gate.shape[::-1], BF16),
+            jax.ShapeDtypeStruct((blocks, ch, n + n // 2), BF16),
+            jax.ShapeDtypeStruct((gate.shape[1], n + n // 2), BF16),
             jax.ShapeDtypeStruct(weight.shape, BF16),
         ],
         scratch_shapes=[
@@ -159,38 +161,43 @@
         ],
         compiler_params=pltpu.CompilerParams(vmem_limit_bytes=28 * 2**20),
         name="convolve",
-    )(packed, skip, table, gate, weight)
-
-
-def project_kernel(weight, mixed, out, *, pieces, chunk):
-    me = lax.axis_index("chan")
-    rows = out.shape[1]
-    for i, (flip, step, offset) in enumerate(pieces):
-        start = ((me // Z + flip) % 2 * Z + (me % Z + step) % Z) * chunk + offset
-        block = weight[pl.ds(pl.multiple_of(start, 16), rows), :]
-        out[i] = jnp.dot(block, mixed[...], preferred_element_type=F32).astype(BF16)
-
-
-def project(weight, mixed, pieces, rows, chunk):
-    channels, tokens = mixed.shape
-    count = len(pieces)
+    )(packed, skip, gate_other, table, gate, weight)
+
+
+def on_chip(body, shapes, *args, flops=0):
     in_vmem = pl.BlockSpec(memory_space=pltpu.VMEM)
     return pl.pallas_call(
-        functools.partial(project_kernel, pieces=pieces, chunk=chunk),
-        in_specs=[in_vmem] * 2,
-        out_specs=in_vmem,
-        out_shape=jax.ShapeDtypeStruct((count, rows, tokens), BF16),
+        body,
+        in_specs=[in_vmem] * len(args),
+        out_specs=[in_vmem] * len(shapes),
+        out_shape=[jax.ShapeDtypeStruct(shape, BF16) for shape in shapes],
         compiler_params=pltpu.CompilerParams(vmem_limit_bytes=8 * 2**20),
-        cost_estimate=pl.CostEstimate(
-            flops=2 * count * rows * channels * tokens,
-            bytes_accessed=2 * count * rows * tokens,
-            transcendentals=0,
-        ),
-        name="project",
-    )(weight, mixed)
+        cost_estimate=pl.CostEstimate(flops=flops, bytes_accessed=1, transcendentals=0),
+    )(*args)
 
 
 Z = 4
+
+
+def project(weight, mixed, pieces, rows, chunk, split=False):
+    channels, wide = mixed.shape
+    tokens = wide // 3 * 2
+    count = len(pieces)
+
+    def body(weight, mixed, *outs):
+        me = lax.axis_index("chan")
+        for i, (flip, step, offset) in enumerate(pieces):
+            start = ((me // Z + flip) % 2 * Z + (me % Z + step) % Z) * chunk + offset
+            block = weight[pl.ds(pl.multiple_of(start, 16), rows), :]
+            columns = mixed[:, wide - tokens :] if flip else mixed[:, :tokens]
+            share = jnp.dot(block, columns, preferred_element_type=F32).astype(BF16)
+            each = tokens // len(outs)
+            for j, out in enumerate(outs):
+                out[i] = share[:, j * each : (j + 1) * each]
+
+    shapes = [(count, rows, tokens // 2)] * 2 if split else [(count, rows, tokens)]
+    results = on_chip(body, shapes, weight, mixed, flops=2 * count * rows * channels * tokens)
+    return results if split else results[0]
 
 
 def to_z(block, step):
@@ -198,57 +205,118 @@
     return lax.ppermute(block, "chan", [(i, i // Z * Z + (i + step) % Z) for i in range(n)])
 
 
-def to_other_x(block):
+def to_near_x(block):
     n = lax.axis_size("chan")
     return lax.ppermute(block, "chan", [(i, (i + Z) % n) for i in range(n)])
 
 
-def reduce_z(plus, minus, keep_plus, keep_minus, own_first, own_second):
-    from_below, from_above = to_z(plus, 1), to_z(minus, -1)
-    k = keep_plus.shape[0]
-    up = to_z((keep_plus.astype(F32) + from_below[:k].astype(F32)).astype(BF16), 1)
-    down = to_z((keep_minus.astype(F32) + from_above[:k].astype(F32)).astype(BF16), -1)
-    first = own_first.astype(F32) + from_above[k:].astype(F32) + up.astype(F32)
-    second = own_second.astype(F32) + from_below[k:].astype(F32) + down.astype(F32)
-    return first, second
+def to_far_x(block):
+    n, m = lax.axis_size("chan"), lax.axis_size("seq")
+    route = [(s * n + c, (s + m // 2) % m * n + (c + Z) % n) for s in range(m) for c in range(n)]
+    return lax.ppermute(block, ("seq", "chan"), route)
+
+
+def wide_sum(*terms):
+    total = terms[0].astype(F32)
+    for term in terms[1:]:
+        total = total + term.astype(F32)
+    return total
+
+
+def beside(far, near):
+    return jnp.concatenate([far.astype(F32), near.astype(F32)], axis=-1)
 
 
 def shards(out_gate, in_gate, signal, filter_taps, skip_gain, out_proj):
     tokens, channels = out_gate.shape
     parts, chans = lax.axis_size("seq"), lax.axis_size("chan")
     per_part = channels // parts
+    gate_other = lax.ppermute(out_gate[: tokens // 2], "seq", [(i, (i + parts // 2) % parts) for i in range(parts)])
     packed = prepare(in_gate, signal, filter_taps, parts)
     packed = lax.all_to_all(packed, "seq", 0, 0)
     skip = lax.dynamic_slice_in_dim(skip_gain, lax.axis_index("seq") * per_part, per_part, 0)
     table = jnp.asarray(transform_table(tokens))
-    conv, out_gate_t, out_proj = convolve(packed, skip[:, None], table, out_gate, out_proj)
-    conv = lax.all_to_all(conv, "seq", 0, 0).reshape(channels, tokens)
-
+    conv, out_gate_t, out_proj = convolve(packed, skip[:, None], table, out_gate, gate_other, out_proj)
+    conv = lax.all_to_all(conv, "seq", 0, 0).reshape(channels, -1)
     mixed = (out_gate_t.astype(F32) * conv.astype(F32)).astype(BF16)
+
     chunk = out_proj.shape[0] // chans
-    half_a = 192
+    half_a = 320
     half_b = chunk // 2 - half_a
     order = [(2, 0), (1, 1), (2, 1), (3, 0), (1, 0), (3, 1), (0, 0), (0, 1)]
     rows_a = [[(flip, s, h * half_a) for s, h in order] for flip in (0, 1)]
     rows_b = [(flip, s, 2 * half_a + h * half_b) for s, h in order for flip in (0, 1)]
-
-    from_x = to_other_x(project(out_proj, mixed, rows_a[1], half_a, chunk))
+    half = tokens // 2
+
+    near, far = project(out_proj, mixed, rows_a[1][:4], half_a, chunk, split=True)
+    near_early, far_early = to_near_x(near), to_far_x(far)
     plus_b = project(out_proj, mixed, rows_b[:4], half_b, chunk)
+    below_b = to_z(plus_b, 1)
     minus_b = project(out_proj, mixed, rows_b[4:8], half_b, chunk)
+    above_b = to_z(minus_b, -1)
+    near, far = project(out_proj, mixed, rows_a[1][4:], half_a, chunk, split=True)
+    near_late, far_late = to_near_x(near), to_far_x(far)
     own_a = project(out_proj, mixed, rows_a[0], half_a, chunk)
     rest_b = project(out_proj, mixed, rows_b[8:], half_b, chunk)
 
-    def summed_a(lo, hi):
-        return own_a[lo:hi].astype(F32) + from_x[lo:hi].astype(F32)
-
-    b_first, b_second = reduce_z(plus_b, minus_b, rest_b[:2], rest_b[2:4], rest_b[4:6], rest_b[6:8])
-    other_b = to_other_x(jnp.stack([b_first[1], b_second[1]]).astype(BF16)).astype(F32)
-    a_first, a_second = reduce_z(
-        summed_a(0, 2).astype(BF16), summed_a(2, 4).astype(BF16),
-        summed_a(4, 5), summed_a(5, 6), summed_a(6, 7), summed_a(7, 8),
+    def first_a(own, near, far, plus, minus):
+        total = wide_sum(own[:4], beside(far[...], near[...])).astype(BF16)
+        plus[...] = total[:2]
+        minus[...] = total[2:]
+
+    plus_a, minus_a = on_chip(first_a, [(2, half_a, tokens)] * 2, own_a, near_early, far_early)
+    below_a, above_a = to_z(plus_a, 1), to_z(minus_a, -1)
+
+    def second_b(place):
+        def body(rest, arrived, out):
+            out[...] = wide_sum(rest[place : place + 2], arrived[:2]).astype(BF16)
+
+        return body
+
+    (up_b,) = on_chip(second_b(0), [(2, half_b, tokens)], rest_b, below_b)
+    up_b = to_z(up_b, 1)
+    (down_b,) = on_chip(second_b(2), [(2, half_b, tokens)], rest_b, above_b)
+    down_b = to_z(down_b, -1)
+
+    def second_a(place):
+        def body(own, near, far, arrived, out):
+            x_sum = beside(far[place : place + 1], near[place : place + 1])
+            out[...] = wide_sum(own[4 + place : 5 + place], x_sum, arrived[:1]).astype(BF16)
+
+        return body
+
+    (up_a,) = on_chip(second_a(0), [(1, half_a, tokens)], own_a, near_late, far_late, below_a)
+    up_a = to_z(up_a, 1)
+    (down_a,) = on_chip(second_a(1), [(1, half_a, tokens)], own_a, near_late, far_late, above_a)
+    down_a = to_z(down_a, -1)
+
+    def reduced_b(flip, rest, below, above, up, down):
+        first = wide_sum(rest[4 + flip], above[2 + flip], up[flip])
+        second = wide_sum(rest[6 + flip], below[2 + flip], down[flip])
+        return jnp.concatenate([first, second], axis=0)
+
+    def third_b(rest, below, above, up, down, near, far):
+        total = reduced_b(1, rest, below, above, up, down).astype(BF16)
+        near[...] = total[:, :half]
+        far[...] = total[:, half:]
+
+    near_b, far_b = on_chip(third_b, [(2 * half_b, half)] * 2, rest_b, below_b, above_b, up_b, down_b)
+    near_b, far_b = to_near_x(near_b), to_far_x(far_b)
+
+    def last(own, near, far, below, above, up, down, rest, b_below, b_above, b_up, b_down, b_near, b_far, out, all_rows):
+        first = wide_sum(own[6], beside(far[2], near[2]), above[1], up[0])
+        second = wide_sum(own[7], beside(far[3], near[3]), below[1], down[0])
+        all_rows[:half_a] = first.astype(BF16)
+        all_rows[half_a : 2 * half_a] = second.astype(BF16)
+        b_rows = reduced_b(0, rest, b_below, b_above, b_up, b_down) + beside(b_far[...], b_near[...])
+        all_rows[2 * half_a :] = b_rows.astype(BF16)
+        out[...] = all_rows[...].T
+
+    out, _ = on_chip(
+        last, [(tokens, chunk), (chunk, tokens)], own_a, near_late, far_late, below_a, above_a, up_a, down_a,
+        rest_b, below_b, above_b, up_b, down_b, near_b, far_b,
     )
-    rows = [a_first[0], a_second[0], b_first[0] + other_b[0], b_second[0] + other_b[1]]
-    return jnp.concatenate([r.astype(BF16) for r in rows], axis=0).T
+    return out
 
 
 def solution(mesh):

time: 102 us -> 94.7 us (0.928)
  waiting for transfers between devices: 48.8 us -> 28.1 us
  starting transfers between devices: 20.9 us -> 30.5 us
  blocking collectives: 15 us -> 19.4 us
  Pallas kernels: 13.8 us -> 15.6 us
  local copies, waits for them, and re-layouts: 1.23 us -> 0.21 us
    all_to_all x1, waiting for transfers between devices: 17.8 us -> 0.01 us  [shards(): packed = lax.all_to_all(packed, 'seq', 0, 0)]
    ppermute x8, waiting for transfers between devices: 15 us -> 3.75 us  [to_z(): lax.ppermute(block, 'chan', [(i, i // Z * Z + (i + step) % Z) for i in ra...]
    ppermute x2 -> x7, waiting for transfers between devices: 16 us -> 24.4 us  [the longest x1 17.8 us: shards(): lax.ppermute(out_gate[:tokens // 2], 'seq', [(i, (i + parts // 2) % parts...]
    ppermute x2 -> x7, starting transfers between devices: 1.44 us -> 8.97 us  [the longest x3 3.52 us: to_far_x(): return lax.ppermute(block, ('seq', 'chan'), route)]
    all_to_all x1, blocking collectives: 15 us -> 19.4 us  [shards(): conv = lax.all_to_all(conv, 'seq', 0, 0).reshape(channels, -1)]
    ppermute x8, starting transfers between devices: 12.2 us -> 14.3 us  [to_z(): lax.ppermute(block, 'chan', [(i, i // Z * Z + (i + step) % Z) for i in ra...]
    pallas_call x6 -> x14, Pallas kernels: 11.1 us -> 12.9 us  [the longest x13 7.03 us: on_chip(): pl.pallas_call(body, in_specs=[in_vmem] * len(args), out_specs=[in_vmem]...]
  transfers between devices with their start and end apart: 11 -> 16, of which waited for: 7 -> 7; matrix products, arithmetic and copies ran while one was open for 1% -> 0% of each run, Pallas kernels for 4% -> 6%
where the time goes in v4:
time: 94.7 us; the launch traced here: 94.3 us
  starting transfers between devices  30.5 us (32%)
  waiting for transfers between devices  28.1 us (30%)
  blocking collectives  19.4 us (20%)
  Pallas kernels  15.6 us (16%)
    all_to_all x1, blocking collectives, shards(): conv = lax.all_to_all(conv, 'seq', 0, 0).reshape(channels, -1)  19.4 us
    ppermute x1, waiting for transfers between devices, shards(): lax.ppermute(out_gate[:tokens // 2], 'seq', [(i, (i + parts // 2) % parts...  17.8 us
    ppermute x8, starting transfers between devices, to_z(): lax.ppermute(block, 'chan', [(i, i // Z * Z + (i + step) % Z) for i in ra...  14.3 us
    all_to_all x1, starting transfers between devices, shards(): packed = lax.all_to_all(packed, 'seq', 0, 0)  7.26 us
    pallas_call x13, Pallas kernels, on_chip(): pl.pallas_call(body, in_specs=[in_vmem] * len(args), out_specs=[in_vmem]...  7.03 us
    pallas_call x1, Pallas kernels, convolve(): pl.pallas_call(conv_kernel, in_specs=[near, near, near, far, far, far], o...  5.9 us
    ppermute x3, waiting for transfers between devices, to_near_x(): return lax.ppermute(block, 'chan', [(i, (i + Z) % n) for i in range(n)])  4.81 us
    ppermute x8, waiting for transfers between devices, to_z(): lax.ppermute(block, 'chan', [(i, i // Z * Z + (i + step) % Z) for i in ra...  3.75 us
  transfers between devices with their start and end apart: 16, of which 7 were waited for; matrix products, arithmetic and copies ran while one was open for 0% of the time, Pallas kernels for 6%

profile of v4, /device:TPU:0, one launch (start us, length us, event | category | flops | bytes accessed | tf_op | source)
XLA Modules:
  0.0 94.3 jit_solution(5304189859226465584)
XLA Ops:
  0.0 2.7 %prepare.1 = bf16[16,128,256]{2,1,0:T(8,128)(2,1)} custom-call(bf16[256,1024]{1,0:T(8,128)(2,1)} %in_gate.1, bf16[256,1024]{1,0:T(8,128)(2,1)} %signal.1, bf16[256,1024]{1,0:T(8,128)(2,1)} %taps.1), custom_call_target="tpu_custom_call" | custom-call | tf_op jit(solution)/shard_map/prepare/pallas_call | solution.py:55
  2.7 0.0 copy-start.1
  2.7 0.0 copy-start.2
  2.7 7.3 %all-to-all-start = ((bf16[16,128,256]{2,1,0:T(8,128)(2,1)}), bf16[16,128,256]{2,1,0:T(8,128)(2,1)S(1)}, u32[]{:S(2)}, u32[]{:S(2)}) async-start(bf16[16,128,256]{2,1,0:T(8,128)(2,1)} %prepare.1), calls=%async_computation | async-start | bytes 2097152 | tf_op jit(solution)/shard_map/all_to_all | solution.py:236
  10.1 3.5 %collective-permute-start = (bf16[128,1024]{1,0:T(8,128)(2,1)S(1)}, bf16[128,1024]{1,0:T(8,128)(2,1)S(1)}, u32[]{:S(2)}, u32[]{:S(2)}) collective-permute-start(bf16[128,1024]{1,0:T(8,128)(2,1)S(1)} %slice.3), channel_id=1, source_target_pairs={{0,64},{8,72},{16,80},{24,88},{32,96},{40,104},{48,112},{56,120},{... | collective-permute-start | bytes 786440 | tf_op jit(solution)/shard_map/ppermute | solution.py:234
  13.6 0.1 dynamic-slice_bitcast_fusion
  13.6 0.1 copy.8.skip
  13.7 17.8 %collective-permute-done.gate_other = bf16[128,1024]{1,0:T(8,128)(2,1)S(1)} collective-permute-done((bf16[128,1024]{1,0:T(8,128)(2,1)S(1)}, bf16[128,1024]{1,0:T(8,128)(2,1)S(1)}, u32[]{:S(2)}, u32[]{:S(2)}) %collective-permute-start) | collective-permute-done | bytes 262176 | tf_op jit(solution)/shard_map/ppermute | solution.py:234
  31.5 0.0 all-to-all-done.packed
  31.5 5.9 %convolve.1 = (bf16[16,64,384]{2,1,0:T(8,128)(2,1)S(1)}, bf16[1024,384]{1,0:T(8,128)(2,1)S(1)}, bf16[8192,1024]{1,0:T(8,128)(2,1)S(1)}) custom-call(bf16[16,128,256]{2,1,0:T(8,128)(2,1)S(1)} %all-to-all-done.packed, f32[64,1]{1,0:T(8,128)S(1)} %copy.8.skip, bf16[128,1024]{1,0:T(8,128)(2,1)S(1)} %collective-permute-done.gate_other, ...), custom_call_target="tpu_custom_call" | custom-call | tf_op jit(solution)/shard_map/convolve/pallas_call | solution.py:144
  37.4 19.4 %all_to_all.10 = bf16[16,64,384]{2,1,0:T(8,128)(2,1)S(1)} all-to-all(bf16[16,64,384]{2,1,0:T(8,128)(2,1)S(1)} %get-tuple-element.19), channel_id=1, replica_groups=mesh['seq'=16,'chan'=8] {'seq'}, dimensions={0} | all-to-all | bytes 1572864 | tf_op jit(solution)/shard_map/all_to_all | solution.py:240
  56.8 0.3 fusion.mixed
  57.1 0.6 shard_map.80
  57.7 2.0 %collective-permute-start.9 = (bf16[4,192,256]{2,1,0:T(8,128)(2,1)S(1)}, bf16[4,192,256]{2,1,0:T(8,128)(2,1)S(1)}, u32[]{:S(2)}, u32[]{:S(2)}) collective-permute-start(bf16[4,192,256]{2,1,0:T(8,128)(2,1)S(1)} %shard_map.80), channel_id=1, source_target_pairs={{0,1},{1,2},{2,3},{3,0},{4,5},{5,6},{6,7},{7,4},{8,9},{9,10},{10,1... | collective-permute-start | bytes 1179656 | tf_op jit(solution)/shard_map/ppermute | solution.py:205
  59.7 0.8 shard_map.75
  60.5 0.7 collective-permute-start.3
  61.2 0.6 collective-permute-start.4
  61.8 0.6 shard_map.81
  62.4 2.2 %collective-permute-start.10 = (bf16[4,192,256]{2,1,0:T(8,128)(2,1)S(1)}, bf16[4,192,256]{2,1,0:T(8,128)(2,1)S(1)}, u32[]{:S(2)}, u32[]{:S(2)}) collective-permute-start(bf16[4,192,256]{2,1,0:T(8,128)(2,1)S(1)} %shard_map.81), channel_id=1, source_target_pairs={{0,3},{1,0},{2,1},{3,2},{4,7},{5,4},{6,5},{7,6},{8,11},{9,8},{10,9... | collective-permute-start | bytes 1179656 | tf_op jit(solution)/shard_map/ppermute | solution.py:205
  64.6 0.8 shard_map.74
  65.4 0.9 collective-permute-start.1
  66.3 1.5 %shard_map.73.own = bf16[8,320,256]{2,1,0:T(8,128)(2,1)S(1)} custom-call(bf16[8192,1024]{1,0:T(8,128)(2,1)S(1)} %get-tuple-element.17.weight, bf16[1024,384]{1,0:T(8,128)(2,1)S(1)} %fusion.mixed), custom_call_target="tpu_custom_call" | custom-call | flops 1342177280 | bytes 1 | tf_op jit(solution)/shard_map/pallas_call | solution.py:169
  67.9 3.4 %collective-permute-done.3.near = bf16[4,320,128]{2,1,0:T(8,128)(2,1)S(1)} collective-permute-done((bf16[4,320,128]{2,1,0:T(8,128)(2,1)S(1)}, bf16[4,320,128]{2,1,0:T(8,128)(2,1)S(1)}, u32[]{:S(2)}, u32[]{:S(2)}) %collective-permute-start.3) | collective-permute-done | bytes 327712 | tf_op jit(solution)/shard_map/ppermute | solution.py:210
  71.2 0.0 collective-permute-start.2
  71.2 0.0 collective-permute-done.4.far
  71.3 0.2 shard_map.76
  71.4 2.3 %collective-permute-start.5 = (bf16[2,320,256]{2,1,0:T(8,128)(2,1)S(1)}, bf16[2,320,256]{2,1,0:T(8,128)(2,1)S(1)}, u32[]{:S(2)}, u32[]{:S(2)}) collective-permute-start(bf16[2,320,256]{2,1,0:T(8,128)(2,1)S(1)} %get-tuple-element.24), channel_id=1, source_target_pairs={{0,1},{1,2},{2,3},{3,0},{4,5},{5,6},{6,7},{7,4},{8,9},{9,10},{10,1... | collective-permute-start | bytes 983048 | tf_op jit(solution)/shard_map/ppermute | solution.py:205
  73.7 0.0 collective-permute-done.9.arrived.below.b_below
  73.7 1.0 %collective-permute-start.6 = (bf16[2,320,256]{2,1,0:T(8,128)(2,1)S(1)}, bf16[2,320,256]{2,1,0:T(8,128)(2,1)S(1)}, u32[]{:S(2)}, u32[]{:S(2)}) collective-permute-start(bf16[2,320,256]{2,1,0:T(8,128)(2,1)S(1)} %get-tuple-element.25), channel_id=1, source_target_pairs={{0,3},{1,0},{2,1},{3,2},{4,7},{5,4},{6,5},{7,6},{8,11},{9,8},{10,9... | collective-permute-start | bytes 983048 | tf_op jit(solution)/shard_map/ppermute | solution.py:205
  74.7 1.0 %shard_map.79.rest = bf16[8,192,256]{2,1,0:T(8,128)(2,1)S(1)} custom-call(bf16[8192,1024]{1,0:T(8,128)(2,1)S(1)} %get-tuple-element.17.weight, bf16[1024,384]{1,0:T(8,128)(2,1)S(1)} %fusion.mixed), custom_call_target="tpu_custom_call" | custom-call | flops 805306368 | bytes 1 | tf_op jit(solution)/shard_map/pallas_call | solution.py:169
  75.8 0.0 collective-permute-done.10.arrived.above.b_above
  75.8 1.1 %collective-permute-start.11 = (bf16[2,192,256]{2,1,0:T(8,128)(2,1)S(1)}, bf16[2,192,256]{2,1,0:T(8,128)(2,1)S(1)}, u32[]{:S(2)}, u32[]{:S(2)}) collective-permute-start(bf16[2,192,256]{2,1,0:T(8,128)(2,1)S(1)} %shard_map.82), channel_id=1, source_target_pairs={{0,1},{1,2},{2,3},{3,0},{4,5},{5,6},{6,7},{7,4},{8,9},{9,10},{10,1... | collective-permute-start | bytes 589832 | tf_op jit(solution)/shard_map/ppermute | solution.py:205
  76.9 0.0 collective-permute-done.1.near
  77.0 2.3 %collective-permute-start.12 = (bf16[2,192,256]{2,1,0:T(8,128)(2,1)S(1)}, bf16[2,192,256]{2,1,0:T(8,128)(2,1)S(1)}, u32[]{:S(2)}, u32[]{:S(2)}) collective-permute-start(bf16[2,192,256]{2,1,0:T(8,128)(2,1)S(1)} %shard_map.83), channel_id=1, source_target_pairs={{0,3},{1,0},{2,1},{3,2},{4,7},{5,4},{6,5},{7,6},{8,11},{9,8},{10,9... | collective-permute-start | bytes 589832 | tf_op jit(solution)/shard_map/ppermute | solution.py:205
  79.2 0.3 collective-permute-done.2.far
  79.5 3.6 %collective-permute-done.5.arrived.below = bf16[2,320,256]{2,1,0:T(8,128)(2,1)S(1)} collective-permute-done((bf16[2,320,256]{2,1,0:T(8,128)(2,1)S(1)}, bf16[2,320,256]{2,1,0:T(8,128)(2,1)S(1)}, u32[]{:S(2)}, u32[]{:S(2)}) %collective-permute-start.5) | collective-permute-done | bytes 327712 | tf_op jit(solution)/shard_map/ppermute | solution.py:205
  83.2 0.1 shard_map.77
  83.2 1.3 %collective-permute-start.7 = (bf16[1,320,256]{2,1,0:T(8,128)(2,1)S(1)}, bf16[1,320,256]{2,1,0:T(8,128)(2,1)S(1)}, u32[]{:S(2)}, u32[]{:S(2)}) collective-permute-start(bf16[1,320,256]{2,1,0:T(8,128)(2,1)S(1)} %shard_map.77), channel_id=1, source_target_pairs={{0,1},{1,2},{2,3},{3,0},{4,5},{5,6},{6,7},{7,4},{8,9},{9,10},{10,1... | collective-permute-start | bytes 491528 | tf_op jit(solution)/shard_map/ppermute | solution.py:205
  84.5 0.1 shard_map.78
  84.6 2.1 %collective-permute-start.8 = (bf16[1,320,256]{2,1,0:T(8,128)(2,1)S(1)}, bf16[1,320,256]{2,1,0:T(8,128)(2,1)S(1)}, u32[]{:S(2)}, u32[]{:S(2)}) collective-permute-start(bf16[1,320,256]{2,1,0:T(8,128)(2,1)S(1)} %shard_map.78), channel_id=1, source_target_pairs={{0,3},{1,0},{2,1},{3,2},{4,7},{5,4},{6,5},{7,6},{8,11},{9,8},{10,9... | collective-permute-start | bytes 491528 | tf_op jit(solution)/shard_map/ppermute | solution.py:205
  86.7 0.1 collective-permute-done.12.down.b_down
  86.8 0.1 shard_map.84
  86.9 0.3 collective-permute-start.13
  87.2 2.9 %collective-permute-start.14 = (bf16[384,128]{1,0:T(8,128)(2,1)S(1)}, bf16[384,128]{1,0:T(8,128)(2,1)S(1)}, u32[]{:S(2)}, u32[]{:S(2)}) collective-permute-start(bf16[384,128]{1,0:T(8,128)(2,1)S(1)} %get-tuple-element.27), channel_id=1, source_target_pairs={{0,68},{1,69},{2,70},{3,71},{4,64},{5,65},{6,66},{7,67},{8,76},{9,... | collective-permute-start | bytes 294920 | tf_op jit(solution)/shard_map/ppermute | solution.py:216
  90.1 1.4 %collective-permute-done.13.b_near = bf16[384,128]{1,0:T(8,128)(2,1)S(1)} collective-permute-done((bf16[384,128]{1,0:T(8,128)(2,1)S(1)}, bf16[384,128]{1,0:T(8,128)(2,1)S(1)}, u32[]{:S(2)}, u32[]{:S(2)}) %collective-permute-start.13) | collective-permute-done | bytes 98336 | tf_op jit(solution)/shard_map/ppermute | solution.py:210
  91.6 1.5 %collective-permute-done.14.b_far = bf16[384,128]{1,0:T(8,128)(2,1)S(1)} collective-permute-done((bf16[384,128]{1,0:T(8,128)(2,1)S(1)}, bf16[384,128]{1,0:T(8,128)(2,1)S(1)}, u32[]{:S(2)}, u32[]{:S(2)}) %collective-permute-start.14) | collective-permute-done | bytes 98336 | tf_op jit(solution)/shard_map/ppermute | solution.py:216
  93.0 0.0 collective-permute-done.7.up
  93.0 1.3 %shard_map.85 = (bf16[256,1024]{1,0:T(8,128)(2,1)}, bf16[1024,256]{1,0:T(8,128)(2,1)}) custom-call(bf16[8,320,256]{2,1,0:T(8,128)(2,1)S(1)} %shard_map.73.own, bf16[4,320,128]{2,1,0:T(8,128)(2,1)S(1)} %collective-permute-done.1.near, bf16[4,320,128]{2,1,0:T(8,128)(2,1)S(1)} %collective-permute-done.2.far, ...), custom_call_target="tpu_custom_call" | custom-call | bytes 1 | tf_op jit(solution)/shard_map/pallas_call | solution.py:169
  (10 shorter events, 0.1 us)
Async XLA Ops:
  0.0 13.6 %copy-start = (f32[1024]{0:T(1024)S(1)}, f32[1024]{0:T(1024)}, u32[]{:S(2)}) copy-start(f32[1024]{0:T(1024)} %param.11) | copy-start | bytes 12292
  2.7 7.3 %copy-start.1 = (bf16[256,1024]{1,0:T(8,128)(2,1)S(1)}, bf16[256,1024]{1,0:T(8,128)(2,1)}, u32[]{:S(2)}) copy-start(bf16[256,1024]{1,0:T(8,128)(2,1)} %gate_far.1) | copy-start | bytes 1572868
  2.7 28.8 %copy-start.2 = (bf16[1024,512]{1,0:T(8,128)(2,1)S(1)}, bf16[1024,512]{1,0:T(8,128)(2,1)}, u32[]{:S(2)}) copy-start(bf16[1024,512]{1,0:T(8,128)(2,1)} %constant.14.clone.table_far) | copy-start | bytes 3145732
  2.7 28.8 %all-to-all-start = ((bf16[16,128,256]{2,1,0:T(8,128)(2,1)}), bf16[16,128,256]{2,1,0:T(8,128)(2,1)S(1)}, u32[]{:S(2)}, u32[]{:S(2)}) async-start(bf16[16,128,256]{2,1,0:T(8,128)(2,1)} %prepare.1), calls=%async_computation | async-start | bytes 2097152 | tf_op jit(solution)/shard_map/all_to_all | solution.py:236
  10.1 21.4 %collective-permute-start = (bf16[128,1024]{1,0:T(8,128)(2,1)S(1)}, bf16[128,1024]{1,0:T(8,128)(2,1)S(1)}, u32[]{:S(2)}, u32[]{:S(2)}) collective-permute-start(bf16[128,1024]{1,0:T(8,128)(2,1)S(1)} %slice.3), channel_id=1, source_target_pairs={{0,64},{8,72},{16,80},{24,88},{32,96},{40,104},{48,112},{56,120},{... | collective-permute-start | bytes 786440 | tf_op jit(solution)/shard_map/ppermute | solution.py:234
  57.7 16.1 %collective-permute-start.9 = (bf16[4,192,256]{2,1,0:T(8,128)(2,1)S(1)}, bf16[4,192,256]{2,1,0:T(8,128)(2,1)S(1)}, u32[]{:S(2)}, u32[]{:S(2)}) collective-permute-start(bf16[4,192,256]{2,1,0:T(8,128)(2,1)S(1)} %shard_map.80), channel_id=1, source_target_pairs={{0,1},{1,2},{2,3},{3,0},{4,5},{5,6},{6,7},{7,4},{8,9},{9,10},{10,1... | collective-permute-start | bytes 1179656 | tf_op jit(solution)/shard_map/ppermute | solution.py:205
  60.5 10.7 %collective-permute-start.3 = (bf16[4,320,128]{2,1,0:T(8,128)(2,1)S(1)}, bf16[4,320,128]{2,1,0:T(8,128)(2,1)S(1)}, u32[]{:S(2)}, u32[]{:S(2)}) collective-permute-start(bf16[4,320,128]{2,1,0:T(8,128)(2,1)S(1)} %get-tuple-element.22), channel_id=1, source_target_pairs={{0,4},{1,5},{2,6},{3,7},{4,0},{5,1},{6,2},{7,3},{8,12},{9,13},{10,... | collective-permute-start | bytes 983048 | tf_op jit(solution)/shard_map/ppermute | solution.py:210
  61.2 10.0 %collective-permute-start.4 = (bf16[4,320,128]{2,1,0:T(8,128)(2,1)S(1)}, bf16[4,320,128]{2,1,0:T(8,128)(2,1)S(1)}, u32[]{:S(2)}, u32[]{:S(2)}) collective-permute-start(bf16[4,320,128]{2,1,0:T(8,128)(2,1)S(1)} %get-tuple-element.23), channel_id=1, source_target_pairs={{0,68},{1,69},{2,70},{3,71},{4,64},{5,65},{6,66},{7,67},{8,76},{9,... | collective-permute-start | bytes 983048 | tf_op jit(solution)/shard_map/ppermute | solution.py:216
  62.4 13.4 %collective-permute-start.10 = (bf16[4,192,256]{2,1,0:T(8,128)(2,1)S(1)}, bf16[4,192,256]{2,1,0:T(8,128)(2,1)S(1)}, u32[]{:S(2)}, u32[]{:S(2)}) collective-permute-start(bf16[4,192,256]{2,1,0:T(8,128)(2,1)S(1)} %shard_map.81), channel_id=1, source_target_pairs={{0,3},{1,0},{2,1},{3,2},{4,7},{5,4},{6,5},{7,6},{8,11},{9,8},{10,9... | collective-permute-start | bytes 1179656 | tf_op jit(solution)/shard_map/ppermute | solution.py:205
  65.4 11.5 %collective-permute-start.1 = (bf16[4,320,128]{2,1,0:T(8,128)(2,1)S(1)}, bf16[4,320,128]{2,1,0:T(8,128)(2,1)S(1)}, u32[]{:S(2)}, u32[]{:S(2)}) collective-permute-start(bf16[4,320,128]{2,1,0:T(8,128)(2,1)S(1)} %get-tuple-element.20), channel_id=1, source_target_pairs={{0,4},{1,5},{2,6},{3,7},{4,0},{5,1},{6,2},{7,3},{8,12},{9,13},{10,... | collective-permute-start | bytes 983048 | tf_op jit(solution)/shard_map/ppermute | solution.py:210
  71.2 8.3 %collective-permute-start.2 = (bf16[4,320,128]{2,1,0:T(8,128)(2,1)S(1)}, bf16[4,320,128]{2,1,0:T(8,128)(2,1)S(1)}, u32[]{:S(2)}, u32[]{:S(2)}) collective-permute-start(bf16[4,320,128]{2,1,0:T(8,128)(2,1)S(1)} %get-tuple-element.21), channel_id=1, source_target_pairs={{0,68},{1,69},{2,70},{3,71},{4,64},{5,65},{6,66},{7,67},{8,76},{9,... | collective-permute-start | bytes 983048 | tf_op jit(solution)/shard_map/ppermute | solution.py:216
  71.4 11.7 %collective-permute-start.5 = (bf16[2,320,256]{2,1,0:T(8,128)(2,1)S(1)}, bf16[2,320,256]{2,1,0:T(8,128)(2,1)S(1)}, u32[]{:S(2)}, u32[]{:S(2)}) collective-permute-start(bf16[2,320,256]{2,1,0:T(8,128)(2,1)S(1)} %get-tuple-element.24), channel_id=1, source_target_pairs={{0,1},{1,2},{2,3},{3,0},{4,5},{5,6},{6,7},{7,4},{8,9},{9,10},{10,1... | collective-permute-start | bytes 983048 | tf_op jit(solution)/shard_map/ppermute | solution.py:205
  73.7 10.8 %collective-permute-start.6 = (bf16[2,320,256]{2,1,0:T(8,128)(2,1)S(1)}, bf16[2,320,256]{2,1,0:T(8,128)(2,1)S(1)}, u32[]{:S(2)}, u32[]{:S(2)}) collective-permute-start(bf16[2,320,256]{2,1,0:T(8,128)(2,1)S(1)} %get-tuple-element.25), channel_id=1, source_target_pairs={{0,3},{1,0},{2,1},{3,2},{4,7},{5,4},{6,5},{7,6},{8,11},{9,8},{10,9... | collective-permute-start | bytes 983048 | tf_op jit(solution)/shard_map/ppermute | solution.py:205
  75.8 10.9 %collective-permute-start.11 = (bf16[2,192,256]{2,1,0:T(8,128)(2,1)S(1)}, bf16[2,192,256]{2,1,0:T(8,128)(2,1)S(1)}, u32[]{:S(2)}, u32[]{:S(2)}) collective-permute-start(bf16[2,192,256]{2,1,0:T(8,128)(2,1)S(1)} %shard_map.82), channel_id=1, source_target_pairs={{0,1},{1,2},{2,3},{3,0},{4,5},{5,6},{6,7},{7,4},{8,9},{9,10},{10,1... | collective-permute-start | bytes 589832 | tf_op jit(solution)/shard_map/ppermute | solution.py:205
  77.0 9.8 %collective-permute-start.12 = (bf16[2,192,256]{2,1,0:T(8,128)(2,1)S(1)}, bf16[2,192,256]{2,1,0:T(8,128)(2,1)S(1)}, u32[]{:S(2)}, u32[]{:S(2)}) collective-permute-start(bf16[2,192,256]{2,1,0:T(8,128)(2,1)S(1)} %shard_map.83), channel_id=1, source_target_pairs={{0,3},{1,0},{2,1},{3,2},{4,7},{5,4},{6,5},{7,6},{8,11},{9,8},{10,9... | collective-permute-start | bytes 589832 | tf_op jit(solution)/shard_map/ppermute | solution.py:205
  83.2 9.8 %collective-permute-start.7 = (bf16[1,320,256]{2,1,0:T(8,128)(2,1)S(1)}, bf16[1,320,256]{2,1,0:T(8,128)(2,1)S(1)}, u32[]{:S(2)}, u32[]{:S(2)}) collective-permute-start(bf16[1,320,256]{2,1,0:T(8,128)(2,1)S(1)} %shard_map.77), channel_id=1, source_target_pairs={{0,1},{1,2},{2,3},{3,0},{4,5},{5,6},{6,7},{7,4},{8,9},{9,10},{10,1... | collective-permute-start | bytes 491528 | tf_op jit(solution)/shard_map/ppermute | solution.py:205
  84.6 8.5 %collective-permute-start.8 = (bf16[1,320,256]{2,1,0:T(8,128)(2,1)S(1)}, bf16[1,320,256]{2,1,0:T(8,128)(2,1)S(1)}, u32[]{:S(2)}, u32[]{:S(2)}) collective-permute-start(bf16[1,320,256]{2,1,0:T(8,128)(2,1)S(1)} %shard_map.78), channel_id=1, source_target_pairs={{0,3},{1,0},{2,1},{3,2},{4,7},{5,4},{6,5},{7,6},{8,11},{9,8},{10,9... | collective-permute-start | bytes 491528 | tf_op jit(solution)/shard_map/ppermute | solution.py:205
  86.9 4.7 %collective-permute-start.13 = (bf16[384,128]{1,0:T(8,128)(2,1)S(1)}, bf16[384,128]{1,0:T(8,128)(2,1)S(1)}, u32[]{:S(2)}, u32[]{:S(2)}) collective-permute-start(bf16[384,128]{1,0:T(8,128)(2,1)S(1)} %get-tuple-element.26), channel_id=1, source_target_pairs={{0,4},{1,5},{2,6},{3,7},{4,0},{5,1},{6,2},{7,3},{8,12},{9,13},{10,... | collective-permute-start | bytes 294920 | tf_op jit(solution)/shard_map/ppermute | solution.py:210
  87.2 5.8 %collective-permute-start.14 = (bf16[384,128]{1,0:T(8,128)(2,1)S(1)}, bf16[384,128]{1,0:T(8,128)(2,1)S(1)}, u32[]{:S(2)}, u32[]{:S(2)}) collective-permute-start(bf16[384,128]{1,0:T(8,128)(2,1)S(1)} %get-tuple-element.27), channel_id=1, source_target_pairs={{0,68},{1,69},{2,70},{3,71},{4,64},{5,65},{6,66},{7,67},{8,76},{9,... | collective-permute-start | bytes 294920 | tf_op jit(solution)/shard_map/ppermute | solution.py:216

commit v5 on v3

--- a/solution.py
+++ b/solution.py
@@ -1,5 +1,3 @@
-import functools
-
 import numpy as np
 
 import jax
@@ -66,17 +64,15 @@
 
 
 def conv_kernel(
-    packed, skip, table_far, gate_far, weight_far, out, gate_t, weight, table, gate, g_spec, p_spec, acc_high, acc_low, sems
+    packed, skip, table_far, weight_far, out, weight, table, g_spec, p_spec, acc_high, acc_low, sems
 ):
     copies = [
         pltpu.make_async_copy(source, target, sems.at[i])
-        for i, (source, target) in enumerate(((table_far, table), (gate_far, gate), (weight_far, weight)))
+        for i, (source, target) in enumerate(((table_far, table), (weight_far, weight)))
     ]
     for copy in copies:
         copy.start()
     copies[0].wait()
-    copies[1].wait()
-    gate_t[...] = gate[...].T
     blocks, both, n = packed.shape
     ch = both // 2
     lane = lax.broadcasted_iota(jnp.int32, (1, n), 1)
@@ -132,65 +128,63 @@
         conv = (inverse(high, 0) + inverse(low, 0) + inverse(high, 1)).reshape(group, ch, n)
         gated = packed[b : b + group, :ch, :].astype(F32)
         out[b : b + group] = (conv + skip[...][None] * gated).astype(BF16)
-    copies[2].wait()
-
-
-def convolve(packed, skip, table, gate, weight):
+    copies[1].wait()
+
+
+def convolve(packed, skip, table, weight):
     blocks, both, n = packed.shape
     ch = both // 2
     near, far = pl.BlockSpec(memory_space=pltpu.VMEM), pl.BlockSpec(memory_space=pltpu.HBM)
     return pl.pallas_call(
         conv_kernel,
-        in_specs=[near, near, far, far, far],
-        out_specs=[near] * 3,
+        in_specs=[near, near, far, far],
+        out_specs=[near] * 2,
         out_shape=[
             jax.ShapeDtypeStruct((blocks, ch, n), BF16),
-            jax.ShapeDtypeStruct(gate.shape[::-1], BF16),
             jax.ShapeDtypeStruct(weight.shape, BF16),
         ],
         scratch_shapes=[
             pltpu.VMEM(table.shape, BF16),
-            pltpu.VMEM(gate.shape, BF16),
             pltpu.VMEM((blocks, ch, 2 * n), F32),
             pltpu.VMEM((blocks, ch, 2 * n), F32),
             pltpu.VMEM((blocks, ch, 2 * n), BF16),
             pltpu.VMEM((blocks, ch, 2 * n), BF16),
-            pltpu.SemaphoreType.DMA((3,)),
+            pltpu.SemaphoreType.DMA((2,)),
         ],
         compiler_params=pltpu.CompilerParams(vmem_limit_bytes=28 * 2**20),
         name="convolve",
-    )(packed, skip, table, gate, weight)
-
-
-def project_kernel(weight, mixed, out, *, pieces, chunk):
-    me = lax.axis_index("chan")
-    rows = out.shape[1]
-    for i, (flip, step, offset) in enumerate(pieces):
-        start = ((me // Z + flip) % 2 * Z + (me % Z + step) % Z) * chunk + offset
-        block = weight[pl.ds(pl.multiple_of(start, 16), rows), :]
-        out[i] = jnp.dot(block, mixed[...], preferred_element_type=F32).astype(BF16)
-
-
-def project(weight, mixed, pieces, rows, chunk):
-    channels, tokens = mixed.shape
-    count = len(pieces)
+    )(packed, skip, table, weight)
+
+
+def on_chip(body, shapes, *args, flops=0):
     in_vmem = pl.BlockSpec(memory_space=pltpu.VMEM)
     return pl.pallas_call(
-        functools.partial(project_kernel, pieces=pieces, chunk=chunk),
-        in_specs=[in_vmem] * 2,
-        out_specs=in_vmem,
-        out_shape=jax.ShapeDtypeStruct((count, rows, tokens), BF16),
+        body,
+        in_specs=[in_vmem] * len(args),
+        out_specs=[in_vmem] * len(shapes),
+        out_shape=[jax.ShapeDtypeStruct(shape, BF16) for shape in shapes],
         compiler_params=pltpu.CompilerParams(vmem_limit_bytes=8 * 2**20),
-        cost_estimate=pl.CostEstimate(
-            flops=2 * count * rows * channels * tokens,
-            bytes_accessed=2 * count * rows * tokens,
-            transcendentals=0,
-        ),
-        name="project",
-    )(weight, mixed)
+        cost_estimate=pl.CostEstimate(flops=flops, bytes_accessed=1, transcendentals=0),
+    )(*args)
 
 
 Z = 4
+
+
+def project(weight, mixed, groups, rows, chunk):
+    channels, tokens = mixed.shape
+
+    def body(weight, mixed, *outs):
+        me = lax.axis_index("chan")
+        for pieces, out in zip(groups, outs, strict=True):
+            for i, (flip, step, offset) in enumerate(pieces):
+                start = ((me // Z + flip) % 2 * Z + (me % Z + step) % Z) * chunk + offset
+                block = weight[pl.ds(pl.multiple_of(start, 16), rows), :]
+                out[i] = jnp.dot(block, mixed[...], preferred_element_type=F32).astype(BF16)
+
+    shapes = [(len(pieces), rows, tokens) for pieces in groups]
+    total = sum(shape[0] for shape in shapes) * rows
+    return on_chip(body, shapes, weight, mixed, flops=2 * total * channels * tokens)
 
 
 def to_z(block, step):
@@ -198,57 +192,109 @@
     return lax.ppermute(block, "chan", [(i, i // Z * Z + (i + step) % Z) for i in range(n)])
 
 
-def to_other_x(block):
+def to_x(block):
     n = lax.axis_size("chan")
     return lax.ppermute(block, "chan", [(i, (i + Z) % n) for i in range(n)])
 
 
-def reduce_z(plus, minus, keep_plus, keep_minus, own_first, own_second):
-    from_below, from_above = to_z(plus, 1), to_z(minus, -1)
-    k = keep_plus.shape[0]
-    up = to_z((keep_plus.astype(F32) + from_below[:k].astype(F32)).astype(BF16), 1)
-    down = to_z((keep_minus.astype(F32) + from_above[:k].astype(F32)).astype(BF16), -1)
-    first = own_first.astype(F32) + from_above[k:].astype(F32) + up.astype(F32)
-    second = own_second.astype(F32) + from_below[k:].astype(F32) + down.astype(F32)
-    return first, second
+def wide_sum(*terms):
+    total = terms[0].astype(F32)
+    for term in terms[1:]:
+        total = total + term.astype(F32)
+    return total
+
+
+def add(*parts):
+    arrays = [part[0] for part in parts]
+    cuts = [part[1:] for part in parts]
+
+    def body(*refs):
+        refs[-1][...] = wide_sum(*(ref[a:b] for ref, (a, b) in zip(refs[:-1], cuts, strict=True))).astype(BF16)
+
+    count = cuts[0][1] - cuts[0][0]
+    (total,) = on_chip(body, [(count,) + arrays[0].shape[1:]], *arrays)
+    return total
 
 
 def shards(out_gate, in_gate, signal, filter_taps, skip_gain, out_proj):
     tokens, channels = out_gate.shape
     parts, chans = lax.axis_size("seq"), lax.axis_size("chan")
     per_part = channels // parts
-    packed = prepare(in_gate, signal, filter_taps, parts)
-    packed = lax.all_to_all(packed, "seq", 0, 0)
+    packed, out_gate = lax.optimization_barrier((prepare(in_gate, signal, filter_taps, parts), out_gate))
+
+    def turn(gate, out):
+        out[...] = gate[...].T
+
+    (gate_t,) = on_chip(turn, [(channels, tokens)], out_gate)
+    packed, gate_t = lax.optimization_barrier((lax.all_to_all(packed, "seq", 0, 0), gate_t))
     skip = lax.dynamic_slice_in_dim(skip_gain, lax.axis_index("seq") * per_part, per_part, 0)
     table = jnp.asarray(transform_table(tokens))
-    conv, out_gate_t, out_proj = convolve(packed, skip[:, None], table, out_gate, out_proj)
+    conv, out_proj = convolve(packed, skip[:, None], table, out_proj)
     conv = lax.all_to_all(conv, "seq", 0, 0).reshape(channels, tokens)
-
-    mixed = (out_gate_t.astype(F32) * conv.astype(F32)).astype(BF16)
+    mixed = (gate_t.astype(F32) * conv.astype(F32)).astype(BF16)
+
     chunk = out_proj.shape[0] // chans
-    half_a = 192
+    half_a = 224
     half_b = chunk // 2 - half_a
-    order = [(2, 0), (1, 1), (2, 1), (3, 0), (1, 0), (3, 1), (0, 0), (0, 1)]
-    rows_a = [[(flip, s, h * half_a) for s, h in order] for flip in (0, 1)]
-    rows_b = [(flip, s, 2 * half_a + h * half_b) for s, h in order for flip in (0, 1)]
-
-    from_x = to_other_x(project(out_proj, mixed, rows_a[1], half_a, chunk))
-    plus_b = project(out_proj, mixed, rows_b[:4], half_b, chunk)
-    minus_b = project(out_proj, mixed, rows_b[4:8], half_b, chunk)
-    own_a = project(out_proj, mixed, rows_a[0], half_a, chunk)
-    rest_b = project(out_proj, mixed, rows_b[8:], half_b, chunk)
-
-    def summed_a(lo, hi):
-        return own_a[lo:hi].astype(F32) + from_x[lo:hi].astype(F32)
-
-    b_first, b_second = reduce_z(plus_b, minus_b, rest_b[:2], rest_b[2:4], rest_b[4:6], rest_b[6:8])
-    other_b = to_other_x(jnp.stack([b_first[1], b_second[1]]).astype(BF16)).astype(F32)
-    a_first, a_second = reduce_z(
-        summed_a(0, 2).astype(BF16), summed_a(2, 4).astype(BF16),
-        summed_a(4, 5), summed_a(5, 6), summed_a(6, 7), summed_a(7, 8),
+
+    def rows_a(flip, *places):
+        return [(flip, step, h * half_a) for step, h in places]
+
+    def rows_b(*places):
+        return [(flip, step, 2 * half_a + h * half_b) for step, h in places for flip in (0, 1)]
+
+    early, late = ((2, 0), (1, 1), (2, 1), (3, 0)), ((1, 0), (3, 1), (0, 0), (0, 1))
+    run = lambda rows, *groups: project(out_proj, mixed, groups, rows, chunk)
+    relay_up, relay_down = run(half_b, rows_b((2, 0)), rows_b((2, 1)))
+    relay_up, relay_down, mixed = lax.optimization_barrier((relay_up, relay_down, mixed))
+    relayed_up, relayed_down = to_z(relay_up, 1), to_z(relay_down, -1)
+    (x_early,) = run(half_a, rows_a(1, *early))
+    x_early = to_x(x_early)
+    direct_up, direct_down = run(half_b, rows_b((1, 1)), rows_b((3, 0)))
+    b_below, b_above = to_z(direct_up, 1), to_z(direct_down, -1)
+    (x_late,) = run(half_a, rows_a(1, *late))
+    x_late = to_x(x_late)
+    (rest_b,) = run(half_b, rows_b(*late))
+    (own_a,) = run(half_a, rows_a(0, *early, *late))
+
+    b_up = to_z(add((rest_b, 0, 2), (relayed_up, 0, 2)), 1)
+    b_down = to_z(add((rest_b, 2, 4), (relayed_down, 0, 2)), -1)
+
+    def first_a(own, arrived, up, down):
+        total = wide_sum(own[:4], arrived[...]).astype(BF16)
+        up[...] = total[:2]
+        down[...] = total[2:]
+
+    up, down = on_chip(first_a, [(2, half_a, tokens)] * 2, own_a, x_early)
+    a_below, a_above = to_z(up, 1), to_z(down, -1)
+    a_up = to_z(add((own_a, 4, 5), (x_late, 0, 1), (a_below, 0, 1)), 1)
+    a_down = to_z(add((own_a, 5, 6), (x_late, 1, 2), (a_above, 0, 1)), -1)
+
+    def reduced_b(flip, rest, below, above, up, down):
+        first = wide_sum(rest[4 + flip], above[flip], up[flip])
+        second = wide_sum(rest[6 + flip], below[flip], down[flip])
+        return jnp.concatenate([first, second], axis=0)
+
+    def third_b(*refs):
+        refs[-1][...] = reduced_b(1, *refs[:-1]).astype(BF16)
+
+    (x_last,) = on_chip(third_b, [(2 * half_b, tokens)], rest_b, b_below, b_above, b_up, b_down)
+    x_last = to_x(x_last)
+
+    def last(own, x_late, below, above, up, down, x_last, rest, b_below, b_above, b_up, b_down, out, all_rows):
+        first = wide_sum(own[6], x_late[2], above[1], up[0])
+        second = wide_sum(own[7], x_late[3], below[1], down[0])
+        all_rows[:half_a] = first.astype(BF16)
+        all_rows[half_a : 2 * half_a] = second.astype(BF16)
+        b_rows = reduced_b(0, rest, b_below, b_above, b_up, b_down) + x_last[...].astype(F32)
+        all_rows[2 * half_a :] = b_rows.astype(BF16)
+        out[...] = all_rows[...].T
+
+    out, _ = on_chip(
+        last, [(tokens, chunk), (chunk, tokens)], own_a, x_late, a_below, a_above, a_up, a_down,
+        x_last, rest_b, b_below, b_above, b_up, b_down,
     )
-    rows = [a_first[0], a_second[0], b_first[0] + other_b[0], b_second[0] + other_b[1]]
-    return jnp.concatenate([r.astype(BF16) for r in rows], axis=0).T
+    return out
 
 
 def solution(mesh):

time: 102 us -> 87.9 us (0.86)
  waiting for transfers between devices: 48.8 us -> 25.8 us
  starting transfers between devices: 20.9 us -> 28.1 us
  Pallas kernels: 13.8 us -> 15.8 us
  local copies, waits for them, and re-layouts: 1.23 us -> 2.45 us
    ppermute x2 -> x3, waiting for transfers between devices: 16 us -> 0.01 us  [to_x(): return lax.ppermute(block, 'chan', [(i, (i + Z) % n) for i in range(n)])]
    ppermute x8 -> x10, waiting for transfers between devices: 15 us -> 9.17 us  [to_z(): lax.ppermute(block, 'chan', [(i, i // Z * Z + (i + step) % Z) for i in ra...]
    ppermute x8 -> x10, starting transfers between devices: 12.2 us -> 17.4 us  [to_z(): lax.ppermute(block, 'chan', [(i, i // Z * Z + (i + step) % Z) for i in ra...]
    unnamed x6, local copies, waits for them, and re-layouts: 0.02 us -> 2.27 us
    ppermute x2 -> x3, starting transfers between devices: 1.44 us -> 3.66 us  [to_x(): return lax.ppermute(block, 'chan', [(i, (i + Z) % n) for i in range(n)])]
    pallas_call x6 -> x15, Pallas kernels: 11.1 us -> 13.1 us  [the longest x14 7.22 us: on_chip(): pl.pallas_call(body, in_specs=[in_vmem] * len(args), out_specs=[in_vmem]...]
    all_to_all x1, waiting for transfers between devices: 17.8 us -> 16.6 us  [shards(): lax.all_to_all(packed, 'seq', 0, 0)]
  transfers between devices with their start and end apart: 11 -> 14, of which waited for: 7 -> 5; matrix products, arithmetic and copies ran while one was open for 1% -> 0% of each run, Pallas kernels for 4% -> 5%
where the time goes in v5:
time: 87.9 us; the launch traced here: 87.5 us
  starting transfers between devices  28.1 us (32%)
  waiting for transfers between devices  25.8 us (29%)
  Pallas kernels  15.8 us (18%)
  blocking collectives  15 us (17%)
  local copies, waits for them, and re-layouts  2.45 us (3%)
    ppermute x10, starting transfers between devices, to_z(): lax.ppermute(block, 'chan', [(i, i // Z * Z + (i + step) % Z) for i in ra...  17.4 us
    all_to_all x1, waiting for transfers between devices, shards(): lax.all_to_all(packed, 'seq', 0, 0)  16.6 us
    all_to_all x1, blocking collectives, shards(): conv = lax.all_to_all(conv, 'seq', 0, 0).reshape(channels, tokens)  15 us
    ppermute x10, waiting for transfers between devices, to_z(): lax.ppermute(block, 'chan', [(i, i // Z * Z + (i + step) % Z) for i in ra...  9.17 us
    pallas_call x14, Pallas kernels, on_chip(): pl.pallas_call(body, in_specs=[in_vmem] * len(args), out_specs=[in_vmem]...  7.22 us
    all_to_all x1, starting transfers between devices, shards(): lax.all_to_all(packed, 'seq', 0, 0)  7.13 us
    pallas_call x1, Pallas kernels, convolve(): pl.pallas_call(conv_kernel, in_specs=[near, near, far, far], out_specs=[n...  5.86 us
    ppermute x3, starting transfers between devices, to_x(): return lax.ppermute(block, 'chan', [(i, (i + Z) % n) for i in range(n)])  3.66 us
  transfers between devices with their start and end apart: 14, of which 5 were waited for; matrix products, arithmetic and copies ran while one was open for 0% of the time, Pallas kernels for 5%

profile of v5, /device:TPU:0, one launch (start us, length us, event | category | flops | bytes accessed | tf_op | source)
XLA Modules:
  0.0 87.5 jit_solution(15075738899246874472)
XLA Ops:
  0.0 2.7 %prepare.1 = bf16[16,128,256]{2,1,0:T(8,128)(2,1)} custom-call(bf16[256,1024]{1,0:T(8,128)(2,1)} %in_gate.1, bf16[256,1024]{1,0:T(8,128)(2,1)} %signal.1, bf16[256,1024]{1,0:T(8,128)(2,1)} %taps.1), custom_call_target="tpu_custom_call" | custom-call | tf_op jit(solution)/shard_map/prepare/pallas_call | solution.py:55
  2.7 7.1 %all-to-all-start = ((bf16[16,128,256]{2,1,0:T(8,128)(2,1)}), bf16[16,128,256]{2,1,0:T(8,128)(2,1)S(1)}, u32[]{:S(2)}, u32[]{:S(2)}) async-start(bf16[16,128,256]{2,1,0:T(8,128)(2,1)} %prepare.1), calls=%async_computation | async-start | bytes 2097152 | tf_op jit(solution)/shard_map/all_to_all | solution.py:229
  9.9 0.1 dynamic-slice_bitcast_fusion
  9.9 0.1 copy.8.skip
  10.1 1.0 %copy-done.2 = bf16[256,1024]{1,0:T(8,128)(2,1)S(1)} copy-done((bf16[256,1024]{1,0:T(8,128)(2,1)S(1)}, bf16[256,1024]{1,0:T(8,128)(2,1)}, u32[]{:S(2)}) %copy-start.2) | copy-done | bytes 524312
  11.1 0.2 shard_map.73
  11.3 16.6 %all-to-all-done.packed = bf16[16,128,256]{2,1,0:T(8,128)(2,1)S(1)} async-done(((bf16[16,128,256]{2,1,0:T(8,128)(2,1)}), bf16[16,128,256]{2,1,0:T(8,128)(2,1)S(1)}, u32[]{:S(2)}, u32[]{:S(2)}) %all-to-all-start) | async-done | bytes 1048608 | tf_op jit(solution)/shard_map/all_to_all | solution.py:229
  27.9 1.2 %copy-done.1 = bf16[1024,512]{1,0:T(8,128)(2,1)S(1)} copy-done((bf16[1024,512]{1,0:T(8,128)(2,1)S(1)}, bf16[1024,512]{1,0:T(8,128)(2,1)}, u32[]{:S(2)}) %copy-start.1) | copy-done | bytes 1048600
  29.1 5.9 %convolve.1 = (bf16[16,64,256]{2,1,0:T(8,128)(2,1)S(1)}, bf16[8192,1024]{1,0:T(8,128)(2,1)S(1)}) custom-call(bf16[16,128,256]{2,1,0:T(8,128)(2,1)S(1)} %all-to-all-done.packed, f32[64,1]{1,0:T(8,128)S(1)} %copy.8.skip, bf16[1024,512]{1,0:T(8,128)(2,1)S(1)} %copy-done.1, bf16[8192,1024]{1,0:T(8,128)(2,1)} %weight_far.1), custom_call_target="tpu_custom_call" | custom-call | tf_op jit(solution)/shard_map/convolve/pallas_call | solution.py:138
  35.0 15.0 %all_to_all.10 = bf16[16,64,256]{2,1,0:T(8,128)(2,1)S(1)} all-to-all(bf16[16,64,256]{2,1,0:T(8,128)(2,1)S(1)} %get-tuple-element.26), channel_id=1, replica_groups=mesh['seq'=16,'chan'=8] {'seq'}, dimensions={0} | all-to-all | bytes 1048576 | tf_op jit(solution)/shard_map/all_to_all | solution.py:233
  50.0 0.2 fusion.mixed
  50.1 0.8 shard_map.74
  50.9 0.6 shard_map.77
  51.6 0.7 collective-permute-start.1
  52.3 1.9 %collective-permute-start.8 = (bf16[2,288,256]{2,1,0:T(8,128)(2,1)S(1)}, bf16[2,288,256]{2,1,0:T(8,128)(2,1)S(1)}, u32[]{:S(2)}, u32[]{:S(2)}) collective-permute-start(bf16[2,288,256]{2,1,0:T(8,128)(2,1)S(1)} %get-tuple-element.34), channel_id=1, source_target_pairs={{0,1},{1,2},{2,3},{3,0},{4,5},{5,6},{6,7},{7,4},{8,9},{9,10},{10,1... | collective-permute-start | bytes 884744 | tf_op jit(solution)/shard_map/ppermute | solution.py:192
  54.2 2.1 %collective-permute-start.10 = (bf16[2,288,256]{2,1,0:T(8,128)(2,1)S(1)}, bf16[2,288,256]{2,1,0:T(8,128)(2,1)S(1)}, u32[]{:S(2)}, u32[]{:S(2)}) collective-permute-start(bf16[2,288,256]{2,1,0:T(8,128)(2,1)S(1)} %get-tuple-element.35), channel_id=1, source_target_pairs={{0,3},{1,0},{2,1},{3,2},{4,7},{5,4},{6,5},{7,6},{8,11},{9,8},{10,9... | collective-permute-start | bytes 884744 | tf_op jit(solution)/shard_map/ppermute | solution.py:192
  56.3 0.8 shard_map.82
  57.1 0.1 collective-permute-start.6
  57.2 3.2 %collective-permute-start.7 = (bf16[2,288,256]{2,1,0:T(8,128)(2,1)S(1)}, bf16[2,288,256]{2,1,0:T(8,128)(2,1)S(1)}, u32[]{:S(2)}, u32[]{:S(2)}) collective-permute-start(bf16[2,288,256]{2,1,0:T(8,128)(2,1)S(1)} %get-tuple-element.33), channel_id=1, source_target_pairs={{0,3},{1,0},{2,1},{3,2},{4,7},{5,4},{6,5},{7,6},{8,11},{9,8},{10,9... | collective-permute-start | bytes 884744 | tf_op jit(solution)/shard_map/ppermute | solution.py:192
  60.4 1.4 %shard_map.81.refs_0_.rest = bf16[8,288,256]{2,1,0:T(8,128)(2,1)S(1)} custom-call(bf16[8192,1024]{1,0:T(8,128)(2,1)S(1)} %get-tuple-element.24.weight, bf16[1024,256]{1,0:T(8,128)(2,1)S(1)} %fusion.mixed), custom_call_target="tpu_custom_call" | custom-call | flops 1207959552 | bytes 1 | tf_op jit(solution)/shard_map/pallas_call | solution.py:161
  61.8 2.4 %collective-permute-done.8.refs_1_ = bf16[2,288,256]{2,1,0:T(8,128)(2,1)S(1)} collective-permute-done((bf16[2,288,256]{2,1,0:T(8,128)(2,1)S(1)}, bf16[2,288,256]{2,1,0:T(8,128)(2,1)S(1)}, u32[]{:S(2)}, u32[]{:S(2)}) %collective-permute-start.8) | collective-permute-done | bytes 294944 | tf_op jit(solution)/shard_map/ppermute | solution.py:192
  64.2 0.1 shard_map.83
  64.3 0.1 collective-permute-start.9
  64.4 0.0 collective-permute-done.10.refs_1_
  64.4 0.1 shard_map.84
  64.5 3.3 %collective-permute-start.11 = (bf16[2,288,256]{2,1,0:T(8,128)(2,1)S(1)}, bf16[2,288,256]{2,1,0:T(8,128)(2,1)S(1)}, u32[]{:S(2)}, u32[]{:S(2)}) collective-permute-start(bf16[2,288,256]{2,1,0:T(8,128)(2,1)S(1)} %shard_map.84), channel_id=1, source_target_pairs={{0,3},{1,0},{2,1},{3,2},{4,7},{5,4},{6,5},{7,6},{8,11},{9,8},{10,9... | collective-permute-start | bytes 884744 | tf_op jit(solution)/shard_map/ppermute | solution.py:192
  67.8 0.6 shard_map.76
  68.4 0.0 collective-permute-done.1.arrived
  68.4 1.5 %collective-permute-start = (bf16[4,224,256]{2,1,0:T(8,128)(2,1)S(1)}, bf16[4,224,256]{2,1,0:T(8,128)(2,1)S(1)}, u32[]{:S(2)}, u32[]{:S(2)}) collective-permute-start(bf16[4,224,256]{2,1,0:T(8,128)(2,1)S(1)} %shard_map.76), channel_id=1, source_target_pairs={{0,4},{1,5},{2,6},{3,7},{4,0},{5,1},{6,2},{7,3},{8,12},{9,13},{10,... | collective-permute-start | bytes 1376264 | tf_op jit(solution)/shard_map/ppermute | solution.py:197
  69.9 1.1 %shard_map.75.own.refs_0_ = bf16[8,224,256]{2,1,0:T(8,128)(2,1)S(1)} custom-call(bf16[8192,1024]{1,0:T(8,128)(2,1)S(1)} %get-tuple-element.24.weight, bf16[1024,256]{1,0:T(8,128)(2,1)S(1)} %fusion.mixed), custom_call_target="tpu_custom_call" | custom-call | flops 939524096 | bytes 1 | tf_op jit(solution)/shard_map/pallas_call | solution.py:161
  71.0 0.1 shard_map.78
  71.1 0.0 collective-permute-done.6.refs_1_.b_below
  71.1 0.1 collective-permute-start.2
  71.2 0.0 collective-permute-done.7.refs_2_.b_above
  71.2 3.2 %collective-permute-start.3 = (bf16[2,224,256]{2,1,0:T(8,128)(2,1)S(1)}, bf16[2,224,256]{2,1,0:T(8,128)(2,1)S(1)}, u32[]{:S(2)}, u32[]{:S(2)}) collective-permute-start(bf16[2,224,256]{2,1,0:T(8,128)(2,1)S(1)} %get-tuple-element.31), channel_id=1, source_target_pairs={{0,3},{1,0},{2,1},{3,2},{4,7},{5,4},{6,5},{7,6},{8,11},{9,8},{10,9... | collective-permute-start | bytes 688136 | tf_op jit(solution)/shard_map/ppermute | solution.py:192
  74.4 2.4 %collective-permute-done.9.refs_3_.b_up = bf16[2,288,256]{2,1,0:T(8,128)(2,1)S(1)} collective-permute-done((bf16[2,288,256]{2,1,0:T(8,128)(2,1)S(1)}, bf16[2,288,256]{2,1,0:T(8,128)(2,1)S(1)}, u32[]{:S(2)}, u32[]{:S(2)}) %collective-permute-start.9) | collective-permute-done | bytes 294944 | tf_op jit(solution)/shard_map/ppermute | solution.py:192
  76.9 0.0 collective-permute-done.11.refs_4_.b_down
  76.9 0.1 shard_map.85
  77.0 1.5 %collective-permute-start.12 = (bf16[576,256]{1,0:T(8,128)(2,1)S(1)}, bf16[576,256]{1,0:T(8,128)(2,1)S(1)}, u32[]{:S(2)}, u32[]{:S(2)}) collective-permute-start(bf16[576,256]{1,0:T(8,128)(2,1)S(1)} %shard_map.85), channel_id=1, source_target_pairs={{0,4},{1,5},{2,6},{3,7},{4,0},{5,1},{6,2},{7,3},{8,12},{9,13},{10,... | collective-permute-start | bytes 884744 | tf_op jit(solution)/shard_map/ppermute | solution.py:197
  78.5 0.0 collective-permute-done.refs_1_.x_late
  78.5 1.6 %collective-permute-done.2.refs_2_.below = bf16[2,224,256]{2,1,0:T(8,128)(2,1)S(1)} collective-permute-done((bf16[2,224,256]{2,1,0:T(8,128)(2,1)S(1)}, bf16[2,224,256]{2,1,0:T(8,128)(2,1)S(1)}, u32[]{:S(2)}, u32[]{:S(2)}) %collective-permute-start.2) | collective-permute-done | bytes 229408 | tf_op jit(solution)/shard_map/ppermute | solution.py:192
  80.2 0.2 collective-permute-start.4
  80.4 0.0 collective-permute-done.3.refs_2_.above
  80.4 3.1 %collective-permute-start.5 = (bf16[1,224,256]{2,1,0:T(8,128)(2,1)S(1)}, bf16[1,224,256]{2,1,0:T(8,128)(2,1)S(1)}, u32[]{:S(2)}, u32[]{:S(2)}) collective-permute-start(bf16[1,224,256]{2,1,0:T(8,128)(2,1)S(1)} %shard_map.80), channel_id=1, source_target_pairs={{0,3},{1,0},{2,1},{3,2},{4,7},{5,4},{6,5},{7,6},{8,11},{9,8},{10,9... | collective-permute-start | bytes 344072 | tf_op jit(solution)/shard_map/ppermute | solution.py:192
  83.6 2.6 %collective-permute-done.4.up = bf16[1,224,256]{2,1,0:T(8,128)(2,1)S(1)} collective-permute-done((bf16[1,224,256]{2,1,0:T(8,128)(2,1)S(1)}, bf16[1,224,256]{2,1,0:T(8,128)(2,1)S(1)}, u32[]{:S(2)}, u32[]{:S(2)}) %collective-permute-start.4) | collective-permute-done | bytes 114720 | tf_op jit(solution)/shard_map/ppermute | solution.py:192
  86.2 0.0 collective-permute-done.5.down
  86.2 0.0 collective-permute-done.12.x_last
  86.2 1.3 %shard_map.86 = (bf16[256,1024]{1,0:T(8,128)(2,1)}, bf16[1024,256]{1,0:T(8,128)(2,1)}) custom-call(bf16[8,224,256]{2,1,0:T(8,128)(2,1)S(1)} %shard_map.75.own.refs_0_, bf16[4,224,256]{2,1,0:T(8,128)(2,1)S(1)} %collective-permute-done.refs_1_.x_late, bf16[2,224,256]{2,1,0:T(8,128)(2,1)S(1)} %collective-permute-done.2.refs_2_.below, ...), custom_call_target="tpu_custom_call" | custom-call | bytes 1 | tf_op jit(solution)/shard_map/pallas_call | solution.py:161
  (6 shorter events, 0.1 us)
Async XLA Ops:
  0.0 9.9 %copy-start = (f32[1024]{0:T(1024)S(1)}, f32[1024]{0:T(1024)}, u32[]{:S(2)}) copy-start(f32[1024]{0:T(1024)} %param.11) | copy-start | bytes 12292
  2.7 25.2 %all-to-all-start = ((bf16[16,128,256]{2,1,0:T(8,128)(2,1)}), bf16[16,128,256]{2,1,0:T(8,128)(2,1)S(1)}, u32[]{:S(2)}, u32[]{:S(2)}) async-start(bf16[16,128,256]{2,1,0:T(8,128)(2,1)} %prepare.1), calls=%async_computation | async-start | bytes 2097152 | tf_op jit(solution)/shard_map/all_to_all | solution.py:229
  10.0 1.0 %copy-start.2 = (bf16[256,1024]{1,0:T(8,128)(2,1)S(1)}, bf16[256,1024]{1,0:T(8,128)(2,1)}, u32[]{:S(2)}) copy-start(bf16[256,1024]{1,0:T(8,128)(2,1)} %gate) | copy-start | bytes 1572868
  27.9 1.2 %copy-start.1 = (bf16[1024,512]{1,0:T(8,128)(2,1)S(1)}, bf16[1024,512]{1,0:T(8,128)(2,1)}, u32[]{:S(2)}) copy-start(bf16[1024,512]{1,0:T(8,128)(2,1)} %constant.14.clone.table_far) | copy-start | bytes 3145732
  51.6 16.8 %collective-permute-start.1 = (bf16[4,224,256]{2,1,0:T(8,128)(2,1)S(1)}, bf16[4,224,256]{2,1,0:T(8,128)(2,1)S(1)}, u32[]{:S(2)}, u32[]{:S(2)}) collective-permute-start(bf16[4,224,256]{2,1,0:T(8,128)(2,1)S(1)} %shard_map.77), channel_id=1, source_target_pairs={{0,4},{1,5},{2,6},{3,7},{4,0},{5,1},{6,2},{7,3},{8,12},{9,13},{10,... | collective-permute-start | bytes 1376264 | tf_op jit(solution)/shard_map/ppermute | solution.py:197
  52.3 12.0 %collective-permute-start.8 = (bf16[2,288,256]{2,1,0:T(8,128)(2,1)S(1)}, bf16[2,288,256]{2,1,0:T(8,128)(2,1)S(1)}, u32[]{:S(2)}, u32[]{:S(2)}) collective-permute-start(bf16[2,288,256]{2,1,0:T(8,128)(2,1)S(1)} %get-tuple-element.34), channel_id=1, source_target_pairs={{0,1},{1,2},{2,3},{3,0},{4,5},{5,6},{6,7},{7,4},{8,9},{9,10},{10,1... | collective-permute-start | bytes 884744 | tf_op jit(solution)/shard_map/ppermute | solution.py:192
  54.2 10.2 %collective-permute-start.10 = (bf16[2,288,256]{2,1,0:T(8,128)(2,1)S(1)}, bf16[2,288,256]{2,1,0:T(8,128)(2,1)S(1)}, u32[]{:S(2)}, u32[]{:S(2)}) collective-permute-start(bf16[2,288,256]{2,1,0:T(8,128)(2,1)S(1)} %get-tuple-element.35), channel_id=1, source_target_pairs={{0,3},{1,0},{2,1},{3,2},{4,7},{5,4},{6,5},{7,6},{8,11},{9,8},{10,9... | collective-permute-start | bytes 884744 | tf_op jit(solution)/shard_map/ppermute | solution.py:192
  57.1 14.0 %collective-permute-start.6 = (bf16[2,288,256]{2,1,0:T(8,128)(2,1)S(1)}, bf16[2,288,256]{2,1,0:T(8,128)(2,1)S(1)}, u32[]{:S(2)}, u32[]{:S(2)}) collective-permute-start(bf16[2,288,256]{2,1,0:T(8,128)(2,1)S(1)} %get-tuple-element.32), channel_id=1, source_target_pairs={{0,1},{1,2},{2,3},{3,0},{4,5},{5,6},{6,7},{7,4},{8,9},{9,10},{10,1... | collective-permute-start | bytes 884744 | tf_op jit(solution)/shard_map/ppermute | solution.py:192
  57.2 14.0 %collective-permute-start.7 = (bf16[2,288,256]{2,1,0:T(8,128)(2,1)S(1)}, bf16[2,288,256]{2,1,0:T(8,128)(2,1)S(1)}, u32[]{:S(2)}, u32[]{:S(2)}) collective-permute-start(bf16[2,288,256]{2,1,0:T(8,128)(2,1)S(1)} %get-tuple-element.33), channel_id=1, source_target_pairs={{0,3},{1,0},{2,1},{3,2},{4,7},{5,4},{6,5},{7,6},{8,11},{9,8},{10,9... | collective-permute-start | bytes 884744 | tf_op jit(solution)/shard_map/ppermute | solution.py:192
  64.3 12.6 %collective-permute-start.9 = (bf16[2,288,256]{2,1,0:T(8,128)(2,1)S(1)}, bf16[2,288,256]{2,1,0:T(8,128)(2,1)S(1)}, u32[]{:S(2)}, u32[]{:S(2)}) collective-permute-start(bf16[2,288,256]{2,1,0:T(8,128)(2,1)S(1)} %shard_map.83), channel_id=1, source_target_pairs={{0,1},{1,2},{2,3},{3,0},{4,5},{5,6},{6,7},{7,4},{8,9},{9,10},{10,1... | collective-permute-start | bytes 884744 | tf_op jit(solution)/shard_map/ppermute | solution.py:192
  64.5 12.4 %collective-permute-start.11 = (bf16[2,288,256]{2,1,0:T(8,128)(2,1)S(1)}, bf16[2,288,256]{2,1,0:T(8,128)(2,1)S(1)}, u32[]{:S(2)}, u32[]{:S(2)}) collective-permute-start(bf16[2,288,256]{2,1,0:T(8,128)(2,1)S(1)} %shard_map.84), channel_id=1, source_target_pairs={{0,3},{1,0},{2,1},{3,2},{4,7},{5,4},{6,5},{7,6},{8,11},{9,8},{10,9... | collective-permute-start | bytes 884744 | tf_op jit(solution)/shard_map/ppermute | solution.py:192
  68.4 10.0 %collective-permute-start = (bf16[4,224,256]{2,1,0:T(8,128)(2,1)S(1)}, bf16[4,224,256]{2,1,0:T(8,128)(2,1)S(1)}, u32[]{:S(2)}, u32[]{:S(2)}) collective-permute-start(bf16[4,224,256]{2,1,0:T(8,128)(2,1)S(1)} %shard_map.76), channel_id=1, source_target_pairs={{0,4},{1,5},{2,6},{3,7},{4,0},{5,1},{6,2},{7,3},{8,12},{9,13},{10,... | collective-permute-start | bytes 1376264 | tf_op jit(solution)/shard_map/ppermute | solution.py:197
  71.1 9.0 %collective-permute-start.2 = (bf16[2,224,256]{2,1,0:T(8,128)(2,1)S(1)}, bf16[2,224,256]{2,1,0:T(8,128)(2,1)S(1)}, u32[]{:S(2)}, u32[]{:S(2)}) collective-permute-start(bf16[2,224,256]{2,1,0:T(8,128)(2,1)S(1)} %get-tuple-element.30), channel_id=1, source_target_pairs={{0,1},{1,2},{2,3},{3,0},{4,5},{5,6},{6,7},{7,4},{8,9},{9,10},{10,1... | collective-permute-start | bytes 688136 | tf_op jit(solution)/shard_map/ppermute | solution.py:192
  71.2 9.2 %collective-permute-start.3 = (bf16[2,224,256]{2,1,0:T(8,128)(2,1)S(1)}, bf16[2,224,256]{2,1,0:T(8,128)(2,1)S(1)}, u32[]{:S(2)}, u32[]{:S(2)}) collective-permute-start(bf16[2,224,256]{2,1,0:T(8,128)(2,1)S(1)} %get-tuple-element.31), channel_id=1, source_target_pairs={{0,3},{1,0},{2,1},{3,2},{4,7},{5,4},{6,5},{7,6},{8,11},{9,8},{10,9... | collective-permute-start | bytes 688136 | tf_op jit(solution)/shard_map/ppermute | solution.py:192
  77.0 9.2 %collective-permute-start.12 = (bf16[576,256]{1,0:T(8,128)(2,1)S(1)}, bf16[576,256]{1,0:T(8,128)(2,1)S(1)}, u32[]{:S(2)}, u32[]{:S(2)}) collective-permute-start(bf16[576,256]{1,0:T(8,128)(2,1)S(1)} %shard_map.85), channel_id=1, source_target_pairs={{0,4},{1,5},{2,6},{3,7},{4,0},{5,1},{6,2},{7,3},{8,12},{9,13},{10,... | collective-permute-start | bytes 884744 | tf_op jit(solution)/shard_map/ppermute | solution.py:197
  80.2 6.1 %collective-permute-start.4 = (bf16[1,224,256]{2,1,0:T(8,128)(2,1)S(1)}, bf16[1,224,256]{2,1,0:T(8,128)(2,1)S(1)}, u32[]{:S(2)}, u32[]{:S(2)}) collective-permute-start(bf16[1,224,256]{2,1,0:T(8,128)(2,1)S(1)} %shard_map.79), channel_id=1, source_target_pairs={{0,1},{1,2},{2,3},{3,0},{4,5},{5,6},{6,7},{7,4},{8,9},{9,10},{10,1... | collective-permute-start | bytes 344072 | tf_op jit(solution)/shard_map/ppermute | solution.py:192
  80.4 5.8 %collective-permute-start.5 = (bf16[1,224,256]{2,1,0:T(8,128)(2,1)S(1)}, bf16[1,224,256]{2,1,0:T(8,128)(2,1)S(1)}, u32[]{:S(2)}, u32[]{:S(2)}) collective-permute-start(bf16[1,224,256]{2,1,0:T(8,128)(2,1)S(1)} %shard_map.80), channel_id=1, source_target_pairs={{0,3},{1,0},{2,1},{3,2},{4,7},{5,4},{6,5},{7,6},{8,11},{9,8},{10,9... | collective-permute-start | bytes 344072 | tf_op jit(solution)/shard_map/ppermute | solution.py:192

commit v6 on v5

--- a/solution.py
+++ b/solution.py
@@ -1,3 +1,5 @@
+import functools
+
 import numpy as np
 
 import jax
@@ -25,10 +27,11 @@
     return np.concatenate([high, low, np.concatenate(inverse, axis=1).astype(BF16)], axis=0)
 
 
-def prepare_kernel(in_gate, signal, taps, packed, gate_buf, signal_buf, taps_buf, sems):
+def prepare_kernel(in_gate, signal, taps, packed, gate_buf, signal_buf, taps_buf, packed_buf, sems, out_sems):
     parts, both, tokens = packed.shape
     half = both // 2
     steps, wide = gate_buf.shape[0], gate_buf.shape[2]
+    count = wide // half
     copies = [
         [
             pltpu.make_async_copy(source.at[:, i * wide : (i + 1) * wide], buf.at[i], sems.at[i, j])
@@ -39,121 +42,146 @@
     for step in copies:
         for copy in step:
             copy.start()
-    count = wide // half
+    results = []
     for i, step in enumerate(copies):
         for copy in step:
             copy.wait()
         gated = (gate_buf[i].astype(F32) * signal_buf[i].astype(F32)).astype(BF16)
-        packed[i * count : (i + 1) * count, :half] = gated.T.reshape(count, half, tokens)
-        packed[i * count : (i + 1) * count, half:] = taps_buf[i].T.reshape(count, half, tokens)
+        places = slice(i * count, (i + 1) * count)
+        packed_buf[places, :half] = gated.T.reshape(count, half, tokens)
+        packed_buf[places, half:] = taps_buf[i].T.reshape(count, half, tokens)
+        results.append(pltpu.make_async_copy(packed_buf.at[places], packed.at[places], out_sems.at[i]))
+        results[-1].start()
+    for copy in results:
+        copy.wait()
 
 
 def prepare(in_gate, signal, taps, parts):
     tokens, channels = in_gate.shape
     steps = 4
     wide = channels // steps
+    packed = jax.ShapeDtypeStruct((parts, 2 * channels // parts, tokens), BF16)
     return pl.pallas_call(
         prepare_kernel,
         in_specs=[pl.BlockSpec(memory_space=pltpu.HBM)] * 3,
-        out_specs=pl.BlockSpec(memory_space=pltpu.VMEM),
-        out_shape=jax.ShapeDtypeStruct((parts, 2 * channels // parts, tokens), BF16),
-        scratch_shapes=[pltpu.VMEM((steps, tokens, wide), BF16)] * 3 + [pltpu.SemaphoreType.DMA((steps, 3))],
+        out_specs=pl.BlockSpec(memory_space=pltpu.HBM),
+        out_shape=packed,
+        scratch_shapes=[pltpu.VMEM((steps, tokens, wide), BF16)] * 3
+        + [pltpu.VMEM(packed.shape, BF16), pltpu.SemaphoreType.DMA((steps, 3)), pltpu.SemaphoreType.DMA((steps,))],
         compiler_params=pltpu.CompilerParams(vmem_limit_bytes=60 * 2**20),
         name="prepare",
     )(in_gate, signal, taps)
 
 
-def conv_kernel(
-    packed, skip, table_far, weight_far, out, weight, table, g_spec, p_spec, acc_high, acc_low, sems
-):
-    copies = [
-        pltpu.make_async_copy(source, target, sems.at[i])
-        for i, (source, target) in enumerate(((table_far, table), (weight_far, weight)))
-    ]
-    for copy in copies:
-        copy.start()
-    copies[0].wait()
+TILE = 16
+REACH = 4
+LANES = 128
+
+
+def conv_kernel(packed, skip, table, out, *scratch):
+    g_specs, p_specs, highs, lows = scratch[:2], scratch[2:4], scratch[4:6], scratch[6:8]
     blocks, both, n = packed.shape
     ch = both // 2
+    tiles, rows = ch // TILE, blocks * TILE
+    real, imag = slice(0, n), slice(n, 2 * n)
     lane = lax.broadcasted_iota(jnp.int32, (1, n), 1)
     sign = jnp.where(lane % 2 == 0, 1.0, -1.0).astype(F32)
 
-    def transform(rows):
-        return jnp.dot(rows, table[:n], preferred_element_type=F32) + jnp.dot(
-            rows, table[n : 2 * n], preferred_element_type=F32
-        )
-
-    def inverse(spectra, part):
-        return jnp.dot(spectra, table[2 * n :, part * n : (part + 1) * n], preferred_element_type=F32)
-
-    group = 4
-    tail = None
-    for b in range(0, blocks, group):
-        rows = packed[b : b + group]
-        g_spec[b : b + group] = transform(rows[:, :ch].reshape(group * ch, n)).reshape(group, ch, 2 * n)
-        h = transform(rows[:, ch:].reshape(group * ch, n)).reshape(group, ch, 2 * n)
-        for j in range(group):
-            if tail is None:
-                p_spec[b + j] = h[j]
-            else:
-                p_spec[b + j, :, :n] = h[j, :, :n] - sign * tail[:, n:]
-                p_spec[b + j, :, n:] = h[j, :, n:] + sign * tail[:, :n]
-            tail = h[j]
-
-    lanes, subs = 128, 16
-
-    def products(step, carry):
-        rows = pl.ds(pl.multiple_of(step * subs, subs), subs)
-        for f in range(0, n, lanes):
-            re, im = slice(f, f + lanes), slice(n + f, n + f + lanes)
-            for i in range(blocks):
-                acc_re = acc_im = None
-                for a in range(i + 1):
-                    gr, gi = g_spec[a, rows, re], g_spec[a, rows, im]
-                    pr, pi = p_spec[i - a, rows, re], p_spec[i - a, rows, im]
-                    t_re, t_im = gr * pr - gi * pi, gr * pi + gi * pr
-                    acc_re = t_re if acc_re is None else acc_re + t_re
-                    acc_im = t_im if acc_im is None else acc_im + t_im
-                for value, cols in ((acc_re, re), (acc_im, im)):
-                    high = value.astype(BF16)
-                    acc_high[i, rows, cols] = high
-                    acc_low[i, rows, cols] = (value - high.astype(F32)).astype(BF16)
-        return carry
-
-    lax.fori_loop(0, ch // subs, products, 0)
-
-    for b in range(0, blocks, group):
-        high = acc_high[b : b + group].reshape(group * ch, 2 * n)
-        low = acc_low[b : b + group].reshape(group * ch, 2 * n)
-        conv = (inverse(high, 0) + inverse(low, 0) + inverse(high, 1)).reshape(group, ch, n)
-        gated = packed[b : b + group, :ch, :].astype(F32)
-        out[b : b + group] = (conv + skip[...][None] * gated).astype(BF16)
-    copies[1].wait()
-
-
-def convolve(packed, skip, table, weight):
+    def spectrum(first, columns):
+        samples = packed[:, first : first + TILE, :].reshape(rows, n)
+        high = jnp.dot(samples, table[:n, columns], preferred_element_type=F32)
+        low = jnp.dot(samples, table[n : 2 * n, columns], preferred_element_type=F32)
+        return (high + low).reshape(blocks, TILE, n)
+
+    def spectra(tile):
+        g_spec, p_spec = g_specs[tile % 2], p_specs[tile % 2]
+
+        def gated(columns):
+            def task():
+                g_spec[:, :, columns] = spectrum(tile * TILE, columns)
+
+            return task
+
+        def pairs():
+            re, im = (spectrum(ch + tile * TILE, columns) for columns in (real, imag))
+            p_spec[0, :, real], p_spec[0, :, imag] = re[0], im[0]
+            for k in range(1, blocks):
+                p_spec[k, :, real] = re[k] - sign * im[k - 1]
+                p_spec[k, :, imag] = im[k] + sign * re[k - 1]
+
+        return [gated(real), gated(imag), pairs]
+
+    def products(tile):
+        g_spec, p_spec = g_specs[tile % 2], p_specs[tile % 2]
+        high, low = highs[tile % 2], lows[tile % 2]
+
+        def task(lanes, start):
+            re, im = slice(lanes, lanes + LANES), slice(n + lanes, n + lanes + LANES)
+            total, window = [None] * REACH, [None] * REACH
+            for a in range(start + REACH):
+                gr, gi = g_spec[a, :, re], g_spec[a, :, im]
+                for r in reversed(range(REACH)):
+                    lag = start + r - a
+                    if lag < 0:
+                        continue
+                    fresh = a == 0 or r == 0
+                    window[r] = (p_spec[lag, :, re], p_spec[lag, :, im]) if fresh else window[r - 1]
+                    pr, pi = window[r]
+                    term = (gr * pr - gi * pi, gr * pi + gi * pr)
+                    total[r] = term if a == 0 else (total[r][0] + term[0], total[r][1] + term[1])
+            for r in range(REACH):
+                for value, columns in zip(total[r], (re, im), strict=True):
+                    rounded = value.astype(BF16)
+                    high[start + r, :, columns] = rounded
+                    low[start + r, :, columns] = (value - rounded.astype(F32)).astype(BF16)
+
+        return [
+            functools.partial(task, lanes, start)
+            for lanes in range(0, n, LANES)
+            for start in range(0, blocks, REACH)
+        ]
+
+    def inverse(tile):
+        def task():
+            high = highs[tile % 2][...].reshape(rows, 2 * n)
+            low = lows[tile % 2][...].reshape(rows, 2 * n)
+            back, back_low = table[2 * n :, :n], table[2 * n :, n:]
+            conv = (
+                jnp.dot(high, back, preferred_element_type=F32)
+                + jnp.dot(low, back, preferred_element_type=F32)
+                + jnp.dot(high, back_low, preferred_element_type=F32)
+            ).reshape(blocks, TILE, n)
+            channels = slice(tile * TILE, (tile + 1) * TILE)
+            gated = packed[:, channels, :].astype(F32)
+            out[:, channels, :] = (conv + skip[channels][None] * gated).astype(BF16)
+
+        return [task]
+
+    for step in range(tiles + 2):
+        matrix = inverse(step - 2) if step >= 2 else []
+        matrix += spectra(step) if step < tiles else []
+        vector = products(step - 1) if 0 <= step - 1 < tiles else []
+        share = max(1, len(vector) // max(1, len(matrix)))
+        while matrix or vector:
+            for task in matrix[:1] + vector[:share]:
+                task()
+            matrix, vector = matrix[1:], vector[share:]
+
+
+def convolve(packed, skip, table):
     blocks, both, n = packed.shape
     ch = both // 2
-    near, far = pl.BlockSpec(memory_space=pltpu.VMEM), pl.BlockSpec(memory_space=pltpu.HBM)
+    near = pl.BlockSpec(memory_space=pltpu.VMEM)
     return pl.pallas_call(
         conv_kernel,
-        in_specs=[near, near, far, far],
-        out_specs=[near] * 2,
-        out_shape=[
-            jax.ShapeDtypeStruct((blocks, ch, n), BF16),
-            jax.ShapeDtypeStruct(weight.shape, BF16),
-        ],
-        scratch_shapes=[
-            pltpu.VMEM(table.shape, BF16),
-            pltpu.VMEM((blocks, ch, 2 * n), F32),
-            pltpu.VMEM((blocks, ch, 2 * n), F32),
-            pltpu.VMEM((blocks, ch, 2 * n), BF16),
-            pltpu.VMEM((blocks, ch, 2 * n), BF16),
-            pltpu.SemaphoreType.DMA((2,)),
-        ],
-        compiler_params=pltpu.CompilerParams(vmem_limit_bytes=28 * 2**20),
+        in_specs=[near] * 3,
+        out_specs=near,
+        out_shape=jax.ShapeDtypeStruct((blocks, ch, n), BF16),
+        scratch_shapes=[pltpu.VMEM((blocks, TILE, 2 * n), F32)] * 4 + [pltpu.VMEM((blocks, TILE, 2 * n), BF16)] * 4,
+        compiler_params=pltpu.CompilerParams(vmem_limit_bytes=8 * 2**20),
+        cost_estimate=pl.CostEstimate(flops=5 * 10**9, bytes_accessed=1, transcendentals=0),
         name="convolve",
-    )(packed, skip, table, weight)
+    )(packed, skip, table)
 
 
 def on_chip(body, shapes, *args, flops=0):
@@ -222,14 +250,15 @@
     per_part = channels // parts
     packed, out_gate = lax.optimization_barrier((prepare(in_gate, signal, filter_taps, parts), out_gate))
 
-    def turn(gate, out):
-        out[...] = gate[...].T
-
-    (gate_t,) = on_chip(turn, [(channels, tokens)], out_gate)
-    packed, gate_t = lax.optimization_barrier((lax.all_to_all(packed, "seq", 0, 0), gate_t))
+    def stage(gate, table, gate_t, staged):
+        gate_t[...] = gate[...].T
+        staged[...] = table[...]
+
+    table = jnp.asarray(transform_table(tokens))
+    gate_t, table = on_chip(stage, [(channels, tokens), table.shape], out_gate, table)
+    packed, gate_t, table = lax.optimization_barrier((lax.all_to_all(packed, "seq", 0, 0), gate_t, table))
     skip = lax.dynamic_slice_in_dim(skip_gain, lax.axis_index("seq") * per_part, per_part, 0)
-    table = jnp.asarray(transform_table(tokens))
-    conv, out_proj = convolve(packed, skip[:, None], table, out_proj)
+    conv = convolve(packed, skip[:, None], table)
     conv = lax.all_to_all(conv, "seq", 0, 0).reshape(channels, tokens)
     mixed = (gate_t.astype(F32) * conv.astype(F32)).astype(BF16)
 
@@ -244,11 +273,14 @@
         return [(flip, step, 2 * half_a + h * half_b) for step, h in places for flip in (0, 1)]
 
     early, late = ((2, 0), (1, 1), (2, 1), (3, 0)), ((1, 0), (3, 1), (0, 0), (0, 1))
-    run = lambda rows, *groups: project(out_proj, mixed, groups, rows, chunk)
+    def run(rows, *groups):
+        return project(out_proj, mixed, groups, rows, chunk)
+
     relay_up, relay_down = run(half_b, rows_b((2, 0)), rows_b((2, 1)))
     relay_up, relay_down, mixed = lax.optimization_barrier((relay_up, relay_down, mixed))
     relayed_up, relayed_down = to_z(relay_up, 1), to_z(relay_down, -1)
     (x_early,) = run(half_a, rows_a(1, *early))
+    x_early, mixed = lax.optimization_barrier((x_early, mixed))
     x_early = to_x(x_early)
     direct_up, direct_down = run(half_b, rows_b((1, 1)), rows_b((3, 0)))
     b_below, b_above = to_z(direct_up, 1), to_z(direct_down, -1)

time: 87.9 us -> 85.4 us (0.972)
  waiting for transfers between devices: 25.8 us -> 24.4 us
  Pallas kernels: 15.8 us -> 14.4 us
    all_to_all x1, waiting for transfers between devices: 16.6 us -> 15.3 us  [shards(): lax.all_to_all(packed, 'seq', 0, 0)]
    pallas_call x1, Pallas kernels: 5.86 us -> 4.75 us  [convolve(): pl.pallas_call(conv_kernel, in_specs=[near] * 3, out_specs=near, out_shap...]
    unnamed x6 -> x8, local copies, waits for them, and re-layouts: 2.27 us -> 2.27 us
where the time goes in v6:
time: 85.4 us; the launch traced here: 85 us
  starting transfers between devices  28.3 us (33%)
  waiting for transfers between devices  24.4 us (29%)
  blocking collectives  15.1 us (18%)
  Pallas kernels  14.4 us (17%)
  local copies, waits for them, and re-layouts  2.45 us (3%)
    ppermute x10, starting transfers between devices, to_z(): lax.ppermute(block, 'chan', [(i, i // Z * Z + (i + step) % Z) for i in ra...  17.4 us
    all_to_all x1, waiting for transfers between devices, shards(): lax.all_to_all(packed, 'seq', 0, 0)  15.3 us
    all_to_all x1, blocking collectives, shards(): conv = lax.all_to_all(conv, 'seq', 0, 0).reshape(channels, tokens)  15.1 us
    ppermute x10, waiting for transfers between devices, to_z(): lax.ppermute(block, 'chan', [(i, i // Z * Z + (i + step) % Z) for i in ra...  9.02 us
    pallas_call x14, Pallas kernels, on_chip(): pl.pallas_call(body, in_specs=[in_vmem] * len(args), out_specs=[in_vmem]...  7.24 us
    all_to_all x1, starting transfers between devices, shards(): lax.all_to_all(packed, 'seq', 0, 0)  7.13 us
    pallas_call x1, Pallas kernels, convolve(): pl.pallas_call(conv_kernel, in_specs=[near] * 3, out_specs=near, out_shap...  4.75 us
    ppermute x3, starting transfers between devices, to_x(): return lax.ppermute(block, 'chan', [(i, (i + Z) % n) for i in range(n)])  3.81 us
  transfers between devices with their start and end apart: 14, of which 5 were waited for; matrix products, arithmetic and copies ran while one was open for 0% of the time, Pallas kernels for 5%

profile of v6, /device:TPU:0, one launch (start us, length us, event | category | flops | bytes accessed | tf_op | source)
XLA Modules:
  0.0 85.0 jit_solution(2589889564114552252)
XLA Ops:
  0.0 2.4 %prepare.1 = bf16[16,128,256]{2,1,0:T(8,128)(2,1)} custom-call(bf16[256,1024]{1,0:T(8,128)(2,1)} %in_gate.1, bf16[256,1024]{1,0:T(8,128)(2,1)} %signal.1, bf16[256,1024]{1,0:T(8,128)(2,1)} %taps.1), custom_call_target="tpu_custom_call" | custom-call | tf_op jit(solution)/shard_map/prepare/pallas_call | solution.py:64
  2.5 7.1 %all-to-all-start = ((bf16[16,128,256]{2,1,0:T(8,128)(2,1)}), bf16[16,128,256]{2,1,0:T(8,128)(2,1)S(1)}, u32[]{:S(2)}, u32[]{:S(2)}) async-start(bf16[16,128,256]{2,1,0:T(8,128)(2,1)} %prepare.1), calls=%async_computation | async-start | bytes 2097152 | tf_op jit(solution)/shard_map/all_to_all | solution.py:259
  9.6 0.1 dynamic-slice_bitcast_fusion
  9.7 0.1 copy.8.skip
  9.8 1.2 %copy-done.2 = bf16[1024,512]{1,0:T(8,128)(2,1)S(1)} copy-done((bf16[1024,512]{1,0:T(8,128)(2,1)S(1)}, bf16[1024,512]{1,0:T(8,128)(2,1)}, u32[]{:S(2)}) %copy-start.2) | copy-done | bytes 1048600
  11.0 1.0 %copy-done.3 = bf16[256,1024]{1,0:T(8,128)(2,1)S(1)} copy-done((bf16[256,1024]{1,0:T(8,128)(2,1)S(1)}, bf16[256,1024]{1,0:T(8,128)(2,1)}, u32[]{:S(2)}) %copy-start.3) | copy-done | bytes 524312
  12.1 0.2 shard_map.73
  12.3 15.3 %all-to-all-done.packed = bf16[16,128,256]{2,1,0:T(8,128)(2,1)S(1)} async-done(((bf16[16,128,256]{2,1,0:T(8,128)(2,1)}), bf16[16,128,256]{2,1,0:T(8,128)(2,1)S(1)}, u32[]{:S(2)}, u32[]{:S(2)}) %all-to-all-start) | async-done | bytes 1048608 | tf_op jit(solution)/shard_map/all_to_all | solution.py:259
  27.6 4.7 %convolve.1 = bf16[16,64,256]{2,1,0:T(8,128)(2,1)S(1)} custom-call(bf16[16,128,256]{2,1,0:T(8,128)(2,1)S(1)} %all-to-all-done.packed, f32[64,1]{1,0:T(8,128)S(1)} %copy.8.skip, bf16[1024,512]{1,0:T(8,128)(2,1)S(1)} %get-tuple-element.30.table), custom_call_target="tpu_custom_call" | custom-call | flops 5000000000 | bytes 1 | tf_op jit(solution)/shard_map/convolve/pallas_call | solution.py:175
  32.4 15.1 %all_to_all.10 = bf16[16,64,256]{2,1,0:T(8,128)(2,1)S(1)} all-to-all(bf16[16,64,256]{2,1,0:T(8,128)(2,1)S(1)} %convolve.1), channel_id=1, replica_groups=mesh['seq'=16,'chan'=8] {'seq'}, dimensions={0} | all-to-all | bytes 1048576 | tf_op jit(solution)/shard_map/all_to_all | solution.py:262
  47.5 0.2 fusion.mixed
  47.7 0.0 copy-done.1
  47.7 0.8 shard_map.74
  48.4 0.6 shard_map.75
  49.1 0.7 collective-permute-start.1
  49.8 1.9 %collective-permute-start.8 = (bf16[2,288,256]{2,1,0:T(8,128)(2,1)S(1)}, bf16[2,288,256]{2,1,0:T(8,128)(2,1)S(1)}, u32[]{:S(2)}, u32[]{:S(2)}) collective-permute-start(bf16[2,288,256]{2,1,0:T(8,128)(2,1)S(1)} %get-tuple-element.40), channel_id=1, source_target_pairs={{0,1},{1,2},{2,3},{3,0},{4,5},{5,6},{6,7},{7,4},{8,9},{9,10},{10,1... | collective-permute-start | bytes 884744 | tf_op jit(solution)/shard_map/ppermute | solution.py:220
  51.7 2.1 %collective-permute-start.10 = (bf16[2,288,256]{2,1,0:T(8,128)(2,1)S(1)}, bf16[2,288,256]{2,1,0:T(8,128)(2,1)S(1)}, u32[]{:S(2)}, u32[]{:S(2)}) collective-permute-start(bf16[2,288,256]{2,1,0:T(8,128)(2,1)S(1)} %get-tuple-element.41), channel_id=1, source_target_pairs={{0,3},{1,0},{2,1},{3,2},{4,7},{5,4},{6,5},{7,6},{8,11},{9,8},{10,9... | collective-permute-start | bytes 884744 | tf_op jit(solution)/shard_map/ppermute | solution.py:220
  53.9 0.8 shard_map.82
  54.6 0.1 collective-permute-start.6
  54.7 3.2 %collective-permute-start.7 = (bf16[2,288,256]{2,1,0:T(8,128)(2,1)S(1)}, bf16[2,288,256]{2,1,0:T(8,128)(2,1)S(1)}, u32[]{:S(2)}, u32[]{:S(2)}) collective-permute-start(bf16[2,288,256]{2,1,0:T(8,128)(2,1)S(1)} %get-tuple-element.39), channel_id=1, source_target_pairs={{0,3},{1,0},{2,1},{3,2},{4,7},{5,4},{6,5},{7,6},{8,11},{9,8},{10,9... | collective-permute-start | bytes 884744 | tf_op jit(solution)/shard_map/ppermute | solution.py:220
  58.0 1.4 %shard_map.81.refs_0_.rest = bf16[8,288,256]{2,1,0:T(8,128)(2,1)S(1)} custom-call(bf16[8192,1024]{1,0:T(8,128)(2,1)S(1)} %copy-done.1, bf16[1024,256]{1,0:T(8,128)(2,1)S(1)} %fusion.mixed), custom_call_target="tpu_custom_call" | custom-call | flops 1207959552 | bytes 1 | tf_op jit(solution)/shard_map/pallas_call | solution.py:189
  59.3 2.4 %collective-permute-done.8.refs_1_ = bf16[2,288,256]{2,1,0:T(8,128)(2,1)S(1)} collective-permute-done((bf16[2,288,256]{2,1,0:T(8,128)(2,1)S(1)}, bf16[2,288,256]{2,1,0:T(8,128)(2,1)S(1)}, u32[]{:S(2)}, u32[]{:S(2)}) %collective-permute-start.8) | collective-permute-done | bytes 294944 | tf_op jit(solution)/shard_map/ppermute | solution.py:220
  61.8 0.1 shard_map.83
  61.9 0.1 collective-permute-start.9
  61.9 0.0 collective-permute-done.10.refs_1_
  61.9 0.1 shard_map.84
  62.0 3.3 %collective-permute-start.11 = (bf16[2,288,256]{2,1,0:T(8,128)(2,1)S(1)}, bf16[2,288,256]{2,1,0:T(8,128)(2,1)S(1)}, u32[]{:S(2)}, u32[]{:S(2)}) collective-permute-start(bf16[2,288,256]{2,1,0:T(8,128)(2,1)S(1)} %shard_map.84), channel_id=1, source_target_pairs={{0,3},{1,0},{2,1},{3,2},{4,7},{5,4},{6,5},{7,6},{8,11},{9,8},{10,9... | collective-permute-start | bytes 884744 | tf_op jit(solution)/shard_map/ppermute | solution.py:220
  65.3 0.6 shard_map.77
  65.9 0.0 collective-permute-done.1.arrived
  66.0 1.6 %collective-permute-start = (bf16[4,224,256]{2,1,0:T(8,128)(2,1)S(1)}, bf16[4,224,256]{2,1,0:T(8,128)(2,1)S(1)}, u32[]{:S(2)}, u32[]{:S(2)}) collective-permute-start(bf16[4,224,256]{2,1,0:T(8,128)(2,1)S(1)} %shard_map.77), channel_id=1, source_target_pairs={{0,4},{1,5},{2,6},{3,7},{4,0},{5,1},{6,2},{7,3},{8,12},{9,13},{10,... | collective-permute-start | bytes 1376264 | tf_op jit(solution)/shard_map/ppermute | solution.py:225
  67.6 1.1 %shard_map.76.own.refs_0_ = bf16[8,224,256]{2,1,0:T(8,128)(2,1)S(1)} custom-call(bf16[8192,1024]{1,0:T(8,128)(2,1)S(1)} %copy-done.1, bf16[1024,256]{1,0:T(8,128)(2,1)S(1)} %fusion.mixed), custom_call_target="tpu_custom_call" | custom-call | flops 939524096 | bytes 1 | tf_op jit(solution)/shard_map/pallas_call | solution.py:189
  68.7 0.1 shard_map.78
  68.8 0.0 collective-permute-done.6.refs_1_.b_below
  68.8 0.1 collective-permute-start.2
  68.9 0.0 collective-permute-done.7.refs_2_.b_above
  68.9 3.2 %collective-permute-start.3 = (bf16[2,224,256]{2,1,0:T(8,128)(2,1)S(1)}, bf16[2,224,256]{2,1,0:T(8,128)(2,1)S(1)}, u32[]{:S(2)}, u32[]{:S(2)}) collective-permute-start(bf16[2,224,256]{2,1,0:T(8,128)(2,1)S(1)} %get-tuple-element.37), channel_id=1, source_target_pairs={{0,3},{1,0},{2,1},{3,2},{4,7},{5,4},{6,5},{7,6},{8,11},{9,8},{10,9... | collective-permute-start | bytes 688136 | tf_op jit(solution)/shard_map/ppermute | solution.py:220
  72.2 2.3 %collective-permute-done.9.refs_3_.b_up = bf16[2,288,256]{2,1,0:T(8,128)(2,1)S(1)} collective-permute-done((bf16[2,288,256]{2,1,0:T(8,128)(2,1)S(1)}, bf16[2,288,256]{2,1,0:T(8,128)(2,1)S(1)}, u32[]{:S(2)}, u32[]{:S(2)}) %collective-permute-start.9) | collective-permute-done | bytes 294944 | tf_op jit(solution)/shard_map/ppermute | solution.py:220
  74.4 0.0 collective-permute-done.11.refs_4_.b_down
  74.4 0.1 shard_map.85
  74.5 1.5 %collective-permute-start.12 = (bf16[576,256]{1,0:T(8,128)(2,1)S(1)}, bf16[576,256]{1,0:T(8,128)(2,1)S(1)}, u32[]{:S(2)}, u32[]{:S(2)}) collective-permute-start(bf16[576,256]{1,0:T(8,128)(2,1)S(1)} %shard_map.85), channel_id=1, source_target_pairs={{0,4},{1,5},{2,6},{3,7},{4,0},{5,1},{6,2},{7,3},{8,12},{9,13},{10,... | collective-permute-start | bytes 884744 | tf_op jit(solution)/shard_map/ppermute | solution.py:225
  76.0 0.0 collective-permute-done.refs_1_.x_late
  76.0 1.7 %collective-permute-done.2.refs_2_.below = bf16[2,224,256]{2,1,0:T(8,128)(2,1)S(1)} collective-permute-done((bf16[2,224,256]{2,1,0:T(8,128)(2,1)S(1)}, bf16[2,224,256]{2,1,0:T(8,128)(2,1)S(1)}, u32[]{:S(2)}, u32[]{:S(2)}) %collective-permute-start.2) | collective-permute-done | bytes 229408 | tf_op jit(solution)/shard_map/ppermute | solution.py:220
  77.7 0.2 collective-permute-start.4
  77.9 0.0 collective-permute-done.3.refs_2_.above
  78.0 3.1 %collective-permute-start.5 = (bf16[1,224,256]{2,1,0:T(8,128)(2,1)S(1)}, bf16[1,224,256]{2,1,0:T(8,128)(2,1)S(1)}, u32[]{:S(2)}, u32[]{:S(2)}) collective-permute-start(bf16[1,224,256]{2,1,0:T(8,128)(2,1)S(1)} %shard_map.80), channel_id=1, source_target_pairs={{0,3},{1,0},{2,1},{3,2},{4,7},{5,4},{6,5},{7,6},{8,11},{9,8},{10,9... | collective-permute-start | bytes 344072 | tf_op jit(solution)/shard_map/ppermute | solution.py:220
  81.1 2.6 %collective-permute-done.4.up = bf16[1,224,256]{2,1,0:T(8,128)(2,1)S(1)} collective-permute-done((bf16[1,224,256]{2,1,0:T(8,128)(2,1)S(1)}, bf16[1,224,256]{2,1,0:T(8,128)(2,1)S(1)}, u32[]{:S(2)}, u32[]{:S(2)}) %collective-permute-start.4) | collective-permute-done | bytes 114720 | tf_op jit(solution)/shard_map/ppermute | solution.py:220
  83.8 0.0 collective-permute-done.5.down
  83.8 1.3 %shard_map.86 = (bf16[256,1024]{1,0:T(8,128)(2,1)}, bf16[1024,256]{1,0:T(8,128)(2,1)}) custom-call(bf16[8,224,256]{2,1,0:T(8,128)(2,1)S(1)} %shard_map.76.own.refs_0_, bf16[4,224,256]{2,1,0:T(8,128)(2,1)S(1)} %collective-permute-done.refs_1_.x_late, bf16[2,224,256]{2,1,0:T(8,128)(2,1)S(1)} %collective-permute-done.2.refs_2_.below, ...), custom_call_target="tpu_custom_call" | custom-call | bytes 1 | tf_op jit(solution)/shard_map/pallas_call | solution.py:189
  (8 shorter events, 0.1 us)
Async XLA Ops:
  0.0 9.6 %copy-start = (f32[1024]{0:T(1024)S(1)}, f32[1024]{0:T(1024)}, u32[]{:S(2)}) copy-start(f32[1024]{0:T(1024)} %param.11) | copy-start | bytes 12292
  2.5 25.2 %all-to-all-start = ((bf16[16,128,256]{2,1,0:T(8,128)(2,1)}), bf16[16,128,256]{2,1,0:T(8,128)(2,1)S(1)}, u32[]{:S(2)}, u32[]{:S(2)}) async-start(bf16[16,128,256]{2,1,0:T(8,128)(2,1)} %prepare.1), calls=%async_computation | async-start | bytes 2097152 | tf_op jit(solution)/shard_map/all_to_all | solution.py:259
  9.8 1.2 %copy-start.2 = (bf16[1024,512]{1,0:T(8,128)(2,1)S(1)}, bf16[1024,512]{1,0:T(8,128)(2,1)}, u32[]{:S(2)}) copy-start(bf16[1024,512]{1,0:T(8,128)(2,1)} %constant.14.clone.table) | copy-start | bytes 3145732
  11.0 1.0 %copy-start.3 = (bf16[256,1024]{1,0:T(8,128)(2,1)S(1)}, bf16[256,1024]{1,0:T(8,128)(2,1)}, u32[]{:S(2)}) copy-start(bf16[256,1024]{1,0:T(8,128)(2,1)} %gate) | copy-start | bytes 1572868
  27.6 20.0 %copy-start.1 = (bf16[8192,1024]{1,0:T(8,128)(2,1)S(1)}, bf16[8192,1024]{1,0:T(8,128)(2,1)}, u32[]{:S(2)}) copy-start(bf16[8192,1024]{1,0:T(8,128)(2,1)} %weight.11) | copy-start | bytes 50331652
  49.1 16.9 %collective-permute-start.1 = (bf16[4,224,256]{2,1,0:T(8,128)(2,1)S(1)}, bf16[4,224,256]{2,1,0:T(8,128)(2,1)S(1)}, u32[]{:S(2)}, u32[]{:S(2)}) collective-permute-start(bf16[4,224,256]{2,1,0:T(8,128)(2,1)S(1)} %shard_map.75), channel_id=1, source_target_pairs={{0,4},{1,5},{2,6},{3,7},{4,0},{5,1},{6,2},{7,3},{8,12},{9,13},{10,... | collective-permute-start | bytes 1376264 | tf_op jit(solution)/shard_map/ppermute | solution.py:225
  49.8 12.0 %collective-permute-start.8 = (bf16[2,288,256]{2,1,0:T(8,128)(2,1)S(1)}, bf16[2,288,256]{2,1,0:T(8,128)(2,1)S(1)}, u32[]{:S(2)}, u32[]{:S(2)}) collective-permute-start(bf16[2,288,256]{2,1,0:T(8,128)(2,1)S(1)} %get-tuple-element.40), channel_id=1, source_target_pairs={{0,1},{1,2},{2,3},{3,0},{4,5},{5,6},{6,7},{7,4},{8,9},{9,10},{10,1... | collective-permute-start | bytes 884744 | tf_op jit(solution)/shard_map/ppermute | solution.py:220
  51.7 10.2 %collective-permute-start.10 = (bf16[2,288,256]{2,1,0:T(8,128)(2,1)S(1)}, bf16[2,288,256]{2,1,0:T(8,128)(2,1)S(1)}, u32[]{:S(2)}, u32[]{:S(2)}) collective-permute-start(bf16[2,288,256]{2,1,0:T(8,128)(2,1)S(1)} %get-tuple-element.41), channel_id=1, source_target_pairs={{0,3},{1,0},{2,1},{3,2},{4,7},{5,4},{6,5},{7,6},{8,11},{9,8},{10,9... | collective-permute-start | bytes 884744 | tf_op jit(solution)/shard_map/ppermute | solution.py:220
  54.6 14.2 %collective-permute-start.6 = (bf16[2,288,256]{2,1,0:T(8,128)(2,1)S(1)}, bf16[2,288,256]{2,1,0:T(8,128)(2,1)S(1)}, u32[]{:S(2)}, u32[]{:S(2)}) collective-permute-start(bf16[2,288,256]{2,1,0:T(8,128)(2,1)S(1)} %get-tuple-element.38), channel_id=1, source_target_pairs={{0,1},{1,2},{2,3},{3,0},{4,5},{5,6},{6,7},{7,4},{8,9},{9,10},{10,1... | collective-permute-start | bytes 884744 | tf_op jit(solution)/shard_map/ppermute | solution.py:220
  54.7 14.2 %collective-permute-start.7 = (bf16[2,288,256]{2,1,0:T(8,128)(2,1)S(1)}, bf16[2,288,256]{2,1,0:T(8,128)(2,1)S(1)}, u32[]{:S(2)}, u32[]{:S(2)}) collective-permute-start(bf16[2,288,256]{2,1,0:T(8,128)(2,1)S(1)} %get-tuple-element.39), channel_id=1, source_target_pairs={{0,3},{1,0},{2,1},{3,2},{4,7},{5,4},{6,5},{7,6},{8,11},{9,8},{10,9... | collective-permute-start | bytes 884744 | tf_op jit(solution)/shard_map/ppermute | solution.py:220
  61.9 12.6 %collective-permute-start.9 = (bf16[2,288,256]{2,1,0:T(8,128)(2,1)S(1)}, bf16[2,288,256]{2,1,0:T(8,128)(2,1)S(1)}, u32[]{:S(2)}, u32[]{:S(2)}) collective-permute-start(bf16[2,288,256]{2,1,0:T(8,128)(2,1)S(1)} %shard_map.83), channel_id=1, source_target_pairs={{0,1},{1,2},{2,3},{3,0},{4,5},{5,6},{6,7},{7,4},{8,9},{9,10},{10,1... | collective-permute-start | bytes 884744 | tf_op jit(solution)/shard_map/ppermute | solution.py:220
  62.0 12.4 %collective-permute-start.11 = (bf16[2,288,256]{2,1,0:T(8,128)(2,1)S(1)}, bf16[2,288,256]{2,1,0:T(8,128)(2,1)S(1)}, u32[]{:S(2)}, u32[]{:S(2)}) collective-permute-start(bf16[2,288,256]{2,1,0:T(8,128)(2,1)S(1)} %shard_map.84), channel_id=1, source_target_pairs={{0,3},{1,0},{2,1},{3,2},{4,7},{5,4},{6,5},{7,6},{8,11},{9,8},{10,9... | collective-permute-start | bytes 884744 | tf_op jit(solution)/shard_map/ppermute | solution.py:220
  66.0 10.0 %collective-permute-start = (bf16[4,224,256]{2,1,0:T(8,128)(2,1)S(1)}, bf16[4,224,256]{2,1,0:T(8,128)(2,1)S(1)}, u32[]{:S(2)}, u32[]{:S(2)}) collective-permute-start(bf16[4,224,256]{2,1,0:T(8,128)(2,1)S(1)} %shard_map.77), channel_id=1, source_target_pairs={{0,4},{1,5},{2,6},{3,7},{4,0},{5,1},{6,2},{7,3},{8,12},{9,13},{10,... | collective-permute-start | bytes 1376264 | tf_op jit(solution)/shard_map/ppermute | solution.py:225
  68.8 8.8 %collective-permute-start.2 = (bf16[2,224,256]{2,1,0:T(8,128)(2,1)S(1)}, bf16[2,224,256]{2,1,0:T(8,128)(2,1)S(1)}, u32[]{:S(2)}, u32[]{:S(2)}) collective-permute-start(bf16[2,224,256]{2,1,0:T(8,128)(2,1)S(1)} %get-tuple-element.36), channel_id=1, source_target_pairs={{0,1},{1,2},{2,3},{3,0},{4,5},{5,6},{6,7},{7,4},{8,9},{9,10},{10,1... | collective-permute-start | bytes 688136 | tf_op jit(solution)/shard_map/ppermute | solution.py:220
  68.9 9.0 %collective-permute-start.3 = (bf16[2,224,256]{2,1,0:T(8,128)(2,1)S(1)}, bf16[2,224,256]{2,1,0:T(8,128)(2,1)S(1)}, u32[]{:S(2)}, u32[]{:S(2)}) collective-permute-start(bf16[2,224,256]{2,1,0:T(8,128)(2,1)S(1)} %get-tuple-element.37), channel_id=1, source_target_pairs={{0,3},{1,0},{2,1},{3,2},{4,7},{5,4},{6,5},{7,6},{8,11},{9,8},{10,9... | collective-permute-start | bytes 688136 | tf_op jit(solution)/shard_map/ppermute | solution.py:220
  74.5 9.2 %collective-permute-start.12 = (bf16[576,256]{1,0:T(8,128)(2,1)S(1)}, bf16[576,256]{1,0:T(8,128)(2,1)S(1)}, u32[]{:S(2)}, u32[]{:S(2)}) collective-permute-start(bf16[576,256]{1,0:T(8,128)(2,1)S(1)} %shard_map.85), channel_id=1, source_target_pairs={{0,4},{1,5},{2,6},{3,7},{4,0},{5,1},{6,2},{7,3},{8,12},{9,13},{10,... | collective-permute-start | bytes 884744 | tf_op jit(solution)/shard_map/ppermute | solution.py:225
  77.7 6.1 %collective-permute-start.4 = (bf16[1,224,256]{2,1,0:T(8,128)(2,1)S(1)}, bf16[1,224,256]{2,1,0:T(8,128)(2,1)S(1)}, u32[]{:S(2)}, u32[]{:S(2)}) collective-permute-start(bf16[1,224,256]{2,1,0:T(8,128)(2,1)S(1)} %shard_map.79), channel_id=1, source_target_pairs={{0,1},{1,2},{2,3},{3,0},{4,5},{5,6},{6,7},{7,4},{8,9},{9,10},{10,1... | collective-permute-start | bytes 344072 | tf_op jit(solution)/shard_map/ppermute | solution.py:220
  78.0 5.8 %collective-permute-start.5 = (bf16[1,224,256]{2,1,0:T(8,128)(2,1)S(1)}, bf16[1,224,256]{2,1,0:T(8,128)(2,1)S(1)}, u32[]{:S(2)}, u32[]{:S(2)}) collective-permute-start(bf16[1,224,256]{2,1,0:T(8,128)(2,1)S(1)} %shard_map.80), channel_id=1, source_target_pairs={{0,3},{1,0},{2,1},{3,2},{4,7},{5,4},{6,5},{7,6},{8,11},{9,8},{10,9... | collective-permute-start | bytes 344072 | tf_op jit(solution)/shard_map/ppermute | solution.py:220

commit v7 on v6

--- a/solution.py
+++ b/solution.py
@@ -83,7 +83,7 @@
     blocks, both, n = packed.shape
     ch = both // 2
     tiles, rows = ch // TILE, blocks * TILE
-    real, imag = slice(0, n), slice(n, 2 * n)
+    real, imag, third = slice(0, n), slice(n, 2 * n), slice(2 * n, 3 * n)
     lane = lax.broadcasted_iota(jnp.int32, (1, n), 1)
     sign = jnp.where(lane % 2 == 0, 1.0, -1.0).astype(F32)
 
@@ -96,39 +96,37 @@
     def spectra(tile):
         g_spec, p_spec = g_specs[tile % 2], p_specs[tile % 2]
 
-        def gated(columns):
-            def task():
-                g_spec[:, :, columns] = spectrum(tile * TILE, columns)
-
-            return task
+        def gated():
+            re, im = (spectrum(tile * TILE, columns) for columns in (real, imag))
+            g_spec[:, :, real], g_spec[:, :, imag], g_spec[:, :, third] = re, im, re + im
 
         def pairs():
             re, im = (spectrum(ch + tile * TILE, columns) for columns in (real, imag))
-            p_spec[0, :, real], p_spec[0, :, imag] = re[0], im[0]
-            for k in range(1, blocks):
-                p_spec[k, :, real] = re[k] - sign * im[k - 1]
-                p_spec[k, :, imag] = im[k] + sign * re[k - 1]
-
-        return [gated(real), gated(imag), pairs]
+            for k in range(blocks):
+                pr, pi = (re[k] - sign * im[k - 1], im[k] + sign * re[k - 1]) if k else (re[k], im[k])
+                p_spec[k, :, real], p_spec[k, :, imag], p_spec[k, :, third] = pr, pi - pr, pr + pi
+
+        return [gated, pairs]
 
     def products(tile):
         g_spec, p_spec = g_specs[tile % 2], p_specs[tile % 2]
         high, low = highs[tile % 2], lows[tile % 2]
 
         def task(lanes, start):
-            re, im = slice(lanes, lanes + LANES), slice(n + lanes, n + lanes + LANES)
+            re, im, both = (slice(k * n + lanes, k * n + lanes + LANES) for k in range(3))
             total, window = [None] * REACH, [None] * REACH
             for a in range(start + REACH):
-                gr, gi = g_spec[a, :, re], g_spec[a, :, im]
+                gr, gi, gs = (g_spec[a, :, part] for part in (re, im, both))
                 for r in reversed(range(REACH)):
                     lag = start + r - a
                     if lag < 0:
                         continue
                     fresh = a == 0 or r == 0
-                    window[r] = (p_spec[lag, :, re], p_spec[lag, :, im]) if fresh else window[r - 1]
-                    pr, pi = window[r]
-                    term = (gr * pr - gi * pi, gr * pi + gi * pr)
-                    total[r] = term if a == 0 else (total[r][0] + term[0], total[r][1] + term[1])
+                    window[r] = tuple(p_spec[lag, :, part] for part in (re, im, both)) if fresh else window[r - 1]
+                    pr, pd, ps = window[r]
+                    term = (gs * pr, gr * pd, gi * ps)
+                    total[r] = term if a == 0 else tuple(t + u for t, u in zip(total[r], term, strict=True))
+            total = [(first - last, first + middle) for first, middle, last in total]
             for r in range(REACH):
                 for value, columns in zip(total[r], (re, im), strict=True):
                     rounded = value.astype(BF16)
@@ -177,8 +175,8 @@
         in_specs=[near] * 3,
         out_specs=near,
         out_shape=jax.ShapeDtypeStruct((blocks, ch, n), BF16),
-        scratch_shapes=[pltpu.VMEM((blocks, TILE, 2 * n), F32)] * 4 + [pltpu.VMEM((blocks, TILE, 2 * n), BF16)] * 4,
-        compiler_params=pltpu.CompilerParams(vmem_limit_bytes=8 * 2**20),
+        scratch_shapes=[pltpu.VMEM((blocks, TILE, 3 * n), F32)] * 4 + [pltpu.VMEM((blocks, TILE, 2 * n), BF16)] * 4,
+        compiler_params=pltpu.CompilerParams(vmem_limit_bytes=10 * 2**20),
         cost_estimate=pl.CostEstimate(flops=5 * 10**9, bytes_accessed=1, transcendentals=0),
         name="convolve",
     )(packed, skip, table)
@@ -263,7 +261,7 @@
     mixed = (gate_t.astype(F32) * conv.astype(F32)).astype(BF16)
 
     chunk = out_proj.shape[0] // chans
-    half_a = 224
+    half_a = 240
     half_b = chunk // 2 - half_a
 
     def rows_a(flip, *places):
@@ -284,10 +282,11 @@
     x_early = to_x(x_early)
     direct_up, direct_down = run(half_b, rows_b((1, 1)), rows_b((3, 0)))
     b_below, b_above = to_z(direct_up, 1), to_z(direct_down, -1)
+    (rest_b,) = run(half_b, rows_b(*late))
     (x_late,) = run(half_a, rows_a(1, *late))
+    (own_a,) = run(half_a, rows_a(0, *early, *late))
+    rest_b, x_late, own_a = lax.optimization_barrier((rest_b, x_late, own_a))
     x_late = to_x(x_late)
-    (rest_b,) = run(half_b, rows_b(*late))
-    (own_a,) = run(half_a, rows_a(0, *early, *late))
 
     b_up = to_z(add((rest_b, 0, 2), (relayed_up, 0, 2)), 1)
     b_down = to_z(add((rest_b, 2, 4), (relayed_down, 0, 2)), -1)

time: 85.4 us -> 84.4 us (0.988)
  waiting for transfers between devices: 24.4 us -> 23.2 us
    ppermute x10, waiting for transfers between devices: 9.02 us -> 7.77 us  [to_z(): lax.ppermute(block, 'chan', [(i, i // Z * Z + (i + step) % Z) for i in ra...]
    ppermute x10, starting transfers between devices: 17.4 us -> 18.4 us  [to_z(): lax.ppermute(block, 'chan', [(i, i // Z * Z + (i + step) % Z) for i in ra...]
  transfers between devices with their start and end apart: 14 -> 14, of which waited for: 5 -> 6; matrix products, arithmetic and copies ran while one was open for 0% -> 0% of each run, Pallas kernels for 5% -> 5%
where the time goes in v7:
time: 84.4 us; the launch traced here: 84.1 us
  starting transfers between devices  28.9 us (34%)
  waiting for transfers between devices  23.2 us (27%)
  blocking collectives  15.1 us (18%)
  Pallas kernels  14.1 us (17%)
  local copies, waits for them, and re-layouts  2.45 us (3%)
    ppermute x10, starting transfers between devices, to_z(): lax.ppermute(block, 'chan', [(i, i // Z * Z + (i + step) % Z) for i in ra...  18.4 us
    all_to_all x1, waiting for transfers between devices, shards(): lax.all_to_all(packed, 'seq', 0, 0)  15.3 us
    all_to_all x1, blocking collectives, shards(): conv = lax.all_to_all(conv, 'seq', 0, 0).reshape(channels, tokens)  15.1 us
    ppermute x10, waiting for transfers between devices, to_z(): lax.ppermute(block, 'chan', [(i, i // Z * Z + (i + step) % Z) for i in ra...  7.77 us
    pallas_call x14, Pallas kernels, on_chip(): pl.pallas_call(body, in_specs=[in_vmem] * len(args), out_specs=[in_vmem]...  7.24 us
    all_to_all x1, starting transfers between devices, shards(): lax.all_to_all(packed, 'seq', 0, 0)  7.13 us
    pallas_call x1, Pallas kernels, convolve(): pl.pallas_call(conv_kernel, in_specs=[near] * 3, out_specs=near, out_shap...  4.38 us
    ppermute x3, starting transfers between devices, to_x(): return lax.ppermute(block, 'chan', [(i, (i + Z) % n) for i in range(n)])  3.36 us
  transfers between devices with their start and end apart: 14, of which 6 were waited for; matrix products, arithmetic and copies ran while one was open for 0% of the time, Pallas kernels for 5%

profile of v7, /device:TPU:0, one launch (start us, length us, event | category | flops | bytes accessed | tf_op | source)
XLA Modules:
  0.0 84.1 jit_solution(11636224394712178751)
XLA Ops:
  0.0 2.4 %prepare.1 = bf16[16,128,256]{2,1,0:T(8,128)(2,1)} custom-call(bf16[256,1024]{1,0:T(8,128)(2,1)} %in_gate.1, bf16[256,1024]{1,0:T(8,128)(2,1)} %signal.1, bf16[256,1024]{1,0:T(8,128)(2,1)} %taps.1), custom_call_target="tpu_custom_call" | custom-call | tf_op jit(solution)/shard_map/prepare/pallas_call | solution.py:64
  2.5 7.1 %all-to-all-start = ((bf16[16,128,256]{2,1,0:T(8,128)(2,1)}), bf16[16,128,256]{2,1,0:T(8,128)(2,1)S(1)}, u32[]{:S(2)}, u32[]{:S(2)}) async-start(bf16[16,128,256]{2,1,0:T(8,128)(2,1)} %prepare.1), calls=%async_computation | async-start | bytes 2097152 | tf_op jit(solution)/shard_map/all_to_all | solution.py:257
  9.6 0.1 dynamic-slice_bitcast_fusion
  9.7 0.1 copy.8.skip
  9.8 1.2 %copy-done.2 = bf16[1024,512]{1,0:T(8,128)(2,1)S(1)} copy-done((bf16[1024,512]{1,0:T(8,128)(2,1)S(1)}, bf16[1024,512]{1,0:T(8,128)(2,1)}, u32[]{:S(2)}) %copy-start.2) | copy-done | bytes 1048600
  11.0 1.0 %copy-done.3 = bf16[256,1024]{1,0:T(8,128)(2,1)S(1)} copy-done((bf16[256,1024]{1,0:T(8,128)(2,1)S(1)}, bf16[256,1024]{1,0:T(8,128)(2,1)}, u32[]{:S(2)}) %copy-start.3) | copy-done | bytes 524312
  12.1 0.2 shard_map.73
  12.3 15.3 %all-to-all-done.packed = bf16[16,128,256]{2,1,0:T(8,128)(2,1)S(1)} async-done(((bf16[16,128,256]{2,1,0:T(8,128)(2,1)}), bf16[16,128,256]{2,1,0:T(8,128)(2,1)S(1)}, u32[]{:S(2)}, u32[]{:S(2)}) %all-to-all-start) | async-done | bytes 1048608 | tf_op jit(solution)/shard_map/all_to_all | solution.py:257
  27.6 4.4 %convolve.1 = bf16[16,64,256]{2,1,0:T(8,128)(2,1)S(1)} custom-call(bf16[16,128,256]{2,1,0:T(8,128)(2,1)S(1)} %all-to-all-done.packed, f32[64,1]{1,0:T(8,128)S(1)} %copy.8.skip, bf16[1024,512]{1,0:T(8,128)(2,1)S(1)} %get-tuple-element.33.table), custom_call_target="tpu_custom_call" | custom-call | flops 5000000000 | bytes 1 | tf_op jit(solution)/shard_map/convolve/pallas_call | solution.py:173
  32.0 15.1 %all_to_all.10 = bf16[16,64,256]{2,1,0:T(8,128)(2,1)S(1)} all-to-all(bf16[16,64,256]{2,1,0:T(8,128)(2,1)S(1)} %convolve.1), channel_id=1, replica_groups=mesh['seq'=16,'chan'=8] {'seq'}, dimensions={0} | all-to-all | bytes 1048576 | tf_op jit(solution)/shard_map/all_to_all | solution.py:260
  47.1 0.2 fusion.mixed
  47.3 0.0 copy-done.1
  47.3 0.7 shard_map.74
  48.1 0.7 shard_map.75
  48.7 0.7 collective-permute-start.1
  49.5 1.9 %collective-permute-start.8 = (bf16[2,272,256]{2,1,0:T(8,128)(2,1)S(1)}, bf16[2,272,256]{2,1,0:T(8,128)(2,1)S(1)}, u32[]{:S(2)}, u32[]{:S(2)}) collective-permute-start(bf16[2,272,256]{2,1,0:T(8,128)(2,1)S(1)} %get-tuple-element.46), channel_id=1, source_target_pairs={{0,1},{1,2},{2,3},{3,0},{4,5},{5,6},{6,7},{7,4},{8,9},{9,10},{10,1... | collective-permute-start | bytes 835592 | tf_op jit(solution)/shard_map/ppermute | solution.py:218
  51.4 2.1 %collective-permute-start.10 = (bf16[2,272,256]{2,1,0:T(8,128)(2,1)S(1)}, bf16[2,272,256]{2,1,0:T(8,128)(2,1)S(1)}, u32[]{:S(2)}, u32[]{:S(2)}) collective-permute-start(bf16[2,272,256]{2,1,0:T(8,128)(2,1)S(1)} %get-tuple-element.47), channel_id=1, source_target_pairs={{0,3},{1,0},{2,1},{3,2},{4,7},{5,4},{6,5},{7,6},{8,11},{9,8},{10,9... | collective-permute-start | bytes 835592 | tf_op jit(solution)/shard_map/ppermute | solution.py:218
  53.5 0.7 shard_map.82
  54.2 0.1 collective-permute-start.6
  54.3 3.2 %collective-permute-start.7 = (bf16[2,272,256]{2,1,0:T(8,128)(2,1)S(1)}, bf16[2,272,256]{2,1,0:T(8,128)(2,1)S(1)}, u32[]{:S(2)}, u32[]{:S(2)}) collective-permute-start(bf16[2,272,256]{2,1,0:T(8,128)(2,1)S(1)} %get-tuple-element.45), channel_id=1, source_target_pairs={{0,3},{1,0},{2,1},{3,2},{4,7},{5,4},{6,5},{7,6},{8,11},{9,8},{10,9... | collective-permute-start | bytes 835592 | tf_op jit(solution)/shard_map/ppermute | solution.py:218
  57.6 1.2 %shard_map.78.own.refs_0_ = bf16[8,240,256]{2,1,0:T(8,128)(2,1)S(1)} custom-call(bf16[8192,1024]{1,0:T(8,128)(2,1)S(1)} %copy-done.1, bf16[1024,256]{1,0:T(8,128)(2,1)S(1)} %fusion.mixed), custom_call_target="tpu_custom_call" | custom-call | flops 1006632960 | bytes 1 | tf_op jit(solution)/shard_map/pallas_call | solution.py:187
  58.7 1.3 %shard_map.76.refs_0_.rest = bf16[8,272,256]{2,1,0:T(8,128)(2,1)S(1)} custom-call(bf16[8192,1024]{1,0:T(8,128)(2,1)S(1)} %copy-done.1, bf16[1024,256]{1,0:T(8,128)(2,1)S(1)} %fusion.mixed), custom_call_target="tpu_custom_call" | custom-call | flops 1140850688 | bytes 1 | tf_op jit(solution)/shard_map/pallas_call | solution.py:187
  60.1 0.7 shard_map.77
  60.7 0.3 collective-permute-done.8.refs_1_
  61.1 1.4 %collective-permute-start = (bf16[4,240,256]{2,1,0:T(8,128)(2,1)S(1)}, bf16[4,240,256]{2,1,0:T(8,128)(2,1)S(1)}, u32[]{:S(2)}, u32[]{:S(2)}) collective-permute-start(bf16[4,240,256]{2,1,0:T(8,128)(2,1)S(1)} %shard_map.77), channel_id=1, source_target_pairs={{0,4},{1,5},{2,6},{3,7},{4,0},{5,1},{6,2},{7,3},{8,12},{9,13},{10,... | collective-permute-start | bytes 1474568 | tf_op jit(solution)/shard_map/ppermute | solution.py:223
  62.4 0.1 shard_map.83
  62.5 0.0 collective-permute-done.10.refs_1_
  62.5 0.4 collective-permute-start.9
  62.9 0.1 shard_map.84
  63.0 0.0 collective-permute-done.1.arrived
  63.0 4.0 %collective-permute-start.11 = (bf16[2,272,256]{2,1,0:T(8,128)(2,1)S(1)}, bf16[2,272,256]{2,1,0:T(8,128)(2,1)S(1)}, u32[]{:S(2)}, u32[]{:S(2)}) collective-permute-start(bf16[2,272,256]{2,1,0:T(8,128)(2,1)S(1)} %shard_map.84), channel_id=1, source_target_pairs={{0,3},{1,0},{2,1},{3,2},{4,7},{5,4},{6,5},{7,6},{8,11},{9,8},{10,9... | collective-permute-start | bytes 835592 | tf_op jit(solution)/shard_map/ppermute | solution.py:218
  67.0 0.1 shard_map.79
  67.1 0.0 collective-permute-done.6.refs_1_.b_below
  67.1 0.1 collective-permute-start.2
  67.2 0.0 collective-permute-done.7.refs_2_.b_above
  67.2 3.2 %collective-permute-start.3 = (bf16[2,240,256]{2,1,0:T(8,128)(2,1)S(1)}, bf16[2,240,256]{2,1,0:T(8,128)(2,1)S(1)}, u32[]{:S(2)}, u32[]{:S(2)}) collective-permute-start(bf16[2,240,256]{2,1,0:T(8,128)(2,1)S(1)} %get-tuple-element.42), channel_id=1, source_target_pairs={{0,3},{1,0},{2,1},{3,2},{4,7},{5,4},{6,5},{7,6},{8,11},{9,8},{10,9... | collective-permute-start | bytes 737288 | tf_op jit(solution)/shard_map/ppermute | solution.py:218
  70.4 3.0 %collective-permute-done.9.refs_3_.b_up = bf16[2,272,256]{2,1,0:T(8,128)(2,1)S(1)} collective-permute-done((bf16[2,272,256]{2,1,0:T(8,128)(2,1)S(1)}, bf16[2,272,256]{2,1,0:T(8,128)(2,1)S(1)}, u32[]{:S(2)}, u32[]{:S(2)}) %collective-permute-start.9) | collective-permute-done | bytes 278560 | tf_op jit(solution)/shard_map/ppermute | solution.py:218
  73.4 0.0 collective-permute-done.11.refs_4_.b_down
  73.4 0.1 shard_map.85
  73.5 1.3 %collective-permute-start.12 = (bf16[544,256]{1,0:T(8,128)(2,1)S(1)}, bf16[544,256]{1,0:T(8,128)(2,1)S(1)}, u32[]{:S(2)}, u32[]{:S(2)}) collective-permute-start(bf16[544,256]{1,0:T(8,128)(2,1)S(1)} %shard_map.85), channel_id=1, source_target_pairs={{0,4},{1,5},{2,6},{3,7},{4,0},{5,1},{6,2},{7,3},{8,12},{9,13},{10,... | collective-permute-start | bytes 835592 | tf_op jit(solution)/shard_map/ppermute | solution.py:223
  74.8 0.0 collective-permute-done.refs_1_.x_late
  74.8 1.8 %collective-permute-done.2.refs_2_.below = bf16[2,240,256]{2,1,0:T(8,128)(2,1)S(1)} collective-permute-done((bf16[2,240,256]{2,1,0:T(8,128)(2,1)S(1)}, bf16[2,240,256]{2,1,0:T(8,128)(2,1)S(1)}, u32[]{:S(2)}, u32[]{:S(2)}) %collective-permute-start.2) | collective-permute-done | bytes 245792 | tf_op jit(solution)/shard_map/ppermute | solution.py:218
  76.6 0.1 collective-permute-start.4
  76.7 0.0 collective-permute-done.3.refs_2_.above
  76.8 3.3 %collective-permute-start.5 = (bf16[1,240,256]{2,1,0:T(8,128)(2,1)S(1)}, bf16[1,240,256]{2,1,0:T(8,128)(2,1)S(1)}, u32[]{:S(2)}, u32[]{:S(2)}) collective-permute-start(bf16[1,240,256]{2,1,0:T(8,128)(2,1)S(1)} %shard_map.81), channel_id=1, source_target_pairs={{0,3},{1,0},{2,1},{3,2},{4,7},{5,4},{6,5},{7,6},{8,11},{9,8},{10,9... | collective-permute-start | bytes 368648 | tf_op jit(solution)/shard_map/ppermute | solution.py:218
  80.1 0.1 collective-permute-done.12.x_last
  80.1 2.7 %collective-permute-done.4.up = bf16[1,240,256]{2,1,0:T(8,128)(2,1)S(1)} collective-permute-done((bf16[1,240,256]{2,1,0:T(8,128)(2,1)S(1)}, bf16[1,240,256]{2,1,0:T(8,128)(2,1)S(1)}, u32[]{:S(2)}, u32[]{:S(2)}) %collective-permute-start.4) | collective-permute-done | bytes 122912 | tf_op jit(solution)/shard_map/ppermute | solution.py:218
  82.8 1.2 %shard_map.86 = (bf16[256,1024]{1,0:T(8,128)(2,1)}, bf16[1024,256]{1,0:T(8,128)(2,1)}) custom-call(bf16[8,240,256]{2,1,0:T(8,128)(2,1)S(1)} %shard_map.78.own.refs_0_, bf16[4,240,256]{2,1,0:T(8,128)(2,1)S(1)} %collective-permute-done.refs_1_.x_late, bf16[2,240,256]{2,1,0:T(8,128)(2,1)S(1)} %collective-permute-done.2.refs_2_.below, ...), custom_call_target="tpu_custom_call" | custom-call | bytes 1 | tf_op jit(solution)/shard_map/pallas_call | solution.py:187
  (8 shorter events, 0.1 us)
Async XLA Ops:
  0.0 9.6 %copy-start = (f32[1024]{0:T(1024)S(1)}, f32[1024]{0:T(1024)}, u32[]{:S(2)}) copy-start(f32[1024]{0:T(1024)} %param.11) | copy-start | bytes 12292
  2.5 25.2 %all-to-all-start = ((bf16[16,128,256]{2,1,0:T(8,128)(2,1)}), bf16[16,128,256]{2,1,0:T(8,128)(2,1)S(1)}, u32[]{:S(2)}, u32[]{:S(2)}) async-start(bf16[16,128,256]{2,1,0:T(8,128)(2,1)} %prepare.1), calls=%async_computation | async-start | bytes 2097152 | tf_op jit(solution)/shard_map/all_to_all | solution.py:257
  9.8 1.2 %copy-start.2 = (bf16[1024,512]{1,0:T(8,128)(2,1)S(1)}, bf16[1024,512]{1,0:T(8,128)(2,1)}, u32[]{:S(2)}) copy-start(bf16[1024,512]{1,0:T(8,128)(2,1)} %constant.14.clone.table) | copy-start | bytes 3145732
  11.0 1.0 %copy-start.3 = (bf16[256,1024]{1,0:T(8,128)(2,1)S(1)}, bf16[256,1024]{1,0:T(8,128)(2,1)}, u32[]{:S(2)}) copy-start(bf16[256,1024]{1,0:T(8,128)(2,1)} %gate) | copy-start | bytes 1572868
  27.6 19.7 %copy-start.1 = (bf16[8192,1024]{1,0:T(8,128)(2,1)S(1)}, bf16[8192,1024]{1,0:T(8,128)(2,1)}, u32[]{:S(2)}) copy-start(bf16[8192,1024]{1,0:T(8,128)(2,1)} %weight.11) | copy-start | bytes 50331652
  48.7 14.2 %collective-permute-start.1 = (bf16[4,240,256]{2,1,0:T(8,128)(2,1)S(1)}, bf16[4,240,256]{2,1,0:T(8,128)(2,1)S(1)}, u32[]{:S(2)}, u32[]{:S(2)}) collective-permute-start(bf16[4,240,256]{2,1,0:T(8,128)(2,1)S(1)} %shard_map.75), channel_id=1, source_target_pairs={{0,4},{1,5},{2,6},{3,7},{4,0},{5,1},{6,2},{7,3},{8,12},{9,13},{10,... | collective-permute-start | bytes 1474568 | tf_op jit(solution)/shard_map/ppermute | solution.py:223
  49.5 11.6 %collective-permute-start.8 = (bf16[2,272,256]{2,1,0:T(8,128)(2,1)S(1)}, bf16[2,272,256]{2,1,0:T(8,128)(2,1)S(1)}, u32[]{:S(2)}, u32[]{:S(2)}) collective-permute-start(bf16[2,272,256]{2,1,0:T(8,128)(2,1)S(1)} %get-tuple-element.46), channel_id=1, source_target_pairs={{0,1},{1,2},{2,3},{3,0},{4,5},{5,6},{6,7},{7,4},{8,9},{9,10},{10,1... | collective-permute-start | bytes 835592 | tf_op jit(solution)/shard_map/ppermute | solution.py:218
  51.4 11.1 %collective-permute-start.10 = (bf16[2,272,256]{2,1,0:T(8,128)(2,1)S(1)}, bf16[2,272,256]{2,1,0:T(8,128)(2,1)S(1)}, u32[]{:S(2)}, u32[]{:S(2)}) collective-permute-start(bf16[2,272,256]{2,1,0:T(8,128)(2,1)S(1)} %get-tuple-element.47), channel_id=1, source_target_pairs={{0,3},{1,0},{2,1},{3,2},{4,7},{5,4},{6,5},{7,6},{8,11},{9,8},{10,9... | collective-permute-start | bytes 835592 | tf_op jit(solution)/shard_map/ppermute | solution.py:218
  54.2 12.9 %collective-permute-start.6 = (bf16[2,272,256]{2,1,0:T(8,128)(2,1)S(1)}, bf16[2,272,256]{2,1,0:T(8,128)(2,1)S(1)}, u32[]{:S(2)}, u32[]{:S(2)}) collective-permute-start(bf16[2,272,256]{2,1,0:T(8,128)(2,1)S(1)} %get-tuple-element.44), channel_id=1, source_target_pairs={{0,1},{1,2},{2,3},{3,0},{4,5},{5,6},{6,7},{7,4},{8,9},{9,10},{10,1... | collective-permute-start | bytes 835592 | tf_op jit(solution)/shard_map/ppermute | solution.py:218
  54.3 12.9 %collective-permute-start.7 = (bf16[2,272,256]{2,1,0:T(8,128)(2,1)S(1)}, bf16[2,272,256]{2,1,0:T(8,128)(2,1)S(1)}, u32[]{:S(2)}, u32[]{:S(2)}) collective-permute-start(bf16[2,272,256]{2,1,0:T(8,128)(2,1)S(1)} %get-tuple-element.45), channel_id=1, source_target_pairs={{0,3},{1,0},{2,1},{3,2},{4,7},{5,4},{6,5},{7,6},{8,11},{9,8},{10,9... | collective-permute-start | bytes 835592 | tf_op jit(solution)/shard_map/ppermute | solution.py:218
  61.1 13.7 %collective-permute-start = (bf16[4,240,256]{2,1,0:T(8,128)(2,1)S(1)}, bf16[4,240,256]{2,1,0:T(8,128)(2,1)S(1)}, u32[]{:S(2)}, u32[]{:S(2)}) collective-permute-start(bf16[4,240,256]{2,1,0:T(8,128)(2,1)S(1)} %shard_map.77), channel_id=1, source_target_pairs={{0,4},{1,5},{2,6},{3,7},{4,0},{5,1},{6,2},{7,3},{8,12},{9,13},{10,... | collective-permute-start | bytes 1474568 | tf_op jit(solution)/shard_map/ppermute | solution.py:223
  62.5 10.9 %collective-permute-start.9 = (bf16[2,272,256]{2,1,0:T(8,128)(2,1)S(1)}, bf16[2,272,256]{2,1,0:T(8,128)(2,1)S(1)}, u32[]{:S(2)}, u32[]{:S(2)}) collective-permute-start(bf16[2,272,256]{2,1,0:T(8,128)(2,1)S(1)} %shard_map.83), channel_id=1, source_target_pairs={{0,1},{1,2},{2,3},{3,0},{4,5},{5,6},{6,7},{7,4},{8,9},{9,10},{10,1... | collective-permute-start | bytes 835592 | tf_op jit(solution)/shard_map/ppermute | solution.py:218
  63.0 10.4 %collective-permute-start.11 = (bf16[2,272,256]{2,1,0:T(8,128)(2,1)S(1)}, bf16[2,272,256]{2,1,0:T(8,128)(2,1)S(1)}, u32[]{:S(2)}, u32[]{:S(2)}) collective-permute-start(bf16[2,272,256]{2,1,0:T(8,128)(2,1)S(1)} %shard_map.84), channel_id=1, source_target_pairs={{0,3},{1,0},{2,1},{3,2},{4,7},{5,4},{6,5},{7,6},{8,11},{9,8},{10,9... | collective-permute-start | bytes 835592 | tf_op jit(solution)/shard_map/ppermute | solution.py:218
  67.1 9.5 %collective-permute-start.2 = (bf16[2,240,256]{2,1,0:T(8,128)(2,1)S(1)}, bf16[2,240,256]{2,1,0:T(8,128)(2,1)S(1)}, u32[]{:S(2)}, u32[]{:S(2)}) collective-permute-start(bf16[2,240,256]{2,1,0:T(8,128)(2,1)S(1)} %get-tuple-element.41), channel_id=1, source_target_pairs={{0,1},{1,2},{2,3},{3,0},{4,5},{5,6},{6,7},{7,4},{8,9},{9,10},{10,1... | collective-permute-start | bytes 737288 | tf_op jit(solution)/shard_map/ppermute | solution.py:218
  67.2 9.5 %collective-permute-start.3 = (bf16[2,240,256]{2,1,0:T(8,128)(2,1)S(1)}, bf16[2,240,256]{2,1,0:T(8,128)(2,1)S(1)}, u32[]{:S(2)}, u32[]{:S(2)}) collective-permute-start(bf16[2,240,256]{2,1,0:T(8,128)(2,1)S(1)} %get-tuple-element.42), channel_id=1, source_target_pairs={{0,3},{1,0},{2,1},{3,2},{4,7},{5,4},{6,5},{7,6},{8,11},{9,8},{10,9... | collective-permute-start | bytes 737288 | tf_op jit(solution)/shard_map/ppermute | solution.py:218
  73.5 6.6 %collective-permute-start.12 = (bf16[544,256]{1,0:T(8,128)(2,1)S(1)}, bf16[544,256]{1,0:T(8,128)(2,1)S(1)}, u32[]{:S(2)}, u32[]{:S(2)}) collective-permute-start(bf16[544,256]{1,0:T(8,128)(2,1)S(1)} %shard_map.85), channel_id=1, source_target_pairs={{0,4},{1,5},{2,6},{3,7},{4,0},{5,1},{6,2},{7,3},{8,12},{9,13},{10,... | collective-permute-start | bytes 835592 | tf_op jit(solution)/shard_map/ppermute | solution.py:223
  76.6 6.2 %collective-permute-start.4 = (bf16[1,240,256]{2,1,0:T(8,128)(2,1)S(1)}, bf16[1,240,256]{2,1,0:T(8,128)(2,1)S(1)}, u32[]{:S(2)}, u32[]{:S(2)}) collective-permute-start(bf16[1,240,256]{2,1,0:T(8,128)(2,1)S(1)} %shard_map.80), channel_id=1, source_target_pairs={{0,1},{1,2},{2,3},{3,0},{4,5},{5,6},{6,7},{7,4},{8,9},{9,10},{10,1... | collective-permute-start | bytes 368648 | tf_op jit(solution)/shard_map/ppermute | solution.py:218
  76.8 6.0 %collective-permute-start.5 = (bf16[1,240,256]{2,1,0:T(8,128)(2,1)S(1)}, bf16[1,240,256]{2,1,0:T(8,128)(2,1)S(1)}, u32[]{:S(2)}, u32[]{:S(2)}) collective-permute-start(bf16[1,240,256]{2,1,0:T(8,128)(2,1)S(1)} %shard_map.81), channel_id=1, source_target_pairs={{0,3},{1,0},{2,1},{3,2},{4,7},{5,4},{6,5},{7,6},{8,11},{9,8},{10,9... | collective-permute-start | bytes 368648 | tf_op jit(solution)/shard_map/ppermute | solution.py:218

commit v8 on v7

--- a/solution.py
+++ b/solution.py
@@ -261,7 +261,7 @@
     mixed = (gate_t.astype(F32) * conv.astype(F32)).astype(BF16)
 
     chunk = out_proj.shape[0] // chans
-    half_a = 240
+    half_a = 256
     half_b = chunk // 2 - half_a
 
     def rows_a(flip, *places):

time: 84.4 us -> 85.8 us (1.017)
  waiting for transfers between devices: 23.2 us -> 25.3 us
    ppermute x10, starting transfers between devices: 18.4 us -> 16.9 us  [to_z(): lax.ppermute(block, 'chan', [(i, i // Z * Z + (i + step) % Z) for i in ra...]
    ppermute x10, waiting for transfers between devices: 7.77 us -> 9.2 us  [to_z(): lax.ppermute(block, 'chan', [(i, i // Z * Z + (i + step) % Z) for i in ra...]
  transfers between devices with their start and end apart: 14 -> 14, of which waited for: 6 -> 9; matrix products, arithmetic and copies ran while one was open for 0% -> 0% of each run, Pallas kernels for 5% -> 5%
where the time goes in v8:
time: 85.8 us; the launch traced here: 85.5 us
  starting transfers between devices  28.2 us (33%)
  waiting for transfers between devices  25.3 us (29%)
  blocking collectives  15.1 us (18%)
  Pallas kernels  14.1 us (16%)
  local copies, waits for them, and re-layouts  2.45 us (3%)
    ppermute x10, starting transfers between devices, to_z(): lax.ppermute(block, 'chan', [(i, i // Z * Z + (i + step) % Z) for i in ra...  16.9 us
    all_to_all x1, waiting for transfers between devices, shards(): lax.all_to_all(packed, 'seq', 0, 0)  15.3 us
    all_to_all x1, blocking collectives, shards(): conv = lax.all_to_all(conv, 'seq', 0, 0).reshape(channels, tokens)  15.1 us
    ppermute x10, waiting for transfers between devices, to_z(): lax.ppermute(block, 'chan', [(i, i // Z * Z + (i + step) % Z) for i in ra...  9.2 us
    pallas_call x14, Pallas kernels, on_chip(): pl.pallas_call(body, in_specs=[in_vmem] * len(args), out_specs=[in_vmem]...  7.24 us
    all_to_all x1, starting transfers between devices, shards(): lax.all_to_all(packed, 'seq', 0, 0)  7.13 us
    pallas_call x1, Pallas kernels, convolve(): pl.pallas_call(conv_kernel, in_specs=[near] * 3, out_specs=near, out_shap...  4.38 us
    ppermute x3, starting transfers between devices, to_x(): return lax.ppermute(block, 'chan', [(i, (i + Z) % n) for i in range(n)])  4.21 us
  transfers between devices with their start and end apart: 14, of which 9 were waited for; matrix products, arithmetic and copies ran while one was open for 0% of the time, Pallas kernels for 5%

profile of v8, /device:TPU:0, one launch (start us, length us, event | category | flops | bytes accessed | tf_op | source)
XLA Modules:
  0.0 85.5 jit_solution(4014414410970421641)
XLA Ops:
  0.0 2.4 %prepare.1 = bf16[16,128,256]{2,1,0:T(8,128)(2,1)} custom-call(bf16[256,1024]{1,0:T(8,128)(2,1)} %in_gate.1, bf16[256,1024]{1,0:T(8,128)(2,1)} %signal.1, bf16[256,1024]{1,0:T(8,128)(2,1)} %taps.1), custom_call_target="tpu_custom_call" | custom-call | tf_op jit(solution)/shard_map/prepare/pallas_call | solution.py:64
  2.5 7.1 %all-to-all-start = ((bf16[16,128,256]{2,1,0:T(8,128)(2,1)}), bf16[16,128,256]{2,1,0:T(8,128)(2,1)S(1)}, u32[]{:S(2)}, u32[]{:S(2)}) async-start(bf16[16,128,256]{2,1,0:T(8,128)(2,1)} %prepare.1), calls=%async_computation | async-start | bytes 2097152 | tf_op jit(solution)/shard_map/all_to_all | solution.py:257
  9.6 0.1 dynamic-slice_bitcast_fusion
  9.7 0.1 copy.8.skip
  9.8 1.2 %copy-done.2 = bf16[1024,512]{1,0:T(8,128)(2,1)S(1)} copy-done((bf16[1024,512]{1,0:T(8,128)(2,1)S(1)}, bf16[1024,512]{1,0:T(8,128)(2,1)}, u32[]{:S(2)}) %copy-start.2) | copy-done | bytes 1048600
  11.0 1.0 %copy-done.3 = bf16[256,1024]{1,0:T(8,128)(2,1)S(1)} copy-done((bf16[256,1024]{1,0:T(8,128)(2,1)S(1)}, bf16[256,1024]{1,0:T(8,128)(2,1)}, u32[]{:S(2)}) %copy-start.3) | copy-done | bytes 524312
  12.1 0.2 shard_map.73
  12.3 15.3 %all-to-all-done.packed = bf16[16,128,256]{2,1,0:T(8,128)(2,1)S(1)} async-done(((bf16[16,128,256]{2,1,0:T(8,128)(2,1)}), bf16[16,128,256]{2,1,0:T(8,128)(2,1)S(1)}, u32[]{:S(2)}, u32[]{:S(2)}) %all-to-all-start) | async-done | bytes 1048608 | tf_op jit(solution)/shard_map/all_to_all | solution.py:257
  27.6 4.4 %convolve.1 = bf16[16,64,256]{2,1,0:T(8,128)(2,1)S(1)} custom-call(bf16[16,128,256]{2,1,0:T(8,128)(2,1)S(1)} %all-to-all-done.packed, f32[64,1]{1,0:T(8,128)S(1)} %copy.8.skip, bf16[1024,512]{1,0:T(8,128)(2,1)S(1)} %get-tuple-element.33.table), custom_call_target="tpu_custom_call" | custom-call | flops 5000000000 | bytes 1 | tf_op jit(solution)/shard_map/convolve/pallas_call | solution.py:173
  32.0 15.1 %all_to_all.10 = bf16[16,64,256]{2,1,0:T(8,128)(2,1)S(1)} all-to-all(bf16[16,64,256]{2,1,0:T(8,128)(2,1)S(1)} %convolve.1), channel_id=1, replica_groups=mesh['seq'=16,'chan'=8] {'seq'}, dimensions={0} | all-to-all | bytes 1048576 | tf_op jit(solution)/shard_map/all_to_all | solution.py:260
  47.1 0.2 fusion.mixed
  47.3 0.7 shard_map.74
  48.0 0.7 shard_map.75
  48.7 0.7 collective-permute-start.1
  49.5 1.9 %collective-permute-start.8 = (bf16[2,256,256]{2,1,0:T(8,128)(2,1)S(1)}, bf16[2,256,256]{2,1,0:T(8,128)(2,1)S(1)}, u32[]{:S(2)}, u32[]{:S(2)}) collective-permute-start(bf16[2,256,256]{2,1,0:T(8,128)(2,1)S(1)} %get-tuple-element.46), channel_id=1, source_target_pairs={{0,1},{1,2},{2,3},{3,0},{4,5},{5,6},{6,7},{7,4},{8,9},{9,10},{10,1... | collective-permute-start | bytes 786440 | tf_op jit(solution)/shard_map/ppermute | solution.py:218
  51.4 2.1 %collective-permute-start.10 = (bf16[2,256,256]{2,1,0:T(8,128)(2,1)S(1)}, bf16[2,256,256]{2,1,0:T(8,128)(2,1)S(1)}, u32[]{:S(2)}, u32[]{:S(2)}) collective-permute-start(bf16[2,256,256]{2,1,0:T(8,128)(2,1)S(1)} %get-tuple-element.47), channel_id=1, source_target_pairs={{0,3},{1,0},{2,1},{3,2},{4,7},{5,4},{6,5},{7,6},{8,11},{9,8},{10,9... | collective-permute-start | bytes 786440 | tf_op jit(solution)/shard_map/ppermute | solution.py:218
  53.5 0.7 shard_map.82
  54.2 0.1 collective-permute-start.6
  54.3 1.2 %shard_map.78.own.refs_0_ = bf16[8,256,256]{2,1,0:T(8,128)(2,1)S(1)} custom-call(bf16[8192,1024]{1,0:T(8,128)(2,1)S(1)} %copy-done.1, bf16[1024,256]{1,0:T(8,128)(2,1)S(1)} %fusion.mixed), custom_call_target="tpu_custom_call" | custom-call | flops 1073741824 | bytes 1 | tf_op jit(solution)/shard_map/pallas_call | solution.py:187
  55.6 0.7 shard_map.77
  56.3 1.2 %shard_map.76.refs_0_.rest = bf16[8,256,256]{2,1,0:T(8,128)(2,1)S(1)} custom-call(bf16[8192,1024]{1,0:T(8,128)(2,1)S(1)} %copy-done.1, bf16[1024,256]{1,0:T(8,128)(2,1)S(1)} %fusion.mixed), custom_call_target="tpu_custom_call" | custom-call | flops 1073741824 | bytes 1 | tf_op jit(solution)/shard_map/pallas_call | solution.py:187
  57.5 1.5 %collective-permute-start = (bf16[4,256,256]{2,1,0:T(8,128)(2,1)S(1)}, bf16[4,256,256]{2,1,0:T(8,128)(2,1)S(1)}, u32[]{:S(2)}, u32[]{:S(2)}) collective-permute-start(bf16[4,256,256]{2,1,0:T(8,128)(2,1)S(1)} %shard_map.77), channel_id=1, source_target_pairs={{0,4},{1,5},{2,6},{3,7},{4,0},{5,1},{6,2},{7,3},{8,12},{9,13},{10,... | collective-permute-start | bytes 1572872 | tf_op jit(solution)/shard_map/ppermute | solution.py:223
  59.0 1.7 %collective-permute-done.8.refs_1_ = bf16[2,256,256]{2,1,0:T(8,128)(2,1)S(1)} collective-permute-done((bf16[2,256,256]{2,1,0:T(8,128)(2,1)S(1)}, bf16[2,256,256]{2,1,0:T(8,128)(2,1)S(1)}, u32[]{:S(2)}, u32[]{:S(2)}) %collective-permute-start.8) | collective-permute-done | bytes 262176 | tf_op jit(solution)/shard_map/ppermute | solution.py:218
  60.7 2.0 %collective-permute-start.7 = (bf16[2,256,256]{2,1,0:T(8,128)(2,1)S(1)}, bf16[2,256,256]{2,1,0:T(8,128)(2,1)S(1)}, u32[]{:S(2)}, u32[]{:S(2)}) collective-permute-start(bf16[2,256,256]{2,1,0:T(8,128)(2,1)S(1)} %get-tuple-element.45), channel_id=1, source_target_pairs={{0,3},{1,0},{2,1},{3,2},{4,7},{5,4},{6,5},{7,6},{8,11},{9,8},{10,9... | collective-permute-start | bytes 786440 | tf_op jit(solution)/shard_map/ppermute | solution.py:218
  62.7 0.1 shard_map.83
  62.8 0.0 collective-permute-done.10.refs_1_
  62.8 0.1 collective-permute-start.9
  62.9 0.1 shard_map.84
  63.0 0.7 collective-permute-done.1.arrived
  63.7 4.0 %collective-permute-start.11 = (bf16[2,256,256]{2,1,0:T(8,128)(2,1)S(1)}, bf16[2,256,256]{2,1,0:T(8,128)(2,1)S(1)}, u32[]{:S(2)}, u32[]{:S(2)}) collective-permute-start(bf16[2,256,256]{2,1,0:T(8,128)(2,1)S(1)} %shard_map.84), channel_id=1, source_target_pairs={{0,3},{1,0},{2,1},{3,2},{4,7},{5,4},{6,5},{7,6},{8,11},{9,8},{10,9... | collective-permute-start | bytes 786440 | tf_op jit(solution)/shard_map/ppermute | solution.py:218
  67.7 0.1 shard_map.79
  67.8 0.1 collective-permute-start.2
  67.9 2.0 %collective-permute-done.7.refs_2_.b_above = bf16[2,256,256]{2,1,0:T(8,128)(2,1)S(1)} collective-permute-done((bf16[2,256,256]{2,1,0:T(8,128)(2,1)S(1)}, bf16[2,256,256]{2,1,0:T(8,128)(2,1)S(1)}, u32[]{:S(2)}, u32[]{:S(2)}) %collective-permute-start.7) | collective-permute-done | bytes 262176 | tf_op jit(solution)/shard_map/ppermute | solution.py:218
  69.9 2.5 %collective-permute-start.3 = (bf16[2,256,256]{2,1,0:T(8,128)(2,1)S(1)}, bf16[2,256,256]{2,1,0:T(8,128)(2,1)S(1)}, u32[]{:S(2)}, u32[]{:S(2)}) collective-permute-start(bf16[2,256,256]{2,1,0:T(8,128)(2,1)S(1)} %get-tuple-element.42), channel_id=1, source_target_pairs={{0,3},{1,0},{2,1},{3,2},{4,7},{5,4},{6,5},{7,6},{8,11},{9,8},{10,9... | collective-permute-start | bytes 786440 | tf_op jit(solution)/shard_map/ppermute | solution.py:218
  72.4 0.4 collective-permute-done.9.refs_3_.b_up
  72.8 1.6 %collective-permute-done.11.refs_4_.b_down = bf16[2,256,256]{2,1,0:T(8,128)(2,1)S(1)} collective-permute-done((bf16[2,256,256]{2,1,0:T(8,128)(2,1)S(1)}, bf16[2,256,256]{2,1,0:T(8,128)(2,1)S(1)}, u32[]{:S(2)}, u32[]{:S(2)}) %collective-permute-start.11) | collective-permute-done | bytes 262176 | tf_op jit(solution)/shard_map/ppermute | solution.py:218
  74.5 0.1 shard_map.85
  74.6 2.0 %collective-permute-start.12 = (bf16[512,256]{1,0:T(8,128)(2,1)S(1)}, bf16[512,256]{1,0:T(8,128)(2,1)S(1)}, u32[]{:S(2)}, u32[]{:S(2)}) collective-permute-start(bf16[512,256]{1,0:T(8,128)(2,1)S(1)} %shard_map.85), channel_id=1, source_target_pairs={{0,4},{1,5},{2,6},{3,7},{4,0},{5,1},{6,2},{7,3},{8,12},{9,13},{10,... | collective-permute-start | bytes 786440 | tf_op jit(solution)/shard_map/ppermute | solution.py:223
  76.6 0.0 collective-permute-done.refs_1_.x_late
  76.6 0.0 collective-permute-done.2.refs_2_.below
  76.6 0.1 shard_map.80
  76.7 0.3 collective-permute-start.4
  76.9 1.0 %collective-permute-done.3.refs_2_.above = bf16[2,256,256]{2,1,0:T(8,128)(2,1)S(1)} collective-permute-done((bf16[2,256,256]{2,1,0:T(8,128)(2,1)S(1)}, bf16[2,256,256]{2,1,0:T(8,128)(2,1)S(1)}, u32[]{:S(2)}, u32[]{:S(2)}) %collective-permute-start.3) | collective-permute-done | bytes 262176 | tf_op jit(solution)/shard_map/ppermute | solution.py:218
  77.9 0.1 shard_map.81
  77.9 3.8 %collective-permute-start.5 = (bf16[1,256,256]{2,1,0:T(8,128)(2,1)S(1)}, bf16[1,256,256]{2,1,0:T(8,128)(2,1)S(1)}, u32[]{:S(2)}, u32[]{:S(2)}) collective-permute-start(bf16[1,256,256]{2,1,0:T(8,128)(2,1)S(1)} %shard_map.81), channel_id=1, source_target_pairs={{0,3},{1,0},{2,1},{3,2},{4,7},{5,4},{6,5},{7,6},{8,11},{9,8},{10,9... | collective-permute-start | bytes 393224 | tf_op jit(solution)/shard_map/ppermute | solution.py:218
  81.7 1.7 %collective-permute-done.4.up = bf16[1,256,256]{2,1,0:T(8,128)(2,1)S(1)} collective-permute-done((bf16[1,256,256]{2,1,0:T(8,128)(2,1)S(1)}, bf16[1,256,256]{2,1,0:T(8,128)(2,1)S(1)}, u32[]{:S(2)}, u32[]{:S(2)}) %collective-permute-start.4) | collective-permute-done | bytes 131104 | tf_op jit(solution)/shard_map/ppermute | solution.py:218
  83.4 0.8 collective-permute-done.5.down
  84.2 1.2 %shard_map.86 = (bf16[256,1024]{1,0:T(8,128)(2,1)}, bf16[1024,256]{1,0:T(8,128)(2,1)}) custom-call(bf16[8,256,256]{2,1,0:T(8,128)(2,1)S(1)} %shard_map.78.own.refs_0_, bf16[4,256,256]{2,1,0:T(8,128)(2,1)S(1)} %collective-permute-done.refs_1_.x_late, bf16[2,256,256]{2,1,0:T(8,128)(2,1)S(1)} %collective-permute-done.2.refs_2_.below, ...), custom_call_target="tpu_custom_call" | custom-call | bytes 1 | tf_op jit(solution)/shard_map/pallas_call | solution.py:187
  (8 shorter events, 0.0 us)
Async XLA Ops:
  0.0 9.6 %copy-start = (f32[1024]{0:T(1024)S(1)}, f32[1024]{0:T(1024)}, u32[]{:S(2)}) copy-start(f32[1024]{0:T(1024)} %param.11) | copy-start | bytes 12292
  2.5 25.2 %all-to-all-start = ((bf16[16,128,256]{2,1,0:T(8,128)(2,1)}), bf16[16,128,256]{2,1,0:T(8,128)(2,1)S(1)}, u32[]{:S(2)}, u32[]{:S(2)}) async-start(bf16[16,128,256]{2,1,0:T(8,128)(2,1)} %prepare.1), calls=%async_computation | async-start | bytes 2097152 | tf_op jit(solution)/shard_map/all_to_all | solution.py:257
  9.8 1.2 %copy-start.2 = (bf16[1024,512]{1,0:T(8,128)(2,1)S(1)}, bf16[1024,512]{1,0:T(8,128)(2,1)}, u32[]{:S(2)}) copy-start(bf16[1024,512]{1,0:T(8,128)(2,1)} %constant.14.clone.table) | copy-start | bytes 3145732
  11.0 1.0 %copy-start.3 = (bf16[256,1024]{1,0:T(8,128)(2,1)S(1)}, bf16[256,1024]{1,0:T(8,128)(2,1)}, u32[]{:S(2)}) copy-start(bf16[256,1024]{1,0:T(8,128)(2,1)} %gate) | copy-start | bytes 1572868
  27.6 19.7 %copy-start.1 = (bf16[8192,1024]{1,0:T(8,128)(2,1)S(1)}, bf16[8192,1024]{1,0:T(8,128)(2,1)}, u32[]{:S(2)}) copy-start(bf16[8192,1024]{1,0:T(8,128)(2,1)} %weight.11) | copy-start | bytes 50331652
  48.7 14.9 %collective-permute-start.1 = (bf16[4,256,256]{2,1,0:T(8,128)(2,1)S(1)}, bf16[4,256,256]{2,1,0:T(8,128)(2,1)S(1)}, u32[]{:S(2)}, u32[]{:S(2)}) collective-permute-start(bf16[4,256,256]{2,1,0:T(8,128)(2,1)S(1)} %shard_map.75), channel_id=1, source_target_pairs={{0,4},{1,5},{2,6},{3,7},{4,0},{5,1},{6,2},{7,3},{8,12},{9,13},{10,... | collective-permute-start | bytes 1572872 | tf_op jit(solution)/shard_map/ppermute | solution.py:223
  49.5 11.3 %collective-permute-start.8 = (bf16[2,256,256]{2,1,0:T(8,128)(2,1)S(1)}, bf16[2,256,256]{2,1,0:T(8,128)(2,1)S(1)}, u32[]{:S(2)}, u32[]{:S(2)}) collective-permute-start(bf16[2,256,256]{2,1,0:T(8,128)(2,1)S(1)} %get-tuple-element.46), channel_id=1, source_target_pairs={{0,1},{1,2},{2,3},{3,0},{4,5},{5,6},{6,7},{7,4},{8,9},{9,10},{10,1... | collective-permute-start | bytes 786440 | tf_op jit(solution)/shard_map/ppermute | solution.py:218
  51.4 11.4 %collective-permute-start.10 = (bf16[2,256,256]{2,1,0:T(8,128)(2,1)S(1)}, bf16[2,256,256]{2,1,0:T(8,128)(2,1)S(1)}, u32[]{:S(2)}, u32[]{:S(2)}) collective-permute-start(bf16[2,256,256]{2,1,0:T(8,128)(2,1)S(1)} %get-tuple-element.47), channel_id=1, source_target_pairs={{0,3},{1,0},{2,1},{3,2},{4,7},{5,4},{6,5},{7,6},{8,11},{9,8},{10,9... | collective-permute-start | bytes 786440 | tf_op jit(solution)/shard_map/ppermute | solution.py:218
  54.2 13.6 %collective-permute-start.6 = (bf16[2,256,256]{2,1,0:T(8,128)(2,1)S(1)}, bf16[2,256,256]{2,1,0:T(8,128)(2,1)S(1)}, u32[]{:S(2)}, u32[]{:S(2)}) collective-permute-start(bf16[2,256,256]{2,1,0:T(8,128)(2,1)S(1)} %get-tuple-element.44), channel_id=1, source_target_pairs={{0,1},{1,2},{2,3},{3,0},{4,5},{5,6},{6,7},{7,4},{8,9},{9,10},{10,1... | collective-permute-start | bytes 786440 | tf_op jit(solution)/shard_map/ppermute | solution.py:218
  57.5 19.1 %collective-permute-start = (bf16[4,256,256]{2,1,0:T(8,128)(2,1)S(1)}, bf16[4,256,256]{2,1,0:T(8,128)(2,1)S(1)}, u32[]{:S(2)}, u32[]{:S(2)}) collective-permute-start(bf16[4,256,256]{2,1,0:T(8,128)(2,1)S(1)} %shard_map.77), channel_id=1, source_target_pairs={{0,4},{1,5},{2,6},{3,7},{4,0},{5,1},{6,2},{7,3},{8,12},{9,13},{10,... | collective-permute-start | bytes 1572872 | tf_op jit(solution)/shard_map/ppermute | solution.py:223
  60.7 9.2 %collective-permute-start.7 = (bf16[2,256,256]{2,1,0:T(8,128)(2,1)S(1)}, bf16[2,256,256]{2,1,0:T(8,128)(2,1)S(1)}, u32[]{:S(2)}, u32[]{:S(2)}) collective-permute-start(bf16[2,256,256]{2,1,0:T(8,128)(2,1)S(1)} %get-tuple-element.45), channel_id=1, source_target_pairs={{0,3},{1,0},{2,1},{3,2},{4,7},{5,4},{6,5},{7,6},{8,11},{9,8},{10,9... | collective-permute-start | bytes 786440 | tf_op jit(solution)/shard_map/ppermute | solution.py:218
  62.8 10.0 %collective-permute-start.9 = (bf16[2,256,256]{2,1,0:T(8,128)(2,1)S(1)}, bf16[2,256,256]{2,1,0:T(8,128)(2,1)S(1)}, u32[]{:S(2)}, u32[]{:S(2)}) collective-permute-start(bf16[2,256,256]{2,1,0:T(8,128)(2,1)S(1)} %shard_map.83), channel_id=1, source_target_pairs={{0,1},{1,2},{2,3},{3,0},{4,5},{5,6},{6,7},{7,4},{8,9},{9,10},{10,1... | collective-permute-start | bytes 786440 | tf_op jit(solution)/shard_map/ppermute | solution.py:218
  63.7 10.8 %collective-permute-start.11 = (bf16[2,256,256]{2,1,0:T(8,128)(2,1)S(1)}, bf16[2,256,256]{2,1,0:T(8,128)(2,1)S(1)}, u32[]{:S(2)}, u32[]{:S(2)}) collective-permute-start(bf16[2,256,256]{2,1,0:T(8,128)(2,1)S(1)} %shard_map.84), channel_id=1, source_target_pairs={{0,3},{1,0},{2,1},{3,2},{4,7},{5,4},{6,5},{7,6},{8,11},{9,8},{10,9... | collective-permute-start | bytes 786440 | tf_op jit(solution)/shard_map/ppermute | solution.py:218
  67.8 8.8 %collective-permute-start.2 = (bf16[2,256,256]{2,1,0:T(8,128)(2,1)S(1)}, bf16[2,256,256]{2,1,0:T(8,128)(2,1)S(1)}, u32[]{:S(2)}, u32[]{:S(2)}) collective-permute-start(bf16[2,256,256]{2,1,0:T(8,128)(2,1)S(1)} %get-tuple-element.41), channel_id=1, source_target_pairs={{0,1},{1,2},{2,3},{3,0},{4,5},{5,6},{6,7},{7,4},{8,9},{9,10},{10,1... | collective-permute-start | bytes 786440 | tf_op jit(solution)/shard_map/ppermute | solution.py:218
  69.9 8.0 %collective-permute-start.3 = (bf16[2,256,256]{2,1,0:T(8,128)(2,1)S(1)}, bf16[2,256,256]{2,1,0:T(8,128)(2,1)S(1)}, u32[]{:S(2)}, u32[]{:S(2)}) collective-permute-start(bf16[2,256,256]{2,1,0:T(8,128)(2,1)S(1)} %get-tuple-element.42), channel_id=1, source_target_pairs={{0,3},{1,0},{2,1},{3,2},{4,7},{5,4},{6,5},{7,6},{8,11},{9,8},{10,9... | collective-permute-start | bytes 786440 | tf_op jit(solution)/shard_map/ppermute | solution.py:218
  74.6 7.1 %collective-permute-start.12 = (bf16[512,256]{1,0:T(8,128)(2,1)S(1)}, bf16[512,256]{1,0:T(8,128)(2,1)S(1)}, u32[]{:S(2)}, u32[]{:S(2)}) collective-permute-start(bf16[512,256]{1,0:T(8,128)(2,1)S(1)} %shard_map.85), channel_id=1, source_target_pairs={{0,4},{1,5},{2,6},{3,7},{4,0},{5,1},{6,2},{7,3},{8,12},{9,13},{10,... | collective-permute-start | bytes 786440 | tf_op jit(solution)/shard_map/ppermute | solution.py:223
  76.7 6.7 %collective-permute-start.4 = (bf16[1,256,256]{2,1,0:T(8,128)(2,1)S(1)}, bf16[1,256,256]{2,1,0:T(8,128)(2,1)S(1)}, u32[]{:S(2)}, u32[]{:S(2)}) collective-permute-start(bf16[1,256,256]{2,1,0:T(8,128)(2,1)S(1)} %shard_map.80), channel_id=1, source_target_pairs={{0,1},{1,2},{2,3},{3,0},{4,5},{5,6},{6,7},{7,4},{8,9},{9,10},{10,1... | collective-permute-start | bytes 393224 | tf_op jit(solution)/shard_map/ppermute | solution.py:218
  77.9 6.3 %collective-permute-start.5 = (bf16[1,256,256]{2,1,0:T(8,128)(2,1)S(1)}, bf16[1,256,256]{2,1,0:T(8,128)(2,1)S(1)}, u32[]{:S(2)}, u32[]{:S(2)}) collective-permute-start(bf16[1,256,256]{2,1,0:T(8,128)(2,1)S(1)} %shard_map.81), channel_id=1, source_target_pairs={{0,3},{1,0},{2,1},{3,2},{4,7},{5,4},{6,5},{7,6},{8,11},{9,8},{10,9... | collective-permute-start | bytes 393224 | tf_op jit(solution)/shard_map/ppermute | solution.py:218
